TPU v7x, 32 devices: a whole 2x2x4 slice. The times are simulated.
32 devices in a mesh: row: 2 (over y), seq: 4 (over x, core), tp: 4 (over z).
Axes of the slice: x: 2, y: 2, z: 4, core: 2. Of those that a mesh axis runs over, the one named last changes fastest.
Arguments:
- block_in: float32 [2, 4096, 1536], P('row', ('seq', 'tp')), may hold values from -6 to 6
- block_grad: float32 [2, 4096, 1536], P('row', ('seq', 'tp')), may hold values from -6 to 6
- norm_gains: float32 [4, 1536], replicated, may hold values from 0.5 to 1.5
- mixer_in: bfloat16 [1536, 2, 3072], P(None, None, 'tp'), may hold values from -0.15625 to 0.15625
- conv_taps: float32 [4, 3072], P(None, 'tp'), may hold values from -3 to 3
- conv_bias: float32 [3072], P('tp'), may hold values from -3 to 3
- state_proj: bfloat16 [3072, 128], P('tp'), may hold values from -0.109375 to 0.109375
- step_proj: bfloat16 [96, 3072], P(None, 'tp'), may hold values from -0.625 to 0.625
- step_bias: float32 [3072], P('tp'), may hold values from -4 to -1
- decay_log: float32 [16, 3072], P(None, 'tp'), may hold values from -4.6 to 2.8
- skip_gain: float32 [3072], P('tp'), may hold values from 0.5 to 1.5
- mixer_out: bfloat16 [3072, 1536], P('tp'), may hold values from -0.3125 to 0.3125
- first_in: bfloat16 [1536, 2, 4096], P(None, None, 'tp'), may hold values from -0.15625 to 0.15625
- first_out: bfloat16 [4096, 1536], P('tp'), may hold values from -0.1875 to 0.1875
- attend_in: bfloat16 [1536, 3, 1536], P(None, None, 'tp'), may hold values from -0.15625 to 0.15625
- attend_out: bfloat16 [1536, 1536], P('tp'), may hold values from -1.25 to 1.25
- second_in: bfloat16 [1536, 2, 4096], P(None, None, 'tp'), may hold values from -0.15625 to 0.15625
- second_out: bfloat16 [4096, 1536], P('tp'), may hold values from -0.1875 to 0.1875
- row_counts: int32 [2], P('row'), may hold values from 1 to 4096, as said below
- doc_starts: int32 [2, 8], P('row'), may hold values from 0 to 4095, as said below
- row_mask: int32 [2], P('row'), may hold values from 0 to 1, as said below
Outputs:
- block_out: float32 [2, 4096, 1536], P('row', ('seq', 'tp'))
- grad_in: float32 [2, 4096, 1536], P('row', ('seq', 'tp'))
- grad_norm_gains: float32 [4, 1536], replicated
- grad_mixer_in: float32 [1536, 2, 3072], P(('row', 'seq'), None, 'tp')
- grad_conv_taps: float32 [4, 3072], P(None, 'tp')
- grad_conv_bias: float32 [3072], P('tp')
- grad_state_proj: float32 [3072, 128], P('tp')
- grad_step_proj: float32 [96, 3072], P(None, 'tp')
- grad_step_bias: float32 [3072], P('tp')
- grad_decay_log: float32 [16, 3072], P(None, 'tp')
- grad_skip_gain: float32 [3072], P('tp')
- grad_mixer_out: float32 [3072, 1536], P('tp', ('row', 'seq'))
- grad_first_in: float32 [1536, 2, 4096], P(('row', 'seq'), None, 'tp')
- grad_first_out: float32 [4096, 1536], P('tp', ('row', 'seq'))
- grad_attend_in: float32 [1536, 3, 1536], P(('row', 'seq'), None, 'tp')
- grad_attend_out: float32 [1536, 1536], P('tp', ('row', 'seq'))
- grad_second_in: float32 [1536, 2, 4096], P(('row', 'seq'), None, 'tp')
- grad_second_out: float32 [4096, 1536], P('tp', ('row', 'seq'))
Inputs may be any that keep to these rules, and one draw needn't show every extreme that they name: `row_counts`: in each aligned block of 1 row one row, drawn from the seed, has a count above 3072; some row has the count 4096. `doc_starts`: each row's starts are non-decreasing and begin with 0; equal starts make empty documents. In the row chosen for row_counts the second document starts within the first 1024 positions and ends after position 3072, and the last start is 4095. `row_mask`: the row chosen for row_counts in each aligned block is real; where 1 >= 2 some other row is padding.
All inputs are finite; a program needn't handle non-finite values.
Results may differ from a plain program's by a relative error of at most 0.02.
Values may be sent and summed in bfloat16 or wider, within the bound.
No kernel may reach another device: no remote copies, remote signals or barrier semaphores. Data moves between devices by JAX's collectives and lax.ppermute only.
A program may use at most 448 MiB of HBM per device.

v0:
```python
import jax
import jax.numpy as jnp
from jax import lax
from jax.sharding import PartitionSpec as P

HDIM = 128
WINDOW = 2048
MBLOCK = 64


epsilon = 1e-05
masked_score = -1e30


def carried_in(value, axis, join, neutral, backward):
    count, mine = (lax.axis_size(axis), lax.axis_index(axis))
    pieces = jax.tree.map(lambda part: lax.all_gather(part, axis), value)
    if backward:
        pieces = jax.tree.map(lambda part: part[::-1], pieces)
        mine = count - 1 - mine
    total = jax.tree.map(
        lambda part, zero: jnp.full_like(part, 0) + jnp.asarray(zero, part.dtype), value, neutral
    )

    def lap(position, total):
        longer = join(total, jax.tree.map(lambda part: part[position], pieces))
        return jax.tree.map(lambda new, old: jnp.where(position < mine, new, old), longer, total)

    return lax.fori_loop(0, count - 1, lap, total)


def from_behind(x, axis, by):
    peers = lax.axis_size(axis)
    pairs = [(i, i + by) for i in range(peers) if 0 <= i + by < peers]
    return lax.ppermute(x, axis, pairs)


def chain_pair(earlier, later):
    return (earlier[0] * later[0], later[0] * earlier[1] + later[1])


def gather_rows(local):
    return lax.all_gather(local, "tp", axis=1, tiled=True)


def reduce_rows(partial_value):
    return lax.psum_scatter(partial_value, "tp", scatter_dimension=1, tiled=True)


def channel_total(partial_value):
    return lax.psum(partial_value, "tp")


def carry_across(pair, backward):
    identity = (jnp.ones_like(pair[0]), jnp.zeros_like(pair[1]))
    return carried_in(pair, "seq", chain_pair, identity, backward)


def settle(pending, grad_weight_in, grad_weight_out):
    return pending + [(grad_weight_in, grad_weight_out)]


def doc_numbers(positions, starts):
    return jnp.sum((starts[:, None, :] <= positions[None, :, None]).astype(jnp.int32), axis=-1)


def norm_forward(stream, gain):
    scale = lax.rsqrt(jnp.mean(stream * stream, axis=-1, keepdims=True) + epsilon)
    return (stream * scale * gain, scale)


def norm_backward(stream, scale, gain, grad_normed):
    unit = stream * scale
    scaled = grad_normed * gain
    grad_gain = jnp.sum(grad_normed * unit, axis=(0, 1))
    grad_stream = scale * (scaled - unit * jnp.mean(scaled * unit, axis=-1, keepdims=True))
    return (grad_stream, grad_gain)


def silu_slope(value):
    logistic = jax.nn.sigmoid(value)
    return logistic * (1.0 + value * (1.0 - logistic))


def to_lanes(value, size):
    rows, length = (value.shape[0], value.shape[1])
    shaped = value.reshape((rows, length // size, size) + value.shape[2:])
    moved = jnp.moveaxis(shaped, 2, 0)
    return moved.reshape((size, rows * (length // size)) + value.shape[2:])


def from_lanes(value, rows):
    size, lanes = (value.shape[0], value.shape[1])
    shaped = value.reshape((size, rows, lanes // rows) + value.shape[2:])
    moved = jnp.moveaxis(shaped, 0, 2)
    return moved.reshape((rows, lanes // rows * size) + value.shape[2:])


def blocks_first(value, rows):
    return jnp.moveaxis(value.reshape((rows, value.shape[0] // rows) + value.shape[1:]), 1, 0)


def blocks_back(value):
    moved = jnp.moveaxis(value, 0, 1)
    return moved.reshape((moved.shape[0] * moved.shape[1],) + moved.shape[2:])


def advance(state, item, rate):
    step_now, write_now, read_now, source_now, keep_now = item
    return (
        jnp.exp(step_now[:, None, :] * rate) * keep_now[:, None, None] * state
        + step_now[:, None, :] * write_now[:, :, None] * source_now[:, None, :]
    )


def block_factors(items, rate):
    total_step = jnp.sum(items[0], axis=0)
    kept = jnp.prod(items[4], axis=0)
    return jnp.exp(rate[None] * total_step[:, None, :]) * kept[:, None, None]


def prefix_pairs(factors, locals_held, reverse):
    identity = (jnp.ones_like(factors[0]), jnp.zeros_like(locals_held[0]))

    def stepper(held, item):
        return (chain_pair(held, item), held)

    total, exclusive = lax.scan(stepper, identity, (factors, locals_held), reverse=reverse)
    return (total, exclusive)


def states_only(start, items, rate):

    def states_token(held, item):
        return (advance(held, item, rate), None)

    last, _ = lax.scan(states_token, start, items)
    return last


def lane_outputs(start, items, rate):

    def lane_token(held, item):
        fresh = advance(held, item, rate)
        return (fresh, jnp.sum(fresh * item[2][:, :, None], axis=1))

    _, outputs = lax.scan(lane_token, start, items)
    return outputs


def mixer_forward(normed, weights, same, flags, size):
    (
        mixer_in,
        conv_taps,
        conv_bias,
        state_proj,
        step_proj,
        step_bias,
        decay_log,
        skip_gain,
        mixer_out,
    ) = weights
    both = jnp.einsum("rtd,dce->rtce", normed, mixer_in, preferred_element_type=jnp.float32)
    signal = both[:, :, 0].astype(jnp.bfloat16)
    gate = both[:, :, 1]
    taps = conv_taps.shape[0]
    length = signal.shape[1]
    rows = signal.shape[0]
    tail = from_behind(signal[:, length - (taps - 1) :], "seq", 1)
    widened = jnp.concatenate([tail, signal], axis=1).astype(jnp.float32)
    conv_sum = conv_bias + jnp.zeros_like(gate)
    for tap in range(taps):
        conv_sum = (
            conv_sum + conv_taps[tap] * widened[:, tap : tap + length] * same[:, :, tap : tap + 1]
        )
    inner = jax.nn.silu(conv_sum).astype(jnp.bfloat16)
    source = inner.astype(jnp.float32)
    mixed = channel_total(
        jnp.einsum("rte,ec->rtc", inner, state_proj, preferred_element_type=jnp.float32)
    )
    rank = step_proj.shape[0]
    states = decay_log.shape[0]
    step_low = mixed[:, :, :rank].astype(jnp.bfloat16)
    write_in = mixed[:, :, rank : rank + states]
    read_out = mixed[:, :, rank + states :]
    step_raw = (
        jnp.einsum("rtk,ke->rte", step_low, step_proj, preferred_element_type=jnp.float32)
        + step_bias
    )
    step = jax.nn.softplus(step_raw)
    rate = -jnp.exp(decay_log)
    items = tuple(
        (to_lanes(value, size) for value in (step, write_in, read_out, source, 1.0 - flags))
    )
    lanes = items[0].shape[1]
    zero = jnp.zeros((lanes,) + rate.shape, jnp.float32)
    local_end = states_only(zero, items, rate)
    factors = blocks_first(block_factors(items, rate), rows)
    total, exclusive = prefix_pairs(factors, blocks_first(local_end, rows), False)
    incoming = carry_across(total, False)[1]
    firsts = exclusive[0] * incoming[None] + exclusive[1]
    scanned = from_lanes(lane_outputs(blocks_back(firsts), items, rate), rows)
    result = scanned + skip_gain * source
    gated = (result * jax.nn.silu(gate)).astype(jnp.bfloat16)
    partial_value = jnp.einsum("rte,ed->rtd", gated, mixer_out, preferred_element_type=jnp.float32)
    cache = (
        normed,
        widened,
        gate,
        conv_sum,
        inner,
        source,
        step_low,
        step_raw,
        step,
        write_in,
        read_out,
        result,
        gated,
        firsts,
        factors,
    )
    return (partial_value, cache)


def mixer_backward(grad_branch, cache, weights, same, flags, size):
    (
        mixer_in,
        conv_taps,
        conv_bias,
        state_proj,
        step_proj,
        step_bias,
        decay_log,
        skip_gain,
        mixer_out,
    ) = weights
    (
        normed,
        widened,
        gate,
        conv_sum,
        inner,
        source,
        step_low,
        step_raw,
        step,
        write_in,
        read_out,
        result,
        gated,
        firsts,
        factors,
    ) = cache
    rows = step.shape[0]
    grad_gated = jnp.einsum(
        "rtd,ed->rte", grad_branch, mixer_out, preferred_element_type=jnp.float32
    )
    grad_mixer_out = jnp.einsum(
        "rte,rtd->ed", gated, grad_branch, preferred_element_type=jnp.float32
    )
    grad_result = grad_gated * jax.nn.silu(gate)
    grad_gate = grad_gated * result * silu_slope(gate)
    grad_skip = jnp.sum(grad_result * source, axis=(0, 1))
    rate = -jnp.exp(decay_log)
    items = tuple(
        (
            to_lanes(value, size)
            for value in (step, write_in, read_out, source, 1.0 - flags, grad_result)
        )
    )
    lanes = items[0].shape[1]
    zero = jnp.zeros((lanes,) + rate.shape, jnp.float32)

    def carry_token(held, item):
        step_now, read_now, keep_now, grad_now = item
        factor = jnp.exp(step_now[:, None, :] * rate) * keep_now[:, None, None]
        return (factor * (read_now[:, :, None] * grad_now[:, None, :] + held), None)

    local_back, _ = lax.scan(
        carry_token, zero, (items[0], items[2], items[4], items[5]), reverse=True
    )
    total_back, exclusive_back = prefix_pairs(factors, blocks_first(local_back, rows), True)
    later = carry_across(total_back, True)[1]
    carry_in = blocks_back(exclusive_back[0] * later[None] + exclusive_back[1])

    def state_token(held, item):
        fresh = advance(held, item, rate)
        return (fresh, (fresh, held))

    _, (after_states, before_states) = lax.scan(state_token, blocks_back(firsts), items[:5])

    def back_token(inner_carry, item):
        weight_next, rate_total = inner_carry
        step_now, write_now, read_now, source_now, keep_now, grad_now, state_now, state_before = (
            item
        )
        factor = jnp.exp(step_now[:, None, :] * rate) * keep_now[:, None, None]
        adjoint = read_now[:, :, None] * grad_now[:, None, :] + weight_next
        weighted = adjoint * state_before * factor
        grad_step = jnp.sum(
            weighted * rate + adjoint * write_now[:, :, None] * source_now[:, None, :], axis=1
        )
        grad_write = jnp.sum(adjoint * (step_now * source_now)[:, None, :], axis=2)
        grad_read = jnp.sum(state_now * grad_now[:, None, :], axis=2)
        grad_source = jnp.sum(adjoint * write_now[:, :, None], axis=1) * step_now
        rate_total = rate_total + jnp.sum(weighted * step_now[:, None, :], axis=0)
        return ((factor * adjoint, rate_total), (grad_step, grad_write, grad_read, grad_source))

    start = (carry_in, jnp.zeros(rate.shape, jnp.float32))
    (_, grad_rate), lane_grads = lax.scan(
        back_token, start, items + (after_states, before_states), reverse=True
    )
    grad_step, grad_write, grad_read, grad_source = tuple(
        (from_lanes(value, rows) for value in lane_grads)
    )
    grad_source = grad_source + skip_gain * grad_result
    grad_step_raw = (grad_step * jax.nn.sigmoid(step_raw)).astype(jnp.bfloat16)
    grad_step_bias = jnp.sum(grad_step_raw.astype(jnp.float32), axis=(0, 1))
    grad_step_proj = jnp.einsum(
        "rtk,rte->ke", step_low, grad_step_raw, preferred_element_type=jnp.float32
    )
    grad_low = jnp.einsum(
        "rte,ke->rtk", grad_step_raw, step_proj, preferred_element_type=jnp.float32
    )
    grad_mixed = channel_total(jnp.concatenate([grad_low, grad_write, grad_read], axis=-1)).astype(
        jnp.bfloat16
    )
    grad_state_proj = jnp.einsum(
        "rte,rtc->ec", inner, grad_mixed, preferred_element_type=jnp.float32
    )
    grad_source = grad_source + jnp.einsum(
        "rtc,ec->rte", grad_mixed, state_proj, preferred_element_type=jnp.float32
    )
    grad_conv = grad_source * silu_slope(conv_sum)
    length = grad_conv.shape[1]
    taps = conv_taps.shape[0]
    grad_widened = jnp.zeros(widened.shape, jnp.float32)
    grad_taps = []
    for tap in range(taps):
        term = grad_conv * same[:, :, tap : tap + 1]
        grad_widened = grad_widened.at[:, tap : tap + length].add(conv_taps[tap] * term)
        grad_taps.append(jnp.sum(widened[:, tap : tap + length] * term, axis=(0, 1)))
    grad_conv_bias = jnp.sum(grad_conv, axis=(0, 1))
    returned = from_behind(grad_widened[:, : taps - 1], "seq", -1)
    grad_signal = grad_widened[:, taps - 1 :] + jnp.pad(
        returned, ((0, 0), (length - taps + 1, 0), (0, 0))
    )
    grad_both = jnp.stack([grad_signal, grad_gate], axis=2).astype(jnp.bfloat16)
    grad_mixer_in = jnp.einsum(
        "rtd,rtce->dce", normed, grad_both, preferred_element_type=jnp.float32
    )
    grad_normed = jnp.einsum(
        "rtce,dce->rtd", grad_both, mixer_in, preferred_element_type=jnp.float32
    )
    small = (
        jnp.stack(grad_taps),
        grad_conv_bias,
        grad_state_proj,
        grad_step_proj,
        grad_step_bias,
        grad_rate * rate,
        grad_skip,
    )
    return (grad_normed, grad_mixer_in, grad_mixer_out, small)


def dense_forward(normed, dense_in, dense_out):
    both = jnp.einsum("rtd,dcf->rtcf", normed, dense_in, preferred_element_type=jnp.float32)
    gate = both[:, :, 0]
    upper = both[:, :, 1]
    hidden = (jax.nn.silu(gate) * upper).astype(jnp.bfloat16)
    partial_value = jnp.einsum("rtf,fd->rtd", hidden, dense_out, preferred_element_type=jnp.float32)
    return (partial_value, (normed, gate, upper, hidden))


def dense_backward(grad_branch, cache, dense_in, dense_out):
    normed, gate, upper, hidden = cache
    grad_hidden = jnp.einsum(
        "rtd,fd->rtf", grad_branch, dense_out, preferred_element_type=jnp.float32
    )
    grad_dense_out = jnp.einsum(
        "rtf,rtd->fd", hidden, grad_branch, preferred_element_type=jnp.float32
    )
    grad_gate = grad_hidden * upper * silu_slope(gate)
    grad_upper = grad_hidden * jax.nn.silu(gate)
    grad_both = jnp.stack([grad_gate, grad_upper], axis=2).astype(jnp.bfloat16)
    grad_dense_in = jnp.einsum(
        "rtd,rtcf->dcf", normed, grad_both, preferred_element_type=jnp.float32
    )
    grad_normed = jnp.einsum(
        "rtcf,dcf->rtd", grad_both, dense_in, preferred_element_type=jnp.float32
    )
    return (grad_normed, grad_dense_in, grad_dense_out)


def window_mask(positions, documents, key_place, key_docs, first, block, span):
    query_place = positions[first : first + block]
    near = key_place[first : first + span]
    allowed = (
        (near[None, :] <= query_place[:, None])
        & (query_place[:, None] - near[None, :] < WINDOW)
        & (near[None, :] >= 0)
    )
    alike = documents[:, first : first + block, None] == key_docs[:, None, first : first + span]
    return (allowed[None] & alike)[:, None]


def block_scores(query, keys_wide, mask, first, block, span):
    scores = jnp.einsum(
        "rqhd,rkhd->rhqk",
        query[:, first : first + block],
        keys_wide[:, first : first + span],
        preferred_element_type=jnp.float32,
    ) * HDIM ** (-0.5)
    return jnp.where(mask, scores, masked_score)


def attention_forward(normed, attend_in, attend_out, positions, documents, key_place, key_docs):
    projected = jnp.einsum(
        "rtd,dch->rtch", normed, attend_in, preferred_element_type=jnp.float32
    ).astype(jnp.bfloat16)
    rows, length = (projected.shape[0], projected.shape[1])
    heads = projected.shape[3] // HDIM
    split = projected.reshape(rows, length, 3, heads, HDIM)
    query, keys, values = (split[:, :, 0], split[:, :, 1], split[:, :, 2])
    reach = key_place.shape[0] // length - 1
    fetched = []
    for back in range(1, reach + 1):
        fetched.append(from_behind((keys, values), "seq", back))
    keys_wide = jnp.concatenate([piece[0] for piece in fetched[::-1]] + [keys], axis=1)
    values_wide = jnp.concatenate([piece[1] for piece in fetched[::-1]] + [values], axis=1)
    block = min(512, length)
    span = reach * length + block
    outputs = []
    totals = []
    for first in range(0, length, block):
        mask = window_mask(positions, documents, key_place, key_docs, first, block, span)
        scores = block_scores(query, keys_wide, mask, first, block, span)
        top = jnp.max(scores, axis=-1, keepdims=True)
        log_total = top + jnp.log(jnp.sum(jnp.exp(scores - top), axis=-1, keepdims=True))
        soft = jnp.exp(scores - log_total).astype(jnp.bfloat16)
        outputs.append(
            jnp.einsum(
                "rhqk,rkhd->rqhd",
                soft,
                values_wide[:, first : first + span],
                preferred_element_type=jnp.float32,
            ).astype(jnp.bfloat16)
        )
        totals.append(log_total)
    attended = jnp.concatenate(outputs, axis=1).reshape(rows, length, heads * HDIM)
    partial_value = jnp.einsum(
        "rth,hd->rtd", attended, attend_out, preferred_element_type=jnp.float32
    )
    return (partial_value, (normed, query, keys_wide, values_wide, attended, totals))


def attention_backward(
    grad_branch, cache, attend_in, attend_out, positions, documents, key_place, key_docs
):
    normed, query, keys_wide, values_wide, attended, totals = cache
    rows, length, heads = (query.shape[0], query.shape[1], query.shape[2])
    grad_attended = (
        jnp.einsum("rtd,hd->rth", grad_branch, attend_out, preferred_element_type=jnp.float32)
        .astype(jnp.bfloat16)
        .reshape(rows, length, heads, HDIM)
    )
    grad_attend_out = jnp.einsum(
        "rth,rtd->hd", attended, grad_branch, preferred_element_type=jnp.float32
    )
    reach = keys_wide.shape[1] // length - 1
    block = min(512, length)
    span = reach * length + block
    grad_keys = jnp.zeros(keys_wide.shape, jnp.float32)
    grad_values = jnp.zeros(values_wide.shape, jnp.float32)
    query_parts = []
    for index, first in enumerate(range(0, length, block)):
        mask = window_mask(positions, documents, key_place, key_docs, first, block, span)
        scores = block_scores(query, keys_wide, mask, first, block, span)
        soft = jnp.exp(scores - totals[index])
        soft_low = soft.astype(jnp.bfloat16)
        grad_slice = grad_attended[:, first : first + block]
        grad_soft = jnp.einsum(
            "rqhd,rkhd->rhqk",
            grad_slice,
            values_wide[:, first : first + span],
            preferred_element_type=jnp.float32,
        )
        grad_values = grad_values.at[:, first : first + span].add(
            jnp.einsum("rhqk,rqhd->rkhd", soft_low, grad_slice, preferred_element_type=jnp.float32)
        )
        grad_scores = (
            soft * (grad_soft - jnp.sum(soft * grad_soft, axis=-1, keepdims=True))
        ).astype(jnp.bfloat16)
        query_parts.append(
            jnp.einsum(
                "rhqk,rkhd->rqhd",
                grad_scores,
                keys_wide[:, first : first + span],
                preferred_element_type=jnp.float32,
            )
            * HDIM ** (-0.5)
        )
        grad_keys = grad_keys.at[:, first : first + span].add(
            jnp.einsum(
                "rhqk,rqhd->rkhd",
                grad_scores,
                query[:, first : first + block],
                preferred_element_type=jnp.float32,
            )
            * HDIM ** (-0.5)
        )
    own_keys = grad_keys[:, reach * length :]
    own_values = grad_values[:, reach * length :]
    for back in range(1, reach + 1):
        start = (reach - back) * length
        returned = (
            from_behind(
                grad_keys[:, start : start + length].astype(jnp.bfloat16), "seq", -back
            ).astype(jnp.float32),
            from_behind(
                grad_values[:, start : start + length].astype(jnp.bfloat16), "seq", -back
            ).astype(jnp.float32),
        )
        own_keys = own_keys + returned[0]
        own_values = own_values + returned[1]
    grad_projected = (
        jnp.stack([jnp.concatenate(query_parts, axis=1), own_keys, own_values], axis=2)
        .astype(jnp.bfloat16)
        .reshape(rows, length, 3, heads * HDIM)
    )
    grad_attend_in = jnp.einsum(
        "rtd,rtch->dch", normed, grad_projected, preferred_element_type=jnp.float32
    )
    grad_normed = jnp.einsum(
        "rtch,dch->rtd", grad_projected, attend_in, preferred_element_type=jnp.float32
    )
    return (grad_normed, grad_attend_in, grad_attend_out)


def shards(
    block_in,
    block_grad,
    norm_gains,
    mixer_in,
    conv_taps,
    conv_bias,
    state_proj,
    step_proj,
    step_bias,
    decay_log,
    skip_gain,
    mixer_out,
    first_in,
    first_out,
    attend_in,
    attend_out,
    second_in,
    second_out,
    row_counts,
    doc_starts,
    row_mask,
):
    local_len = block_in.shape[1]
    length = local_len * lax.axis_size("tp")
    anchor = lax.axis_index("seq") * length
    positions = anchor + jnp.arange(length, dtype=jnp.int32)
    own_place = anchor + lax.axis_index("tp") * local_len + jnp.arange(local_len, dtype=jnp.int32)
    valid = ((own_place[None, :] < row_counts[:, None]) & (row_mask[:, None] == 1)).astype(
        jnp.float32
    )[:, :, None]
    documents = doc_numbers(positions, doc_starts)
    flags = jnp.any(doc_starts[:, None, :] == positions[None, :, None], axis=-1).astype(jnp.float32)
    taps = conv_taps.shape[0]
    same = jnp.stack(
        [
            (
                (positions - (taps - 1 - tap) >= 0)[None, :]
                & (doc_numbers(positions - (taps - 1 - tap), doc_starts) == documents)
            ).astype(jnp.float32)
            for tap in range(taps)
        ],
        axis=-1,
    )
    size = min(MBLOCK, length)
    reach = -(-WINDOW // length)
    key_place = anchor - reach * length + jnp.arange((reach + 1) * length, dtype=jnp.int32)
    key_docs = doc_numbers(key_place, doc_starts)
    mixer_weights = (
        mixer_in,
        conv_taps,
        conv_bias,
        state_proj,
        step_proj,
        step_bias,
        decay_log,
        skip_gain,
        mixer_out,
    )
    normed_mix, scale_mix = norm_forward(block_in, norm_gains[0])
    partial_value, cache_mix = mixer_forward(
        gather_rows(normed_mix.astype(jnp.bfloat16)), mixer_weights, same, flags, size
    )
    stream_mix = block_in + reduce_rows(partial_value)
    normed_first, scale_first = norm_forward(stream_mix, norm_gains[1])
    partial_value, cache_first = dense_forward(
        gather_rows(normed_first.astype(jnp.bfloat16)), first_in, first_out
    )
    stream_first = stream_mix + reduce_rows(partial_value)
    normed_attend, scale_attend = norm_forward(stream_first, norm_gains[2])
    partial_value, cache_attend = attention_forward(
        gather_rows(normed_attend.astype(jnp.bfloat16)),
        attend_in,
        attend_out,
        positions,
        documents,
        key_place,
        key_docs,
    )
    stream_attend = stream_first + reduce_rows(partial_value)
    normed_second, scale_second = norm_forward(stream_attend, norm_gains[3])
    partial_value, cache_second = dense_forward(
        gather_rows(normed_second.astype(jnp.bfloat16)), second_in, second_out
    )
    stream_out = stream_attend + reduce_rows(partial_value)
    block_out = stream_out * valid
    grad_stream = block_grad * valid
    grad_normed, grad_second_in, grad_second_out = dense_backward(
        gather_rows(grad_stream.astype(jnp.bfloat16)), cache_second, second_in, second_out
    )
    pending = settle([], grad_second_in, grad_second_out)
    grad_back, gain_four = norm_backward(
        stream_attend, scale_second, norm_gains[3], reduce_rows(grad_normed)
    )
    grad_stream = grad_stream + grad_back
    grad_normed, grad_attend_in, grad_attend_out = attention_backward(
        gather_rows(grad_stream.astype(jnp.bfloat16)),
        cache_attend,
        attend_in,
        attend_out,
        positions,
        documents,
        key_place,
        key_docs,
    )
    pending = settle(pending, grad_attend_in, grad_attend_out)
    grad_back, gain_three = norm_backward(
        stream_first, scale_attend, norm_gains[2], reduce_rows(grad_normed)
    )
    grad_stream = grad_stream + grad_back
    grad_normed, grad_first_in, grad_first_out = dense_backward(
        gather_rows(grad_stream.astype(jnp.bfloat16)), cache_first, first_in, first_out
    )
    pending = settle(pending, grad_first_in, grad_first_out)
    grad_back, gain_two = norm_backward(
        stream_mix, scale_first, norm_gains[1], reduce_rows(grad_normed)
    )
    grad_stream = grad_stream + grad_back
    grad_normed, grad_mixer_in, grad_mixer_out, small = mixer_backward(
        gather_rows(grad_stream.astype(jnp.bfloat16)), cache_mix, mixer_weights, same, flags, size
    )
    pending = settle(pending, grad_mixer_in, grad_mixer_out)
    grad_back, gain_one = norm_backward(
        block_in, scale_mix, norm_gains[0], reduce_rows(grad_normed)
    )
    grad_stream = grad_stream + grad_back
    ordered = [pending[3], pending[2], pending[1], pending[0]]
    flat = tuple((member for pair in ordered for member in pair))
    flat = (
        lax.psum_scatter(
            flat[0].astype(jnp.bfloat16), ("row", "seq"), scatter_dimension=0, tiled=True
        ).astype(jnp.float32),
        lax.psum_scatter(
            flat[1].astype(jnp.bfloat16), ("row", "seq"), scatter_dimension=1, tiled=True
        ).astype(jnp.float32),
        lax.psum_scatter(
            flat[2].astype(jnp.bfloat16), ("row", "seq"), scatter_dimension=0, tiled=True
        ).astype(jnp.float32),
        lax.psum_scatter(
            flat[3].astype(jnp.bfloat16), ("row", "seq"), scatter_dimension=1, tiled=True
        ).astype(jnp.float32),
        lax.psum_scatter(
            flat[4].astype(jnp.bfloat16), ("row", "seq"), scatter_dimension=0, tiled=True
        ).astype(jnp.float32),
        lax.psum_scatter(
            flat[5].astype(jnp.bfloat16), ("row", "seq"), scatter_dimension=1, tiled=True
        ).astype(jnp.float32),
        lax.psum_scatter(
            flat[6].astype(jnp.bfloat16), ("row", "seq"), scatter_dimension=0, tiled=True
        ).astype(jnp.float32),
        lax.psum_scatter(
            flat[7].astype(jnp.bfloat16), ("row", "seq"), scatter_dimension=1, tiled=True
        ).astype(jnp.float32),
    )
    small = (
        lax.psum(small[0].astype(jnp.bfloat16), ("row", "seq")).astype(jnp.float32),
        lax.psum(small[1].astype(jnp.bfloat16), ("row", "seq")).astype(jnp.float32),
        lax.psum(small[2].astype(jnp.bfloat16), ("row", "seq")).astype(jnp.float32),
        lax.psum(small[3].astype(jnp.bfloat16), ("row", "seq")).astype(jnp.float32),
        lax.psum(small[4].astype(jnp.bfloat16), ("row", "seq")).astype(jnp.float32),
        lax.psum(small[5].astype(jnp.bfloat16), ("row", "seq")).astype(jnp.float32),
        lax.psum(small[6].astype(jnp.bfloat16), ("row", "seq")).astype(jnp.float32),
    )
    gains = lax.psum(jnp.stack([gain_one, gain_two, gain_three, gain_four]), ("row", "seq", "tp"))
    return (
        block_out,
        grad_stream,
        gains,
        flat[0],
        small[0],
        small[1],
        small[2],
        small[3],
        small[4],
        small[5],
        small[6],
        flat[1],
        flat[2],
        flat[3],
        flat[4],
        flat[5],
        flat[6],
        flat[7],
    )


def solution(mesh):
    in_specs = (
        P("row", ("seq", "tp"), None),
        P("row", ("seq", "tp"), None),
        P(),
        P(None, None, "tp"),
        P(None, "tp"),
        P("tp"),
        P("tp", None),
        P(None, "tp"),
        P("tp"),
        P(None, "tp"),
        P("tp"),
        P("tp", None),
        P(None, None, "tp"),
        P("tp", None),
        P(None, None, "tp"),
        P("tp", None),
        P(None, None, "tp"),
        P("tp", None),
        P("row"),
        P("row", None),
        P("row"),
    )
    out_specs = (
        P("row", ("seq", "tp"), None),
        P("row", ("seq", "tp"), None),
        P(),
        P(("row", "seq"), None, "tp"),
        P(None, "tp"),
        P("tp"),
        P("tp", None),
        P(None, "tp"),
        P("tp"),
        P(None, "tp"),
        P("tp"),
        P("tp", ("row", "seq")),
        P(("row", "seq"), None, "tp"),
        P("tp", ("row", "seq")),
        P(("row", "seq"), None, "tp"),
        P("tp", ("row", "seq")),
        P(("row", "seq"), None, "tp"),
        P("tp", ("row", "seq")),
    )
    return jax.shard_map(shards, mesh=mesh, in_specs=in_specs, out_specs=out_specs, check_vma=False)
```

profile of v0, /device:TPU:0, one launch (start us, length us, event | category | flops | bytes accessed | tf_op | source)
XLA Modules:
  0.0 3754.1 jit_solution(7151862798746231724)
XLA Ops:
  17.2 62.8 %all-gather.13.cloned.1.call-done = bf16[1,1024,1536]{2,1,0:T(8,128)(2,1)} async-done(((bf16[1,256,1536]{2,1,0:T(8,128)(2,1)}), bf16[1,1024,1536]{2,1,0:T(8,128)(2,1)}) %all-gather.13.cloned.1.call-update) | async-done | bytes 3145744 | tf_op jit(solution)/shard_map/all_gather | solution.py:43
  80.0 8.3 fusion.109
  114.1 28.2 all-reduce.10.cloned.1.call-done
  155.2 287.7 %while.153 = (s32[]{:T(128)}, f32[16,16,768]{2,1,0:T(8,128)}, f32[64,16,768]{2,1,0:T(8,128)}, f32[16,768]{1,0:T(8,128)}, f32[64,16]{1,0:T(8,128)}, /*index=5*/f3...) while((s32[]{:T(128)}, f32[16,16,768]{2,1,0:T(8,128)}, ...), condition=%wide.region_10.11_spmd.clone, body=%wide.region_9.10_spmd.clone.sunk | while | flops 1376259 | bytes 1920315 | solution.py:137
  446.7 46.9 %while.154 = (s32[]{:T(128)}, f32[1,16,768]{2,1,0:T(8,128)}, f32[1,16,768]{2,1,0:T(8,128)}, f32[16,1,16,768]{3,2,1,0:T(8,128)}, f32[16,1,16,768]{3,2,1,0:T(8,128...) while((s32[]{:T(128)}, f32[1,16,768]{2,1,0:T(8,128)}, ...), condition=%wide.region_12.13_spmd.clone, body=%wide.region_11.12_spmd.clone.sunk | while | flops 86019 | bytes 491640 | solution.py:128
  493.5 7.1 all-gather
  500.6 7.0 all-gather.1
  517.2 337.1 %while.151 = (s32[]{:T(128)}, f32[16,16,768]{2,1,0:T(8,128)}, f32[64,16,768]{2,1,0:T(8,128)}, f32[64,16,768]{2,1,0:T(8,128)}, f32[16,768]{1,0:T(8,128)}, /*index...) while((s32[]{:T(128)}, f32[16,16,768]{2,1,0:T(8,128)}, ...), condition=%wide.region_17.18_spmd, body=%wide.region_15.17_spmd.sunk | while | flops 1560578 | bytes 2070845 | solution.py:147
  868.0 110.8 %reduce-scatter.17.cloned.1.call-done = f32[1,256,1536]{2,1,0:T(8,128)} async-done(((f32[1,1024,1536]{2,1,0:T(8,128)}), f32[1,256,1536]{2,1,0:T(8,128)}) %reduce-scatter.17.cloned.1.call-update) | async-done | bytes 1572880 | tf_op jit(solution)/shard_map/reduce_scatter | solution.py:47
  983.3 64.1 %all-gather.15.cloned.1.call-done = bf16[1,1024,1536]{2,1,0:T(8,128)(2,1)} async-done(((bf16[1,256,1536]{2,1,0:T(8,128)(2,1)}), bf16[1,1024,1536]{2,1,0:T(8,128)(2,1)}) %all-gather.15.cloned.1.call-update) | async-done | bytes 3145744 | tf_op jit(solution)/shard_map/all_gather | solution.py:43
  1047.4 10.2 fusion.60
  1066.3 109.5 %reduce-scatter.19.cloned.1.call-done = f32[1,256,1536]{2,1,0:T(8,128)} async-done(((f32[1,1024,1536]{2,1,0:T(8,128)}), f32[1,256,1536]{2,1,0:T(8,128)}) %reduce-scatter.19.cloned.1.call-update) | async-done | bytes 1572880 | tf_op jit(solution)/shard_map/reduce_scatter | solution.py:47
  1184.9 59.5 %all-gather.17.cloned.1.call-done = bf16[1,1024,1536]{2,1,0:T(8,128)(2,1)} async-done(((bf16[1,256,1536]{2,1,0:T(8,128)(2,1)}), bf16[1,1024,1536]{2,1,0:T(8,128)(2,1)}) %all-gather.17.cloned.1.call-update) | async-done | bytes 3145744 | tf_op jit(solution)/shard_map/all_gather | solution.py:43
  1244.4 5.8 fusion.122
  1282.7 8.2 fusion.13
  1305.8 6.3 fusion.158
  1312.2 8.4 fusion.157
  1326.5 121.8 %reduce-scatter.21.cloned.1.call-done = f32[1,256,1536]{2,1,0:T(8,128)} async-done(((f32[1,1024,1536]{2,1,0:T(8,128)}), f32[1,256,1536]{2,1,0:T(8,128)}) %reduce-scatter.21.cloned.1.call-update) | async-done | bytes 1572880 | tf_op jit(solution)/shard_map/reduce_scatter | solution.py:47
  1457.1 59.7 %all-gather.19.cloned.1.call-done = bf16[1,1024,1536]{2,1,0:T(8,128)(2,1)} async-done(((bf16[1,256,1536]{2,1,0:T(8,128)(2,1)}), bf16[1,1024,1536]{2,1,0:T(8,128)(2,1)}) %all-gather.19.cloned.1.call-update) | async-done | bytes 3145744 | tf_op jit(solution)/shard_map/all_gather | solution.py:43
  1516.8 12.0 fusion.63
  1528.9 52.3 %all-gather.21.cloned.1.call-done = bf16[1,1024,1536]{2,1,0:T(8,128)(2,1)} async-done(((bf16[1,256,1536]{2,1,0:T(8,128)(2,1)}), bf16[1,1024,1536]{2,1,0:T(8,128)(2,1)}) %all-gather.21.cloned.1.call-update) | async-done | bytes 3145744 | tf_op jit(solution)/shard_map/all_gather | solution.py:43
  1581.2 10.0 fusion.121
  1593.1 10.7 fusion.38
  1603.9 10.5 convolution_bitcast_fusion.4
  1614.5 98.9 %reduce-scatter.25.cloned.1.call-done = f32[1,256,1536]{2,1,0:T(8,128)} async-done(((f32[1,1024,1536]{2,1,0:T(8,128)}), f32[1,256,1536]{2,1,0:T(8,128)}) %reduce-scatter.25.cloned.1.call-update) | async-done | bytes 1572880 | tf_op jit(solution)/shard_map/reduce_scatter | solution.py:47
  1716.9 110.1 %reduce-scatter.23.cloned.1.call-done = f32[1,256,1536]{2,1,0:T(8,128)} async-done(((f32[1,1024,1536]{2,1,0:T(8,128)}), f32[1,256,1536]{2,1,0:T(8,128)}) %reduce-scatter.23.cloned.1.call-update) | async-done | bytes 1572880 | tf_op jit(solution)/shard_map/reduce_scatter | solution.py:47
  1832.9 63.7 %all-gather.23.cloned.1.call-done = bf16[1,1024,1536]{2,1,0:T(8,128)(2,1)} async-done(((bf16[1,256,1536]{2,1,0:T(8,128)(2,1)}), bf16[1,1024,1536]{2,1,0:T(8,128)(2,1)}) %all-gather.23.cloned.1.call-update) | async-done | bytes 3145744 | tf_op jit(solution)/shard_map/all_gather | solution.py:43
  1900.4 8.1 convolution_bitcast_fusion.1
  1908.5 12.5 multiply_reduce_fusion.5
  1921.0 12.3 multiply_reduce_fusion.4
  1933.7 10.6 constant_dynamic-update-slice_fusion
  1950.4 12.4 multiply_convert_fusion.1
  1969.7 8.1 multiply_convert_fusion
  1977.8 6.1 constant_dynamic-update-slice_fusion.1
  2005.1 18.5 collective-permute-done.6
  2029.0 7.8 convolution_bitcast_fusion.2
  2036.9 108.6 %reduce-scatter.27.cloned.1.call-done = f32[1,256,1536]{2,1,0:T(8,128)} async-done(((f32[1,1024,1536]{2,1,0:T(8,128)}), f32[1,256,1536]{2,1,0:T(8,128)}) %reduce-scatter.27.cloned.1.call-update) | async-done | bytes 1572880 | tf_op jit(solution)/shard_map/reduce_scatter | solution.py:47
  2150.3 63.9 %all-gather.25.cloned.1.call-done = bf16[1,1024,1536]{2,1,0:T(8,128)(2,1)} async-done(((bf16[1,256,1536]{2,1,0:T(8,128)(2,1)}), bf16[1,1024,1536]{2,1,0:T(8,128)(2,1)}) %all-gather.25.cloned.1.call-update) | async-done | bytes 3145744 | tf_op jit(solution)/shard_map/all_gather | solution.py:43
  2214.2 10.0 fusion.120
  2225.5 10.7 fusion.35
  2236.3 109.5 %reduce-scatter.29.cloned.1.call-done = f32[1,256,1536]{2,1,0:T(8,128)} async-done(((f32[1,1024,1536]{2,1,0:T(8,128)}), f32[1,256,1536]{2,1,0:T(8,128)}) %reduce-scatter.29.cloned.1.call-update) | async-done | bytes 1572880 | tf_op jit(solution)/shard_map/reduce_scatter | solution.py:47
  2350.4 9.6 convolution_convert_fusion.4
  2361.9 10.9 convolution_convert_fusion
  2378.8 8.6 convolution_convert_fusion.3
  2387.5 9.7 convolution_convert_fusion.5
  2398.3 234.9 %while.152 = (s32[]{:T(128)}, f32[16,16,768]{2,1,0:T(8,128)S(1)}, f32[64,16,16,768]{3,2,1,0:T(8,128)}, f32[64,16,16,768]{3,2,1,0:T(8,128)}, f32[64,16,768]{2,1,0...) while((s32[]{:T(128)}, f32[16,16,768]{2,1,0:T(8,128)S(1)}, ...), condition=%wide.region_45.46_spmd, body=%wide.region_44.45_spmd.sunk | while | flops 1179650 | bytes 3493181 | solution.py:291
  2633.3 11.7 convolution_convert_fusion.1
  2646.7 9.3 fusion.68
  2659.4 163.1 %while.156 = (s32[]{:T(128)}, f32[16,16,768]{2,1,0:T(8,128)S(1)}, f32[64,16,768]{2,1,0:T(8,128)}, f32[16,768]{1,0:T(8,128)S(1)}, f32[64,16]{1,0:T(8,128)}, /*ind...) while((s32[]{:T(128)}, f32[16,16,768]{2,1,0:T(8,128)S(1)}, ...), condition=%wide.region_39.40_spmd.clone, body=%wide.region_38.39_spmd.clone.sunk | while | flops 1179652 | bytes 1920335 | solution.py:280
  2823.6 23.8 while.157
  2847.4 5.6 all-gather.2
  2853.0 5.8 all-gather.3
  2865.2 522.4 %while.159 = (s32[]{:T(128)}, f32[16,16,768]{2,1,0:T(8,128)S(1)}, f32[16,768]{1,0:T(8,128)S(1)}, f32[64,16,768]{2,1,0:T(8,128)}, f32[64,16,16]{2,1,0:T(8,128)}, ...) while((s32[]{:T(128)}, f32[16,16,768]{2,1,0:T(8,128)S(1)}, ...), condition=%wide.region_52.53_spmd.clone, body=%wide.region_46.52_spmd.clone.sunk | while | flops 3747332 | bytes 4317611 | solution.py:311
  3395.6 30.9 all-reduce.13
  3431.0 6.6 convolution_convert_fusion.6
  3450.9 11.9 scatter-add.31
  3468.7 8.9 scatter-add.34
  3481.7 5.7 multiply_reduce_fusion.9
  3488.5 6.9 convolution_convert_fusion.2
  3497.4 9.5 convolution_bitcast_fusion.3
  3521.2 25.3 all-reduce.4
  3554.6 32.5 reduce-scatter.33.cloned.1.call-done
  3589.8 110.4 %reduce-scatter.31.cloned.1.call-done = f32[1,256,1536]{2,1,0:T(8,128)} async-done(((f32[1,1024,1536]{2,1,0:T(8,128)}), f32[1,256,1536]{2,1,0:T(8,128)}) %reduce-scatter.31.cloned.1.call-update) | async-done | bytes 1572880 | tf_op jit(solution)/shard_map/reduce_scatter | solution.py:47
  3702.1 41.3 %psum.72 = f32[4,1536]{1,0:T(4,128)} all-reduce(f32[4,1536]{1,0:T(4,128)S(1)} %pad_maximum_fusion.17), channel_id=1, replica_groups=mesh['row'=2,'seq'=4,'tp'=4] {'row','seq','tp'}, use_global_device_ids=true, to_apply=%region_60.61 | all-reduce | flops 6144 | bytes 49152 | tf_op jit(solution)/shard_map/psum | solution.py:705
  (2205 shorter events, 1931.6 us)
Async XLA Ops:
  7.2 1237.2 %copy-start = (bf16[1536,3,384]{2,0,1:T(8,128)(2,1)S(1)}, bf16[1536,3,384]{2,0,1:T(8,128)(2,1)}, u32[]{:S(2)}) copy-start(bf16[1536,3,384]{2,0,1:T(8,128)(2,1)} %param.69) | copy-start | bytes 10616836
  7.2 72.8 %all-gather.13.cloned.1.call-start = ((), (), s32[]{:S(2)}) async-start(), calls=%async_computation.16 | async-start | bytes 3932160 | tf_op jit(solution)/shard_map/all_gather | solution.py:43
  10.6 970.4 %copy-start.59 = (f32[1536]{0:T(1024)}, f32[1536]{0:T(1024)S(1)}, u32[]{:S(2)}) copy-start(f32[1536]{0:T(1024)S(1)} %get-tuple-element.1533) | copy-start | bytes 18436
  10.6 1167.4 %copy-start.61 = (f32[1536]{0:T(1024)}, f32[1536]{0:T(1024)S(1)}, u32[]{:S(2)}) copy-start(f32[1536]{0:T(1024)S(1)} %get-tuple-element.1535) | copy-start | bytes 18436
  13.7 128.6 %all-reduce.10.cloned.1.call-start = ((), (), s32[]{:S(2)}) async-start(), calls=%async_computation.17 | async-start | bytes 1048576 | tf_op jit(solution)/shard_map/psum | solution.py:51
  91.5 3.0 collective-permute-start
  102.9 875.9 %reduce-scatter.17.cloned.1.call-start = ((), (), s32[]{:S(2)}) async-start(), calls=%async_computation.18 | async-start | bytes 7864320 | tf_op jit(solution)/shard_map/reduce_scatter | solution.py:47
  868.0 179.4 %all-gather.15.cloned.1.call-start = ((), (), s32[]{:S(2)}) async-start(), calls=%async_computation.19 | async-start | bytes 3932160 | tf_op jit(solution)/shard_map/all_gather | solution.py:43
  983.2 192.6 %reduce-scatter.19.cloned.1.call-start = ((), (), s32[]{:S(2)}) async-start(), calls=%async_computation.20 | async-start | bytes 7864320 | tf_op jit(solution)/shard_map/reduce_scatter | solution.py:47
  1047.4 13.4 copy-start.98
  1066.3 116.9 %copy-start.69 = (s32[1024]{0:T(1024)S(1)}, s32[1024]{0:T(1024)}, u32[]{:S(2)}) copy-start(s32[1024]{0:T(1024)} %copy-done.68) | copy-start | bytes 12292
  1066.3 178.1 %all-gather.17.cloned.1.call-start = ((), (), s32[]{:S(2)}) async-start(), calls=%async_computation.21 | async-start | bytes 3932160 | tf_op jit(solution)/shard_map/all_gather | solution.py:43
  1180.2 268.1 %reduce-scatter.21.cloned.1.call-start = ((), (), s32[]{:S(2)}) async-start(), calls=%async_computation.22 | async-start | bytes 7864320 | tf_op jit(solution)/shard_map/reduce_scatter | solution.py:47
  1253.9 20.4 collective-permute-start.4
  1256.5 21.0 collective-permute-start.3
  1267.6 35.2 collective-permute-start.2
  1269.8 33.0 collective-permute-start.1
  1282.7 23.1 copy-start.2
  1326.2 190.6 %all-gather.19.cloned.1.call-start = ((), (), s32[]{:S(2)}) async-start(), calls=%async_computation.23 | async-start | bytes 3932160 | tf_op jit(solution)/shard_map/all_gather | solution.py:43
  1452.7 128.5 %all-gather.21.cloned.1.call-start = ((), (), s32[]{:S(2)}) async-start(), calls=%async_computation.25 | async-start | bytes 3932160 | tf_op jit(solution)/shard_map/all_gather | solution.py:43
  1457.1 256.3 %reduce-scatter.25.cloned.1.call-start = ((), (), s32[]{:S(2)}) async-start(), calls=%async_computation.26 | async-start | bytes 7864320 | tf_op jit(solution)/shard_map/reduce_scatter | solution.py:47
  1603.8 223.2 %reduce-scatter.23.cloned.1.call-start = ((), (), s32[]{:S(2)}) async-start(), calls=%async_computation.24 | async-start | bytes 7864320 | tf_op jit(solution)/shard_map/reduce_scatter | solution.py:47
  1614.4 282.2 %all-gather.23.cloned.1.call-start = ((), (), s32[]{:S(2)}) async-start(), calls=%async_computation.27 | async-start | bytes 3932160 | tf_op jit(solution)/shard_map/all_gather | solution.py:43
  1832.5 313.1 %reduce-scatter.27.cloned.1.call-start = ((), (), s32[]{:S(2)}) async-start(), calls=%async_computation.28 | async-start | bytes 7864320 | tf_op jit(solution)/shard_map/reduce_scatter | solution.py:47
  1908.5 12.5 copy-start.9
  1947.6 52.1 %collective-permute-start.7 = (bf16[1,1024,3,128]{1,3,2,0:T(8,128)(2,1)}, bf16[1,1024,3,128]{1,3,2,0:T(8,128)(2,1)}, u32[]{:S(2)}, u32[]{:S(2)}) collective-permute-start(bf16[1,1024,3,128]{1,3,2,0:T(8,128)(2,1)} %slice.632), channel_id=1, source_target_pairs={{4,0},{8,4},{12,8},{5,1},{9,5},{13,9},{6,2},{10,6},{14,10},{7,3},{... | collective-permute-start | bytes 2359304 | tf_op jit(solution)/shard_map/ppermute | solution.py:35
  1948.9 50.8 %collective-permute-start.8 = (bf16[1,1024,3,128]{1,3,2,0:T(8,128)(2,1)}, bf16[1,1024,3,128]{1,3,2,0:T(8,128)(2,1)}, u32[]{:S(2)}, u32[]{:S(2)}) collective-permute-start(bf16[1,1024,3,128]{1,3,2,0:T(8,128)(2,1)} %slice.631), channel_id=1, source_target_pairs={{8,0},{12,4},{9,1},{13,5},{10,2},{14,6},{11,3},{15,7},{24,16},{28,... | collective-permute-start | bytes 2359304 | tf_op jit(solution)/shard_map/ppermute | solution.py:35
  1950.4 12.5 copy-start.41
  1950.4 19.2 slice-start
  1950.4 19.2 slice-start.1
  1950.4 19.2 slice-start.2
  1991.1 14.0 collective-permute-start.5
  1992.4 31.2 collective-permute-start.6
  2036.8 108.7 %copy-start.13 = (f32[1,256,1536]{2,1,0:T(8,128)S(1)}, f32[1,256,1536]{2,1,0:T(8,128)}, u32[]{:S(2)}) copy-start(f32[1,256,1536]{2,1,0:T(8,128)} %copy-done.12) | copy-start | bytes 4718596
  2036.8 108.7 %copy-start.62 = (f32[1536]{0:T(1024)S(1)}, f32[1536]{0:T(1024)}, u32[]{:S(2)}) copy-start(f32[1536]{0:T(1024)} %copy-done.61) | copy-start | bytes 18436
  2036.8 108.7 %copy-start.89 = (f32[256]{0:T(256)S(1)}, f32[256]{0:T(256)}, u32[]{:S(2)}) copy-start(f32[256]{0:T(256)} %copy-done.88) | copy-start | bytes 3076
  2036.9 111.3 %copy-start.33 = (f32[1,256,1536]{2,1,0:T(8,128)S(1)}, f32[1,256,1536]{2,1,0:T(8,128)}, u32[]{:S(2)}) copy-start(f32[1,256,1536]{2,1,0:T(8,128)} %get-tuple-element.1713) | copy-start | bytes 4718596
  2036.9 177.3 %all-gather.25.cloned.1.call-start = ((), (), s32[]{:S(2)}) async-start(), calls=%async_computation.29 | async-start | bytes 3932160 | tf_op jit(solution)/shard_map/all_gather | solution.py:43
  2150.0 195.8 %reduce-scatter.29.cloned.1.call-start = ((), (), s32[]{:S(2)}) async-start(), calls=%async_computation.30 | async-start | bytes 7864320 | tf_op jit(solution)/shard_map/reduce_scatter | solution.py:47
  2224.2 12.1 copy-start.107
  2236.2 109.6 %copy-start.11 = (f32[1,256,1536]{2,1,0:T(8,128)S(1)}, f32[1,256,1536]{2,1,0:T(8,128)}, u32[]{:S(2)}) copy-start(f32[1,256,1536]{2,1,0:T(8,128)} %copy-done.10) | copy-start | bytes 4718596
  2236.2 109.6 %copy-start.60 = (f32[1536]{0:T(1024)S(1)}, f32[1536]{0:T(1024)}, u32[]{:S(2)}) copy-start(f32[1536]{0:T(1024)} %copy-done.59) | copy-start | bytes 18436
  2236.2 109.6 %copy-start.87 = (f32[256]{0:T(256)S(1)}, f32[256]{0:T(256)}, u32[]{:S(2)}) copy-start(f32[256]{0:T(256)} %copy-done.86) | copy-start | bytes 3076
  2236.3 112.2 %copy-start.34 = (f32[1,256,1536]{2,1,0:T(8,128)S(1)}, f32[1,256,1536]{2,1,0:T(8,128)}, u32[]{:S(2)}) copy-start(f32[1,256,1536]{2,1,0:T(8,128)} %get-tuple-element.1711) | copy-start | bytes 4718596
  2236.3 408.7 %all-gather.27.cloned.1.call-start = ((), (), s32[]{:S(2)}) async-start(), calls=%async_computation.31 | async-start | bytes 3932160 | tf_op jit(solution)/shard_map/all_gather | solution.py:43
  2350.3 1156.7 %reduce-scatter.47.cloned.1.call-start = ((), (), s32[]{:S(2)}) async-start(), calls=%async_computation.40 | async-start | bytes 3538944 | tf_op jit(solution)/shard_map/reduce_scatter | solution.py:692
  2360.0 1149.1 %reduce-scatter.45.cloned.1.call-start = ((), (), s32[]{:S(2)}) async-start(), calls=%async_computation.39 | async-start | bytes 7077888 | tf_op jit(solution)/shard_map/reduce_scatter | solution.py:689
  2372.9 1139.3 %reduce-scatter.43.cloned.1.call-start = ((), (), s32[]{:S(2)}) async-start(), calls=%async_computation.38 | async-start | bytes 1327104 | tf_op jit(solution)/shard_map/reduce_scatter | solution.py:686
  2378.7 1135.1 %reduce-scatter.41.cloned.1.call-start = ((), (), s32[]{:S(2)}) async-start(), calls=%async_computation.37 | async-start | bytes 3981312 | tf_op jit(solution)/shard_map/reduce_scatter | solution.py:683
  2387.4 1128.4 %reduce-scatter.39.cloned.1.call-start = ((), (), s32[]{:S(2)}) async-start(), calls=%async_computation.36 | async-start | bytes 3538944 | tf_op jit(solution)/shard_map/reduce_scatter | solution.py:680
  2397.2 1120.6 %reduce-scatter.37.cloned.1.call-start = ((), (), s32[]{:S(2)}) async-start(), calls=%async_computation.35 | async-start | bytes 7077888 | tf_op jit(solution)/shard_map/reduce_scatter | solution.py:677
  2645.0 904.5 %all-reduce.12.cloned.1.call-start = ((), (), s32[]{:S(2)}) async-start(), calls=%async_computation.41 | async-start | bytes 688128 | tf_op jit(solution)/shard_map/psum | solution.py:699
  3430.9 121.9 %reduce-scatter.35.cloned.1.call-start = ((), (), s32[]{:S(2)}) async-start(), calls=%async_computation.34 | async-start | bytes 2654208 | tf_op jit(solution)/shard_map/reduce_scatter | solution.py:674
  3441.1 146.1 %reduce-scatter.33.cloned.1.call-start = ((), (), s32[]{:S(2)}) async-start(), calls=%async_computation.33 | async-start | bytes 5308416 | tf_op jit(solution)/shard_map/reduce_scatter | solution.py:671
  3450.9 13.6 copy-start.65
  3450.9 13.6 copy-start.75
  3468.7 13.0 copy-start.4
  3468.7 13.0 copy-start.71
  3468.7 13.0 copy-start.79
  3478.3 3.3 collective-permute-start.9
  3495.4 204.8 %reduce-scatter.31.cloned.1.call-start = ((), (), s32[]{:S(2)}) async-start(), calls=%async_computation.32 | async-start | bytes 7864320 | tf_op jit(solution)/shard_map/reduce_scatter | solution.py:47
  3517.8 182.4 %copy-start.14 = (f32[1,256,1536]{2,1,0:T(8,128)S(1)}, f32[1,256,1536]{2,1,0:T(8,128)}, u32[]{:S(2)}) copy-start(f32[1,256,1536]{2,1,0:T(8,128)} %param.55) | copy-start | bytes 4718596
  3517.8 182.4 %copy-start.58 = (f32[1536]{0:T(1024)S(1)}, f32[1536]{0:T(1024)}, u32[]{:S(2)}) copy-start(f32[1536]{0:T(1024)} %copy-done.57) | copy-start | bytes 18436
  3517.8 182.4 %copy-start.85 = (f32[256]{0:T(256)S(1)}, f32[256]{0:T(256)}, u32[]{:S(2)}) copy-start(f32[256]{0:T(256)} %copy-done.84) | copy-start | bytes 3076
  (85 other events, 285.9 us)
Sparse Core Ops, SparseCore 0:
  13.8 66.1 all-gather.12
  103.0 39.2 all-reduce.9
  868.1 110.6 reduce-scatter.16
  983.3 63.9 all-gather.14
  1066.4 109.3 reduce-scatter.18
  1180.3 64.0 all-gather.16
  1326.3 121.8 reduce-scatter.20
  1452.8 63.9 all-gather.18
  1519.0 62.1 all-gather.20
  1603.9 109.3 reduce-scatter.24
  1715.7 111.2 reduce-scatter.22
  1832.6 64.0 all-gather.22
  2037.0 108.4 reduce-scatter.26
  2150.1 63.9 all-gather.24
  2236.4 109.3 reduce-scatter.28
  2350.4 64.0 all-gather.26
  2417.7 44.8 reduce-scatter.46
  2466.3 61.7 reduce-scatter.44
  2531.8 36.7 reduce-scatter.42
  2572.4 48.0 reduce-scatter.40
  2624.2 46.2 reduce-scatter.38
  2673.9 61.7 reduce-scatter.36
  3431.1 51.5 all-reduce.11
  3486.2 43.3 reduce-scatter.34
  3533.1 54.0 reduce-scatter.32
  3589.4 110.7 reduce-scatter.30
where the time goes:
time: 3820 us; the launch traced here: 3750 us
  waiting for transfers between devices  1390 us (36%)
  local copies, waits for them, and re-layouts  967 us (25%)
  other arithmetic  929 us (24%)
  matrix products  301 us (8%)
  blocking collectives  123 us (3%)
    reduce_scatter x8, waiting for transfers between devices, reduce_rows(): lax.psum_scatter(partial_value, 'tp', scatter_dimension=1, tiled=True)  880 us
    all_gather x8, waiting for transfers between devices, gather_rows(): return lax.all_gather(local, 'tp', axis=1, tiled=True)  426 us
    mul x320, local copies, waits for them, and re-layouts, advance(): step_now[:, None, :] * write_now[:, :, None] * source_now[:, None, :]  249 us
    reduce_sum x64, other arithmetic, lane_token(): return (fresh, jnp.sum(fresh * item[2][:, :, None], axis=1))  155 us
    reduce_sum x64, other arithmetic, back_token(): jnp.sum(weighted * rate + adjoint * write_now[:, :, None] * source_now[:,...  151 us
    add x64, other arithmetic, advance(): jnp.exp(step_now[:, None, :] * rate) * keep_now[:, None, None] * state  146 us
    mul x192, local copies, waits for them, and re-layouts, advance(): jnp.exp(step_now[:, None, :] * rate) * keep_now[:, None, None] * state  131 us
    mul x128, local copies, waits for them, and re-layouts, carry_token(): return (factor * (read_now[:, :, None] * grad_now[:, None, :] + held), None)  97.9 us
  transfers between devices with their start and end apart: 36, of which 20 were waited for; matrix products, arithmetic and copies ran while one was open for 33% of the time, Pallas kernels for 0%

commit v1 on v0

--- a/solution.py
+++ b/solution.py
@@ -1,11 +1,15 @@
 import jax
 import jax.numpy as jnp
 from jax import lax
+from jax.experimental import pallas as pl
+from jax.experimental.pallas import tpu as pltpu
 from jax.sharding import PartitionSpec as P
 
 HDIM = 128
 WINDOW = 2048
-MBLOCK = 64
+f32 = jnp.float32
+LOG2E = 1.4426950408889634
+FAR = 1e30
 
 
 epsilon = 1e-05
@@ -44,7 +48,8 @@
 
 
 def reduce_rows(partial_value):
-    return lax.psum_scatter(partial_value, "tp", scatter_dimension=1, tiled=True)
+    low = partial_value.astype(jnp.bfloat16)
+    return lax.psum_scatter(low, "tp", scatter_dimension=1, tiled=True).astype(jnp.float32)
 
 
 def channel_total(partial_value):
@@ -82,73 +87,198 @@
     return logistic * (1.0 + value * (1.0 - logistic))
 
 
-def to_lanes(value, size):
-    rows, length = (value.shape[0], value.shape[1])
-    shaped = value.reshape((rows, length // size, size) + value.shape[2:])
-    moved = jnp.moveaxis(shaped, 2, 0)
-    return moved.reshape((size, rows * (length // size)) + value.shape[2:])
-
-
-def from_lanes(value, rows):
-    size, lanes = (value.shape[0], value.shape[1])
-    shaped = value.reshape((size, rows, lanes // rows) + value.shape[2:])
-    moved = jnp.moveaxis(shaped, 0, 2)
-    return moved.reshape((rows, lanes // rows * size) + value.shape[2:])
-
-
-def blocks_first(value, rows):
-    return jnp.moveaxis(value.reshape((rows, value.shape[0] // rows) + value.shape[1:]), 1, 0)
-
-
-def blocks_back(value):
-    moved = jnp.moveaxis(value, 0, 1)
-    return moved.reshape((moved.shape[0] * moved.shape[1],) + moved.shape[2:])
-
-
-def advance(state, item, rate):
-    step_now, write_now, read_now, source_now, keep_now = item
-    return (
-        jnp.exp(step_now[:, None, :] * rate) * keep_now[:, None, None] * state
-        + step_now[:, None, :] * write_now[:, :, None] * source_now[:, None, :]
-    )
-
-
-def block_factors(items, rate):
-    total_step = jnp.sum(items[0], axis=0)
-    kept = jnp.prod(items[4], axis=0)
-    return jnp.exp(rate[None] * total_step[:, None, :]) * kept[:, None, None]
-
-
-def prefix_pairs(factors, locals_held, reverse):
-    identity = (jnp.ones_like(factors[0]), jnp.zeros_like(locals_held[0]))
-
-    def stepper(held, item):
-        return (chain_pair(held, item), held)
-
-    total, exclusive = lax.scan(stepper, identity, (factors, locals_held), reverse=reverse)
-    return (total, exclusive)
-
-
-def states_only(start, items, rate):
-
-    def states_token(held, item):
-        return (advance(held, item, rate), None)
-
-    last, _ = lax.scan(states_token, start, items)
-    return last
-
-
-def lane_outputs(start, items, rate):
-
-    def lane_token(held, item):
-        fresh = advance(held, item, rate)
-        return (fresh, jnp.sum(fresh * item[2][:, :, None], axis=1))
-
-    _, outputs = lax.scan(lane_token, start, items)
-    return outputs
-
-
-def mixer_forward(normed, weights, same, flags, size):
+TB = 128
+VM = 48 * 1024 * 1024
+
+def params():
+    return pltpu.CompilerParams(vmem_limit_bytes=VM, dimension_semantics=("arbitrary",))
+
+def turned(ref, b, base, tb):
+    return pltpu.roll(ref[b], lax.rem(tb - base, tb), axis=1)
+
+def ends_kernel(step_ref, push_ref, write_ref, rate_ref, end_ref):
+    rows, tb = step_ref.shape[0], step_ref.shape[1]
+    @pl.when(pl.program_id(0) == 0)
+    def _():
+        end_ref[...] = jnp.zeros_like(end_ref)
+    def group(j, held):
+        base = pl.multiple_of(j * 8, 8)
+        held = list(held)
+        for b in range(rows):
+            steps = step_ref[b, pl.ds(base, 8), :]
+            pushes = push_ref[b, pl.ds(base, 8), :]
+            writes = turned(write_ref, b, base, tb)
+            for k in range(8):
+                factor = jnp.exp2(steps[k:k+1] * rate_ref[...])
+                held[b] = factor * held[b] + writes[:, k:k+1] * pushes[k:k+1]
+        return tuple(held)
+    held = lax.fori_loop(0, tb // 8, group, tuple(end_ref[b] for b in range(rows)))
+    for b in range(rows):
+        end_ref[b] = held[b]
+
+def scan_ends(step, push, write, rate):
+    rows, length, chans = step.shape
+    states = rate.shape[0]
+    tb = min(TB, length)
+    big = pl.BlockSpec((rows, tb, chans), lambda i: (0, i, 0))
+    thin = pl.BlockSpec((rows, states, tb), lambda i: (0, 0, i))
+    return pl.pallas_call(ends_kernel, grid=(length // tb,),
+        in_specs=[big, big, thin, pl.BlockSpec((states, chans), lambda i: (0, 0))],
+        out_specs=pl.BlockSpec((rows, states, chans), lambda i: (0, 0, 0)),
+        out_shape=jax.ShapeDtypeStruct((rows, states, chans), f32),
+        compiler_params=params())(step, push, write, rate)
+
+def outputs_kernel(step_ref, push_ref, write_ref, read_ref, rate_ref, first_ref, out_ref, start_ref, held_ref):
+    rows, tb = step_ref.shape[0], step_ref.shape[1]
+    @pl.when(pl.program_id(0) == 0)
+    def _():
+        held_ref[...] = first_ref[...]
+    start_ref[:, 0] = held_ref[...]
+    def group(j, held):
+        base = pl.multiple_of(j * 8, 8)
+        held = list(held)
+        for b in range(rows):
+            steps = step_ref[b, pl.ds(base, 8), :]
+            pushes = push_ref[b, pl.ds(base, 8), :]
+            writes = turned(write_ref, b, base, tb)
+            reads = turned(read_ref, b, base, tb)
+            lines = []
+            for k in range(8):
+                factor = jnp.exp2(steps[k:k+1] * rate_ref[...])
+                held[b] = factor * held[b] + writes[:, k:k+1] * pushes[k:k+1]
+                lines.append(jnp.sum(held[b] * reads[:, k:k+1], axis=0, keepdims=True))
+            out_ref[b, pl.ds(base, 8), :] = jnp.concatenate(lines, axis=0)
+        return tuple(held)
+    held = lax.fori_loop(0, tb // 8, group, tuple(held_ref[b] for b in range(rows)))
+    for b in range(rows):
+        held_ref[b] = held[b]
+
+def scan_outputs(step, push, write, read, rate, first):
+    rows, length, chans = step.shape
+    states = rate.shape[0]
+    tb = min(TB, length)
+    big = pl.BlockSpec((rows, tb, chans), lambda i: (0, i, 0))
+    thin = pl.BlockSpec((rows, states, tb), lambda i: (0, 0, i))
+    whole = pl.BlockSpec((rows, states, chans), lambda i: (0, 0, 0))
+    return pl.pallas_call(outputs_kernel, grid=(length // tb,),
+        in_specs=[big, big, thin, thin, pl.BlockSpec((states, chans), lambda i: (0, 0)), whole],
+        out_specs=[big, pl.BlockSpec((rows, 1, states, chans), lambda i: (0, i, 0, 0))],
+        out_shape=[jax.ShapeDtypeStruct((rows, length, chans), f32),
+                   jax.ShapeDtypeStruct((rows, length // tb, states, chans), f32)],
+        scratch_shapes=[pltpu.VMEM((rows, states, chans), f32)],
+        compiler_params=params())(step, push, write, read, rate, first)
+
+def tail_kernel(step_ref, grad_ref, read_ref, rate_ref, end_ref):
+    rows, tb = step_ref.shape[0], step_ref.shape[1]
+    @pl.when(pl.program_id(0) == 0)
+    def _():
+        end_ref[...] = jnp.zeros_like(end_ref)
+    def group(j, held):
+        base = pl.multiple_of(tb - 8 - j * 8, 8)
+        held = list(held)
+        for b in range(rows):
+            steps = step_ref[b, pl.ds(base, 8), :]
+            grads = grad_ref[b, pl.ds(base, 8), :]
+            reads = turned(read_ref, b, base, tb)
+            for k in range(7, -1, -1):
+                factor = jnp.exp2(steps[k:k+1] * rate_ref[...])
+                held[b] = factor * (held[b] + reads[:, k:k+1] * grads[k:k+1])
+        return tuple(held)
+    held = lax.fori_loop(0, tb // 8, group, tuple(end_ref[b] for b in range(rows)))
+    for b in range(rows):
+        end_ref[b] = held[b]
+
+def scan_tail(step, grad, read, rate):
+    rows, length, chans = step.shape
+    states = rate.shape[0]
+    tb = min(TB, length)
+    n = length // tb
+    big = pl.BlockSpec((rows, tb, chans), lambda i: (0, n - 1 - i, 0))
+    thin = pl.BlockSpec((rows, states, tb), lambda i: (0, 0, n - 1 - i))
+    return pl.pallas_call(tail_kernel, grid=(n,),
+        in_specs=[big, big, thin, pl.BlockSpec((states, chans), lambda i: (0, 0))],
+        out_specs=pl.BlockSpec((rows, states, chans), lambda i: (0, 0, 0)),
+        out_shape=jax.ShapeDtypeStruct((rows, states, chans), f32),
+        compiler_params=params())(step, grad, read, rate)
+
+def back_kernel(step_ref, push_ref, grad_ref, write_ref, read_ref, rate_ref, start_ref, later_ref,
+                decay_ref, weight_ref, gwrite_ref, gread_ref, grate_ref, carry_ref, factor_sc, kept_sc):
+    rows, tb = step_ref.shape[0], step_ref.shape[1]
+    @pl.when(pl.program_id(0) == 0)
+    def _():
+        carry_ref[...] = later_ref[...]
+        grate_ref[...] = jnp.zeros_like(grate_ref)
+    def redo(j, held):
+        base = pl.multiple_of(j * 8, 8)
+        held = list(held)
+        for b in range(rows):
+            steps = step_ref[b, pl.ds(base, 8), :]
+            pushes = push_ref[b, pl.ds(base, 8), :]
+            writes = turned(write_ref, b, base, tb)
+            for k in range(8):
+                factor = jnp.exp2(steps[k:k+1] * rate_ref[...])
+                kept = factor * held[b]
+                factor_sc[b, base + k] = factor
+                kept_sc[b, base + k] = kept
+                held[b] = kept + writes[:, k:k+1] * pushes[k:k+1]
+        return tuple(held)
+    lax.fori_loop(0, tb // 8, redo, tuple(start_ref[b, 0] for b in range(rows)))
+    lanes = lax.broadcasted_iota(jnp.int32, (1, tb), 1)
+    def group(j, carried):
+        base = pl.multiple_of(tb - 8 - j * 8, 8)
+        carry, total = list(carried[0]), carried[1]
+        for b in range(rows):
+            steps = step_ref[b, pl.ds(base, 8), :]
+            pushes = push_ref[b, pl.ds(base, 8), :]
+            grads = grad_ref[b, pl.ds(base, 8), :]
+            writes = turned(write_ref, b, base, tb)
+            reads = turned(read_ref, b, base, tb)
+            gwrite, gread = gwrite_ref[b], gread_ref[b]
+            decays, weights = [None] * 8, [None] * 8
+            for k in range(7, -1, -1):
+                kept = kept_sc[b, base + k]
+                adjoint = reads[:, k:k+1] * grads[k:k+1] + carry[b]
+                weighted = adjoint * kept
+                decays[k] = jnp.sum(weighted * rate_ref[...], axis=0, keepdims=True)
+                weights[k] = jnp.sum(adjoint * writes[:, k:k+1], axis=0, keepdims=True)
+                here = lanes == base + k
+                gwrite = jnp.where(here, jnp.sum(adjoint * pushes[k:k+1], axis=1, keepdims=True), gwrite)
+                gread = jnp.where(here, jnp.sum(kept * grads[k:k+1], axis=1, keepdims=True), gread)
+                total = total + weighted * steps[k:k+1]
+                carry[b] = factor_sc[b, base + k] * adjoint
+            gwrite_ref[b], gread_ref[b] = gwrite, gread
+            decay_ref[b, pl.ds(base, 8), :] = jnp.concatenate(decays, axis=0)
+            weight_ref[b, pl.ds(base, 8), :] = jnp.concatenate(weights, axis=0)
+        return (tuple(carry), total)
+    gwrite_ref[...] = jnp.zeros_like(gwrite_ref)
+    gread_ref[...] = jnp.zeros_like(gread_ref)
+    carry, total = lax.fori_loop(0, tb // 8, group, (tuple(carry_ref[b] for b in range(rows)), grate_ref[...]))
+    grate_ref[...] = total
+    for b in range(rows):
+        carry_ref[b] = carry[b]
+
+def scan_back(step, push, grad, write, read, rate, starts, later):
+    rows, length, chans = step.shape
+    states = rate.shape[0]
+    tb = min(TB, length)
+    n = length // tb
+    big = pl.BlockSpec((rows, tb, chans), lambda i: (0, n - 1 - i, 0))
+    thin = pl.BlockSpec((rows, states, tb), lambda i: (0, 0, n - 1 - i))
+    whole = pl.BlockSpec((rows, states, chans), lambda i: (0, 0, 0))
+    flat = pl.BlockSpec((states, chans), lambda i: (0, 0))
+    return pl.pallas_call(back_kernel, grid=(n,),
+        in_specs=[big, big, big, thin, thin, flat, pl.BlockSpec((rows, 1, states, chans), lambda i: (0, n - 1 - i, 0, 0)), whole],
+        out_specs=[big, big, thin, thin, flat],
+        out_shape=[jax.ShapeDtypeStruct((rows, length, chans), f32)] * 2
+                 + [jax.ShapeDtypeStruct((rows, states, length), f32)] * 2
+                 + [jax.ShapeDtypeStruct((states, chans), f32)],
+        scratch_shapes=[pltpu.VMEM((rows, states, chans), f32),
+                        pltpu.VMEM((rows, tb, states, chans), f32),
+                        pltpu.VMEM((rows, tb, states, chans), f32)],
+        compiler_params=params())(step, push, grad, write, read, rate, starts, later)
+
+
+def mixer_forward(normed, weights, same, flags):
     (
         mixer_in,
         conv_taps,
@@ -189,17 +319,15 @@
     )
     step = jax.nn.softplus(step_raw)
     rate = -jnp.exp(decay_log)
-    items = tuple(
-        (to_lanes(value, size) for value in (step, write_in, read_out, source, 1.0 - flags))
-    )
-    lanes = items[0].shape[1]
-    zero = jnp.zeros((lanes,) + rate.shape, jnp.float32)
-    local_end = states_only(zero, items, rate)
-    factors = blocks_first(block_factors(items, rate), rows)
-    total, exclusive = prefix_pairs(factors, blocks_first(local_end, rows), False)
-    incoming = carry_across(total, False)[1]
-    firsts = exclusive[0] * incoming[None] + exclusive[1]
-    scanned = from_lanes(lane_outputs(blocks_back(firsts), items, rate), rows)
+    step_far = jnp.where(flags[:, :, None] > 0, FAR, step)
+    push = step * source
+    write_cols = jnp.swapaxes(write_in, 1, 2)
+    read_cols = jnp.swapaxes(read_out, 1, 2)
+    ends = scan_ends(step_far, push, write_cols, rate * LOG2E)
+    kept = 1.0 - jnp.max(flags, axis=1)
+    factors = jnp.exp(rate[None] * jnp.sum(step, axis=1)[:, None, :]) * kept[:, None, None]
+    incoming = carry_across((factors, ends), False)[1]
+    scanned, firsts = scan_outputs(step_far, push, write_cols, read_cols, rate * LOG2E, incoming)
     result = scanned + skip_gain * source
     gated = (result * jax.nn.silu(gate)).astype(jnp.bfloat16)
     partial_value = jnp.einsum("rte,ed->rtd", gated, mixer_out, preferred_element_type=jnp.float32)
@@ -213,8 +341,11 @@
         step_low,
         step_raw,
         step,
+        step_far,
+        push,
         write_in,
-        read_out,
+        write_cols,
+        read_cols,
         result,
         gated,
         firsts,
@@ -223,7 +354,7 @@
     return (partial_value, cache)
 
 
-def mixer_backward(grad_branch, cache, weights, same, flags, size):
+def mixer_backward(grad_branch, cache, weights, same, flags):
     (
         mixer_in,
         conv_taps,
@@ -245,14 +376,16 @@
         step_low,
         step_raw,
         step,
+        step_far,
+        push,
         write_in,
-        read_out,
+        write_cols,
+        read_cols,
         result,
         gated,
         firsts,
         factors,
     ) = cache
-    rows = step.shape[0]
     grad_gated = jnp.einsum(
         "rtd,ed->rte", grad_branch, mixer_out, preferred_element_type=jnp.float32
     )
@@ -263,56 +396,16 @@
     grad_gate = grad_gated * result * silu_slope(gate)
     grad_skip = jnp.sum(grad_result * source, axis=(0, 1))
     rate = -jnp.exp(decay_log)
-    items = tuple(
-        (
-            to_lanes(value, size)
-            for value in (step, write_in, read_out, source, 1.0 - flags, grad_result)
-        )
-    )
-    lanes = items[0].shape[1]
-    zero = jnp.zeros((lanes,) + rate.shape, jnp.float32)
-
-    def carry_token(held, item):
-        step_now, read_now, keep_now, grad_now = item
-        factor = jnp.exp(step_now[:, None, :] * rate) * keep_now[:, None, None]
-        return (factor * (read_now[:, :, None] * grad_now[:, None, :] + held), None)
-
-    local_back, _ = lax.scan(
-        carry_token, zero, (items[0], items[2], items[4], items[5]), reverse=True
-    )
-    total_back, exclusive_back = prefix_pairs(factors, blocks_first(local_back, rows), True)
-    later = carry_across(total_back, True)[1]
-    carry_in = blocks_back(exclusive_back[0] * later[None] + exclusive_back[1])
-
-    def state_token(held, item):
-        fresh = advance(held, item, rate)
-        return (fresh, (fresh, held))
-
-    _, (after_states, before_states) = lax.scan(state_token, blocks_back(firsts), items[:5])
-
-    def back_token(inner_carry, item):
-        weight_next, rate_total = inner_carry
-        step_now, write_now, read_now, source_now, keep_now, grad_now, state_now, state_before = (
-            item
-        )
-        factor = jnp.exp(step_now[:, None, :] * rate) * keep_now[:, None, None]
-        adjoint = read_now[:, :, None] * grad_now[:, None, :] + weight_next
-        weighted = adjoint * state_before * factor
-        grad_step = jnp.sum(
-            weighted * rate + adjoint * write_now[:, :, None] * source_now[:, None, :], axis=1
-        )
-        grad_write = jnp.sum(adjoint * (step_now * source_now)[:, None, :], axis=2)
-        grad_read = jnp.sum(state_now * grad_now[:, None, :], axis=2)
-        grad_source = jnp.sum(adjoint * write_now[:, :, None], axis=1) * step_now
-        rate_total = rate_total + jnp.sum(weighted * step_now[:, None, :], axis=0)
-        return ((factor * adjoint, rate_total), (grad_step, grad_write, grad_read, grad_source))
-
-    start = (carry_in, jnp.zeros(rate.shape, jnp.float32))
-    (_, grad_rate), lane_grads = lax.scan(
-        back_token, start, items + (after_states, before_states), reverse=True
-    )
-    grad_step, grad_write, grad_read, grad_source = tuple(
-        (from_lanes(value, rows) for value in lane_grads)
+    tail = scan_tail(step_far, grad_result, read_cols, rate * LOG2E)
+    later = carry_across((factors, tail), True)[1]
+    decays, weights_back, write_back, read_back, grad_rate = scan_back(
+        step_far, push, grad_result, write_cols, read_cols, rate * LOG2E, firsts, later
+    )
+    grad_step = decays * (1.0 / LOG2E) + weights_back * source
+    grad_source = weights_back * step
+    grad_write = jnp.swapaxes(write_back, 1, 2)
+    grad_read = jnp.swapaxes(read_back, 1, 2) + write_in * jnp.sum(
+        push * grad_result, axis=2, keepdims=True
     )
     grad_source = grad_source + skip_gain * grad_result
     grad_step_raw = (grad_step * jax.nn.sigmoid(step_raw)).astype(jnp.bfloat16)
@@ -583,7 +676,6 @@
         ],
         axis=-1,
     )
-    size = min(MBLOCK, length)
     reach = -(-WINDOW // length)
     key_place = anchor - reach * length + jnp.arange((reach + 1) * length, dtype=jnp.int32)
     key_docs = doc_numbers(key_place, doc_starts)
@@ -600,7 +692,7 @@
     )
     normed_mix, scale_mix = norm_forward(block_in, norm_gains[0])
     partial_value, cache_mix = mixer_forward(
-        gather_rows(normed_mix.astype(jnp.bfloat16)), mixer_weights, same, flags, size
+        gather_rows(normed_mix.astype(jnp.bfloat16)), mixer_weights, same, flags
     )
     stream_mix = block_in + reduce_rows(partial_value)
     normed_first, scale_first = norm_forward(stream_mix, norm_gains[1])
@@ -658,7 +750,7 @@
     )
     grad_stream = grad_stream + grad_back
     grad_normed, grad_mixer_in, grad_mixer_out, small = mixer_backward(
-        gather_rows(grad_stream.astype(jnp.bfloat16)), cache_mix, mixer_weights, same, flags, size
+        gather_rows(grad_stream.astype(jnp.bfloat16)), cache_mix, mixer_weights, same, flags
     )
     pending = settle(pending, grad_mixer_in, grad_mixer_out)
     grad_back, gain_one = norm_backward(

time: 3820 us -> 1990 us (0.52); the launches traced: 3750 us -> 1980 us
  local copies, waits for them, and re-layouts: 967 us -> 104 us
  other arithmetic: 929 us -> 146 us
  waiting for transfers between devices: 1390 us -> 1110 us
  Pallas kernels: 0 us -> 168 us
    mul x1024 -> x0, local copies, waits for them, and re-layouts: 751 us -> none  [the longest x320 249 us: advance(): step_now[:, None, :] * write_now[:, :, None] * source_now[:, None, :]]
    reduce_scatter x8, waiting for transfers between devices: 880 us -> 477 us  [reduce_rows(): lax.psum_scatter(low, 'tp', scatter_dimension=1, tiled=True)]
    reduce_sum x129 -> x1, other arithmetic: 309 us -> 2.07 us  [mixer_forward(): jnp.sum(step, axis=1)[:, None, :]]
    dynamic_update_slice x160 -> x0, other arithmetic: 219 us -> none  [the longest x64 93.2 us: mixer_backward(): lax.scan(state_token, blocks_back(firsts), items[:5])]
    add x160 -> x1, other arithmetic: 185 us -> 1.3 us  [mixer_backward(): jnp.swapaxes(read_back, 1, 2)]
    pallas_call x0 -> x4, Pallas kernels: none -> 168 us  [the longest x1 85.7 us: scan_back(): pl.pallas_call(back_kernel, grid=(n,), in_specs=[big, big, big, thin, thi...]
    dynamic_update_slice x128 -> x0, local copies, waits for them, and re-layouts: 78.4 us -> none  [the longest x64 39.5 us: lane_outputs(): _, outputs = lax.scan(lane_token, start, items)]
    mul x129 -> x1, other arithmetic: 74.7 us -> 0.03 us  [mixer_forward(): jnp.exp(rate[None] * jnp.sum(step, axis=1)[:, None, :])]
  transfers between devices with their start and end apart: 36 -> 36, of which waited for: 20 -> 26; matrix products, arithmetic and copies ran while one was open for 33% -> 14% of each run, Pallas kernels for 0% -> 6%
where the time goes in v1:
time: 1990 us; the launch traced here: 1980 us
  waiting for transfers between devices  1110 us (56%)
  matrix products  299 us (15%)
  Pallas kernels  168 us (8%)
  other arithmetic  146 us (7%)
  blocking collectives  112 us (6%)
  local copies, waits for them, and re-layouts  104 us (5%)
  starting transfers between devices  22.4 us (1%)
    reduce_scatter x8, waiting for transfers between devices, reduce_rows(): lax.psum_scatter(low, 'tp', scatter_dimension=1, tiled=True)  477 us
    all_gather x8, waiting for transfers between devices, gather_rows(): return lax.all_gather(local, 'tp', axis=1, tiled=True)  426 us
    pallas_call x1, Pallas kernels, scan_back(): pl.pallas_call(back_kernel, grid=(n,), in_specs=[big, big, big, thin, thi...  85.7 us
    reduce_scatter x1, waiting for transfers between devices, shards(): lax.psum_scatter(flat[2].astype(jnp.bfloat16), ('row', 'seq'), scatter_di...  63.1 us
    unnamed x278, local copies, waits for them, and re-layouts  56.1 us
    reduce_scatter x1, waiting for transfers between devices, shards(): lax.psum_scatter(flat[1].astype(jnp.bfloat16), ('row', 'seq'), scatter_di...  43.5 us
    psum x1, blocking collectives, shards(): lax.psum(jnp.stack([gain_one, gain_two, gain_three, gain_four]), ('row',...  41 us
  transfers between devices with their start and end apart: 36, of which 26 were waited for; matrix products, arithmetic and copies ran while one was open for 14% of the time, Pallas kernels for 6%

profile of v1, /device:TPU:0, one launch (start us, length us, event | category | flops | bytes accessed | tf_op | source)
XLA Modules:
  0.0 1977.4 jit_solution(8224937404899819224)
XLA Ops:
  17.2 62.8 %all-gather.12.cloned.1.call-done = bf16[1,1024,1536]{2,1,0:T(8,128)(2,1)} async-done(((bf16[1,256,1536]{2,1,0:T(8,128)(2,1)}), bf16[1,1024,1536]{2,1,0:T(8,128)(2,1)}) %all-gather.12.cloned.1.call-update) | async-done | bytes 3145744 | tf_op jit(solution)/shard_map/all_gather | solution.py:47
  80.0 8.3 fusion.113
  102.2 35.6 %all-reduce.10.cloned.1.call-done = f32[1,1024,128]{1,2,0:T(8,128)} async-done(((f32[1,1024,128]{1,2,0:T(8,128)}), f32[1,1024,128]{1,2,0:T(8,128)}) %all-reduce.10.cloned.1.call-update) | async-done | bytes 524304 | tf_op jit(solution)/shard_map/psum | solution.py:56
  147.1 24.2 %shard_map.340 = f32[1,16,768]{2,1,0:T(8,128)S(1)} custom-call(f32[1,1024,768]{2,1,0:T(8,128)S(1)} %get-tuple-element.514.step_ref, f32[1,1024,768]{2,1,0:T(8,128)} %get-tuple-element.534.push_ref, f32[1,16,1024]{2,1,0:T(8,128)S(1)} %get-tuple-element.520.write_ref, f32[16,768]{1,0:T(8,128)S(1)} %get-tuple-element.522.rate_ref), custom_call_target="tpu_custom_call" | custom-call | tf_op jit(solution)/shard_map/pallas_call | solution.py:125
  171.4 6.1 all-gather.1
  177.4 6.3 all-gather
  190.6 33.8 %shard_map.341 = (f32[1,1024,768]{2,1,0:T(8,128)S(1)}, f32[1,8,16,768]{3,2,1,0:T(8,128)S(1)}) custom-call(f32[1,1024,768]{2,1,0:T(8,128)} %copy-done.2, f32[1,1024,768]{2,1,0:T(8,128)} %get-tuple-element.534.push_ref, f32[1,16,1024]{2,1,0:T(8,128)S(1)} %copy-done.13, f32[1,16,1024]{2,1,0:T(8,128)S(1)} %copy-done.9, f32[16,768]{1,0:T(8,128)S(1)} %copy-done.6, ...), custom_call_target="tpu_custom_call" | custom-call | tf_op jit(solution)/shard_map/pallas_call | solution.py:163
  233.9 60.4 %reduce-scatter.17.cloned.1.call-done = bf16[1,256,1536]{2,1,0:T(8,128)(2,1)} async-done(((bf16[1,1024,1536]{2,1,0:T(8,128)(2,1)}), bf16[1,256,1536]{2,1,0:T(8,128)(2,1)}) %reduce-scatter.17.cloned.1.call-update) | async-done | bytes 786448 | tf_op jit(solution)/shard_map/reduce_scatter | solution.py:52
  298.5 63.6 %all-gather.14.cloned.1.call-done = bf16[1,1024,1536]{2,1,0:T(8,128)(2,1)} async-done(((bf16[1,256,1536]{2,1,0:T(8,128)(2,1)}), bf16[1,1024,1536]{2,1,0:T(8,128)(2,1)}) %all-gather.14.cloned.1.call-update) | async-done | bytes 3145744 | tf_op jit(solution)/shard_map/all_gather | solution.py:47
  362.1 10.2 fusion.61
  380.5 59.0 %reduce-scatter.19.cloned.1.call-done = bf16[1,256,1536]{2,1,0:T(8,128)(2,1)} async-done(((bf16[1,1024,1536]{2,1,0:T(8,128)(2,1)}), bf16[1,256,1536]{2,1,0:T(8,128)(2,1)}) %reduce-scatter.19.cloned.1.call-update) | async-done | bytes 786448 | tf_op jit(solution)/shard_map/reduce_scatter | solution.py:52
  448.7 59.4 %all-gather.16.cloned.1.call-done = bf16[1,1024,1536]{2,1,0:T(8,128)(2,1)} async-done(((bf16[1,256,1536]{2,1,0:T(8,128)(2,1)}), bf16[1,1024,1536]{2,1,0:T(8,128)(2,1)}) %all-gather.16.cloned.1.call-update) | async-done | bytes 3145744 | tf_op jit(solution)/shard_map/all_gather | solution.py:47
  508.1 5.8 fusion.126
  546.5 7.9 fusion.2
  569.6 6.3 fusion.191
  576.0 8.8 fusion.190
  589.5 71.5 %reduce-scatter.21.cloned.1.call-done = bf16[1,256,1536]{2,1,0:T(8,128)(2,1)} async-done(((bf16[1,1024,1536]{2,1,0:T(8,128)(2,1)}), bf16[1,256,1536]{2,1,0:T(8,128)(2,1)}) %reduce-scatter.21.cloned.1.call-update) | async-done | bytes 786448 | tf_op jit(solution)/shard_map/reduce_scatter | solution.py:52
  669.9 59.2 %all-gather.18.cloned.1.call-done = bf16[1,1024,1536]{2,1,0:T(8,128)(2,1)} async-done(((bf16[1,256,1536]{2,1,0:T(8,128)(2,1)}), bf16[1,1024,1536]{2,1,0:T(8,128)(2,1)}) %all-gather.18.cloned.1.call-update) | async-done | bytes 3145744 | tf_op jit(solution)/shard_map/all_gather | solution.py:47
  729.1 12.0 fusion.64
  741.2 52.3 %all-gather.20.cloned.1.call-done = bf16[1,1024,1536]{2,1,0:T(8,128)(2,1)} async-done(((bf16[1,256,1536]{2,1,0:T(8,128)(2,1)}), bf16[1,1024,1536]{2,1,0:T(8,128)(2,1)}) %all-gather.20.cloned.1.call-update) | async-done | bytes 3145744 | tf_op jit(solution)/shard_map/all_gather | solution.py:47
  793.5 10.0 fusion.125
  805.5 10.2 fusion.55
  815.7 9.4 fusion.53
  825.2 49.5 %reduce-scatter.25.cloned.1.call-done = bf16[1,256,1536]{2,1,0:T(8,128)(2,1)} async-done(((bf16[1,1024,1536]{2,1,0:T(8,128)(2,1)}), bf16[1,256,1536]{2,1,0:T(8,128)(2,1)}) %reduce-scatter.25.cloned.1.call-update) | async-done | bytes 786448 | tf_op jit(solution)/shard_map/reduce_scatter | solution.py:52
  878.1 59.3 %reduce-scatter.23.cloned.1.call-done = bf16[1,256,1536]{2,1,0:T(8,128)(2,1)} async-done(((bf16[1,1024,1536]{2,1,0:T(8,128)(2,1)}), bf16[1,256,1536]{2,1,0:T(8,128)(2,1)}) %reduce-scatter.23.cloned.1.call-update) | async-done | bytes 786448 | tf_op jit(solution)/shard_map/reduce_scatter | solution.py:52
  942.5 63.5 %all-gather.22.cloned.1.call-done = bf16[1,1024,1536]{2,1,0:T(8,128)(2,1)} async-done(((bf16[1,256,1536]{2,1,0:T(8,128)(2,1)}), bf16[1,1024,1536]{2,1,0:T(8,128)(2,1)}) %all-gather.22.cloned.1.call-update) | async-done | bytes 3145744 | tf_op jit(solution)/shard_map/all_gather | solution.py:47
  1009.8 8.1 convolution_bitcast_fusion.1
  1017.9 12.5 multiply_reduce_fusion.1
  1030.4 12.3 multiply_reduce_fusion
  1043.1 10.7 constant_dynamic-update-slice_fusion
  1060.1 12.4 multiply_convert_fusion.1
  1079.3 8.1 multiply_convert_fusion
  1087.4 6.0 constant_dynamic-update-slice_fusion.1
  1114.7 18.5 collective-permute-done.6
  1138.6 7.4 fusion.48
  1146.0 58.1 %reduce-scatter.27.cloned.1.call-done = bf16[1,256,1536]{2,1,0:T(8,128)(2,1)} async-done(((bf16[1,1024,1536]{2,1,0:T(8,128)(2,1)}), bf16[1,256,1536]{2,1,0:T(8,128)(2,1)}) %reduce-scatter.27.cloned.1.call-update) | async-done | bytes 786448 | tf_op jit(solution)/shard_map/reduce_scatter | solution.py:52
  1208.4 63.5 %all-gather.24.cloned.1.call-done = bf16[1,1024,1536]{2,1,0:T(8,128)(2,1)} async-done(((bf16[1,256,1536]{2,1,0:T(8,128)(2,1)}), bf16[1,1024,1536]{2,1,0:T(8,128)(2,1)}) %all-gather.24.cloned.1.call-update) | async-done | bytes 3145744 | tf_op jit(solution)/shard_map/all_gather | solution.py:47
  1271.9 10.0 fusion.124
  1283.9 10.2 fusion.58
  1294.1 59.0 %reduce-scatter.29.cloned.1.call-done = bf16[1,256,1536]{2,1,0:T(8,128)(2,1)} async-done(((bf16[1,1024,1536]{2,1,0:T(8,128)(2,1)}), bf16[1,256,1536]{2,1,0:T(8,128)(2,1)}) %reduce-scatter.29.cloned.1.call-update) | async-done | bytes 786448 | tf_op jit(solution)/shard_map/reduce_scatter | solution.py:52
  1358.6 9.6 convolution_convert_fusion.6
  1370.1 10.9 convolution_convert_fusion
  1387.0 8.6 convolution_convert_fusion.3
  1397.4 8.7 convolution_convert_fusion.7
  1408.0 10.9 convolution_convert_fusion.1
  1422.2 11.7 fusion.71
  1433.8 24.4 %shard_map.342 = f32[1,16,768]{2,1,0:T(8,128)S(1)} custom-call(f32[1,1024,768]{2,1,0:T(8,128)S(1)} %copy-done.3, f32[1,1024,768]{2,1,0:T(8,128)} %bitcast.506, f32[1,16,1024]{2,1,0:T(8,128)S(1)} %copy-done.10, f32[16,768]{1,0:T(8,128)S(1)} %copy-done.7), custom_call_target="tpu_custom_call" | custom-call | tf_op jit(solution)/shard_map/pallas_call | solution.py:198
  1458.3 5.6 all-gather.2
  1470.6 85.7 %shard_map.343 = (f32[1,1024,768]{2,1,0:T(8,128)S(1)}, f32[1,1024,768]{2,1,0:T(8,128)}, f32[1,16,1024]{2,1,0:T(8,128)S(1)}, f32[1,16,1024]{2,1,0:T(8,128)S(1)}, f32[16,768]{1,0:T(8,128)S(1)}) custom-call(f32[1,1024,768]{2,1,0:T(8,128)} %copy-done.2, f32[1,1024,768]{2,1,0:T(8,128)} %get-tuple-element.534.push_ref, f32[1,1024,768]{2,1,0:T(8,128)} %bitcast.507, ...), custom_call_target="tpu_custom_call" | custom-call | tf_op jit(solution)/shard_map/pallas_call | solution.py:269
  1562.2 29.2 %all-reduce.13 = bf16[1,1024,128]{1,2,0:T(8,128)(2,1)} all-reduce(f32[1,1024,128]{1,2,0:T(8,128)} %pad_maximum_fusion.16), channel_id=1, replica_groups=mesh['row'=2,'seq'=4,'tp'=4] {'tp'}, use_global_device_ids=true, to_apply=%region_34.35 | all-reduce | flops 131072 | bytes 786432 | tf_op jit(solution)/shard_map/psum | solution.py:56
  1596.1 6.6 convolution_convert_fusion.10
  1602.8 7.2 multiply_multiply_fusion
  1614.1 12.0 scatter-add.31
  1632.0 9.0 scatter-add.34
  1645.2 5.7 multiply_reduce_fusion.5
  1652.1 6.6 fusion.49
  1660.6 8.9 convolution_convert_fusion.2
  1680.7 63.1 %reduce-scatter.37.cloned.1.call-done = bf16[192,2,1024]{2,0,1:T(8,128)(2,1)} async-done(((bf16[1536,2,1024]{2,0,1:T(8,128)(2,1)}), bf16[192,2,1024]{2,0,1:T(8,128)(2,1)}) %reduce-scatter.37.cloned.1.call-update) | async-done | bytes 786448 | tf_op jit(solution)/shard_map/reduce_scatter | solution.py:769
  1746.9 23.5 %all-reduce.4 = (bf16[4,768]{1,0:T(4,128)(2,1)S(1)}, bf16[768]{0:T(1024)(128)(2,1)S(1)}, bf16[768]{0:T(1024)(128)(2,1)S(1)}, bf16[16,768]{1,0:T(8,128)(2,1)S(1)}, bf16[768]{0:T(1024)(128)(2,1)S(1)}) all-reduce(bf16[4,768]{1,0:T(4,128)(2,1)S(1)} %pad_maximum_fusion.18, ...), channel_id=1, replica_groups=mesh['row'=2,'seq'=4,'tp'=4] {'row','seq'}, use_global_device_ids=true, to_apply=%region_47.48 | all-reduce | flops 17664 | bytes 70656 | tf_op jit(solution)/shard_map/psum | solution.py:789
  1773.4 27.3 %all-reduce.12.cloned.1.call-done = (bf16[768,128]{1,0:T(8,128)(2,1)}, bf16[96,768]{1,0:T(8,128)(2,1)}) async-done(((bf16[768,128]{1,0:T(8,128)(2,1)}, bf16[96,768]{1,0:T(8,128)(2,1)}), (bf16[768,128]{1,0:T(8,128)(2,1)}, bf16[96,768]{1,0:T(8,128)(2,1)})) %all-reduce.12.cloned.1.call-update) | async-done | bytes 344080 | tf_op jit(solution)/shard_map/psum | solution.py:791
  1804.0 43.5 %reduce-scatter.35.cloned.1.call-done = bf16[768,192]{0,1:T(8,128)(2,1)} async-done(((bf16[768,1536]{0,1:T(8,128)(2,1)}), bf16[768,192]{0,1:T(8,128)(2,1)}) %reduce-scatter.35.cloned.1.call-update) | async-done | bytes 294928 | tf_op jit(solution)/shard_map/reduce_scatter | solution.py:766
  1849.4 60.8 %reduce-scatter.31.cloned.1.call-done = bf16[1,256,1536]{2,1,0:T(8,128)(2,1)} async-done(((bf16[1,1024,1536]{2,1,0:T(8,128)(2,1)}), bf16[1,256,1536]{2,1,0:T(8,128)(2,1)}) %reduce-scatter.31.cloned.1.call-update) | async-done | bytes 786448 | tf_op jit(solution)/shard_map/reduce_scatter | solution.py:52
  1911.9 41.0 %psum.72 = f32[4,1536]{1,0:T(4,128)} all-reduce(f32[4,1536]{1,0:T(4,128)S(1)} %pad_maximum_fusion.17), channel_id=1, replica_groups=mesh['row'=2,'seq'=4,'tp'=4] {'row','seq','tp'}, use_global_device_ids=true, to_apply=%region_41.42 | all-reduce | flops 6144 | bytes 49152 | tf_op jit(solution)/shard_map/psum | solution.py:797
  1956.8 11.2 reduce-scatter.33.cloned.1.call-done
  (485 shorter events, 282.6 us)
Async XLA Ops:
  7.2 500.9 %copy-start = (bf16[1536,3,384]{2,0,1:T(8,128)(2,1)S(1)}, bf16[1536,3,384]{2,0,1:T(8,128)(2,1)}, u32[]{:S(2)}) copy-start(bf16[1536,3,384]{2,0,1:T(8,128)(2,1)} %param.55) | copy-start | bytes 10616836
  7.2 72.8 %all-gather.12.cloned.1.call-start = ((), (), s32[]{:S(2)}) async-start(), calls=%async_computation.16 | async-start | bytes 3932160 | tf_op jit(solution)/shard_map/all_gather | solution.py:47
  10.6 285.6 %copy-start.76 = (f32[1536]{0:T(1024)}, f32[1536]{0:T(1024)S(1)}, u32[]{:S(2)}) copy-start(f32[1536]{0:T(1024)S(1)} %get-tuple-element.454) | copy-start | bytes 18436
  10.6 431.0 %copy-start.68 = (f32[1536]{0:T(1024)}, f32[1536]{0:T(1024)S(1)}, u32[]{:S(2)}) copy-start(f32[1536]{0:T(1024)S(1)} %get-tuple-element.456) | copy-start | bytes 18436
  13.7 124.2 %all-reduce.10.cloned.1.call-start = ((), (), s32[]{:S(2)}) async-start(), calls=%async_computation.17 | async-start | bytes 1048576 | tf_op jit(solution)/shard_map/psum | solution.py:56
  88.6 2.7 collective-permute-start
  98.3 195.9 %reduce-scatter.17.cloned.1.call-start = ((), (), s32[]{:S(2)}) async-start(), calls=%async_computation.18 | async-start | bytes 3932160 | tf_op jit(solution)/shard_map/reduce_scatter | solution.py:52
  145.4 26.0 %copy-start.2 = (f32[1,1024,768]{2,1,0:T(8,128)}, f32[1,1024,768]{2,1,0:T(8,128)S(1)}, u32[]{:S(2)}) copy-start(f32[1,1024,768]{2,1,0:T(8,128)S(1)} %get-tuple-element.514.step_ref) | copy-start | bytes 9437188
  145.4 25.9 %copy-start.5 = (f32[16,768]{1,0:T(8,128)}, f32[16,768]{1,0:T(8,128)S(1)}, u32[]{:S(2)}) copy-start(f32[16,768]{1,0:T(8,128)S(1)} %get-tuple-element.522.rate_ref) | copy-start | bytes 147460
  147.1 24.2 %copy-start.12 = (f32[1,16,1024]{2,1,0:T(8,128)}, f32[1,16,1024]{2,1,0:T(8,128)S(1)}, u32[]{:S(2)}) copy-start(f32[1,16,1024]{2,1,0:T(8,128)S(1)} %get-tuple-element.520.write_ref) | copy-start | bytes 196612
  190.6 33.9 %copy-start.31 = (bf16[1,1024,768]{2,1,0:T(8,128)(2,1)S(1)}, bf16[1,1024,768]{2,1,0:T(8,128)(2,1)}, u32[]{:S(2)}) copy-start(bf16[1,1024,768]{2,1,0:T(8,128)(2,1)} %copy-done.30) | copy-start | bytes 4718596
  190.6 33.9 %copy-start.113 = (f32[768]{0:T(1024)S(1)}, f32[768]{0:T(1024)}, u32[]{:S(2)}) copy-start(f32[768]{0:T(1024)} %param.51) | copy-start | bytes 9220
  233.9 128.2 %all-gather.14.cloned.1.call-start = ((), (), s32[]{:S(2)}) async-start(), calls=%async_computation.19 | async-start | bytes 3932160 | tf_op jit(solution)/shard_map/all_gather | solution.py:47
  298.4 141.1 %reduce-scatter.19.cloned.1.call-start = ((), (), s32[]{:S(2)}) async-start(), calls=%async_computation.20 | async-start | bytes 3932160 | tf_op jit(solution)/shard_map/reduce_scatter | solution.py:52
  380.5 65.8 %copy-start.97 = (s32[1024]{0:T(1024)S(1)}, s32[1024]{0:T(1024)}, u32[]{:S(2)}) copy-start(s32[1024]{0:T(1024)} %copy-done.96) | copy-start | bytes 12292
  380.5 66.4 %copy-start.84 = (s32[1024]{0:T(1024)S(1)}, s32[1024]{0:T(1024)}, u32[]{:S(2)}) copy-start(s32[1024]{0:T(1024)} %copy-done.83) | copy-start | bytes 12292
  380.5 127.6 %all-gather.16.cloned.1.call-start = ((), (), s32[]{:S(2)}) async-start(), calls=%async_computation.21 | async-start | bytes 3932160 | tf_op jit(solution)/shard_map/all_gather | solution.py:47
  444.4 216.5 %reduce-scatter.21.cloned.1.call-start = ((), (), s32[]{:S(2)}) async-start(), calls=%async_computation.22 | async-start | bytes 3932160 | tf_op jit(solution)/shard_map/reduce_scatter | solution.py:52
  517.6 20.4 %collective-permute-start.4 = (bf16[1,1024,3,128]{3,1,2,0:T(8,128)(2,1)}, bf16[1,1024,3,128]{3,1,2,0:T(8,128)(2,1)}, u32[]{:S(2)}, u32[]{:S(2)}) collective-permute-start(bf16[1,1024,3,128]{3,1,2,0:T(8,128)(2,1)} %bitcast.512), channel_id=1, source_target_pairs={{0,4},{4,8},{8,12},{1,5},{5,9},{9,13},{2,6},{6,10},{10,14},{3,7},{... | collective-permute-start | bytes 2359304 | tf_op jit(solution)/shard_map/ppermute | solution.py:39
  520.2 21.0 %collective-permute-start.3 = (bf16[1,1024,3,128]{3,1,2,0:T(8,128)(2,1)}, bf16[1,1024,3,128]{3,1,2,0:T(8,128)(2,1)}, u32[]{:S(2)}, u32[]{:S(2)}) collective-permute-start(bf16[1,1024,3,128]{3,1,2,0:T(8,128)(2,1)} %bitcast.513), channel_id=1, source_target_pairs={{0,8},{4,12},{1,9},{5,13},{2,10},{6,14},{3,11},{7,15},{16,24},{20,... | collective-permute-start | bytes 2359304 | tf_op jit(solution)/shard_map/ppermute | solution.py:39
  531.3 35.3 %collective-permute-start.2 = (bf16[1,1024,3,128]{1,3,2,0:T(8,128)(2,1)}, bf16[1,1024,3,128]{1,3,2,0:T(8,128)(2,1)}, u32[]{:S(2)}, u32[]{:S(2)}) collective-permute-start(bf16[1,1024,3,128]{1,3,2,0:T(8,128)(2,1)} %get-tuple-element.517), channel_id=1, source_target_pairs={{0,4},{4,8},{8,12},{1,5},{5,9},{9,13},{2,6},{6,10},{10,14},{3,7},{... | collective-permute-start | bytes 2359304 | tf_op jit(solution)/shard_map/ppermute | solution.py:39
  533.6 33.0 %collective-permute-start.1 = (bf16[1,1024,3,128]{1,3,2,0:T(8,128)(2,1)}, bf16[1,1024,3,128]{1,3,2,0:T(8,128)(2,1)}, u32[]{:S(2)}, u32[]{:S(2)}) collective-permute-start(bf16[1,1024,3,128]{1,3,2,0:T(8,128)(2,1)} %get-tuple-element.517), channel_id=1, source_target_pairs={{0,8},{4,12},{1,9},{5,13},{2,10},{6,14},{3,11},{7,15},{16,24},{20,... | collective-permute-start | bytes 2359304 | tf_op jit(solution)/shard_map/ppermute | solution.py:39
  546.5 23.1 %copy-start.19 = (f32[3,512,2560]{2,1,0:T(8,128)}, f32[3,512,2560]{2,1,0:T(8,128)S(1)}, u32[]{:S(2)}) copy-start(f32[3,512,2560]{2,1,0:T(8,128)S(1)} %get-tuple-element.537) | copy-start | bytes 47185924
  589.4 139.7 %all-gather.18.cloned.1.call-start = ((), (), s32[]{:S(2)}) async-start(), calls=%async_computation.23 | async-start | bytes 3932160 | tf_op jit(solution)/shard_map/all_gather | solution.py:47
  665.4 128.0 %all-gather.20.cloned.1.call-start = ((), (), s32[]{:S(2)}) async-start(), calls=%async_computation.25 | async-start | bytes 3932160 | tf_op jit(solution)/shard_map/all_gather | solution.py:47
  669.8 204.9 %reduce-scatter.25.cloned.1.call-start = ((), (), s32[]{:S(2)}) async-start(), calls=%async_computation.26 | async-start | bytes 3932160 | tf_op jit(solution)/shard_map/reduce_scatter | solution.py:52
  815.7 121.7 %reduce-scatter.23.cloned.1.call-start = ((), (), s32[]{:S(2)}) async-start(), calls=%async_computation.24 | async-start | bytes 3932160 | tf_op jit(solution)/shard_map/reduce_scatter | solution.py:52
  825.2 180.8 %all-gather.22.cloned.1.call-start = ((), (), s32[]{:S(2)}) async-start(), calls=%async_computation.27 | async-start | bytes 3932160 | tf_op jit(solution)/shard_map/all_gather | solution.py:47
  942.3 261.8 %reduce-scatter.27.cloned.1.call-start = ((), (), s32[]{:S(2)}) async-start(), calls=%async_computation.28 | async-start | bytes 3932160 | tf_op jit(solution)/shard_map/reduce_scatter | solution.py:52
  1057.1 52.2 %collective-permute-start.7 = (bf16[1,1024,3,128]{1,3,2,0:T(8,128)(2,1)}, bf16[1,1024,3,128]{1,3,2,0:T(8,128)(2,1)}, u32[]{:S(2)}, u32[]{:S(2)}) collective-permute-start(bf16[1,1024,3,128]{1,3,2,0:T(8,128)(2,1)} %slice.637), channel_id=1, source_target_pairs={{4,0},{8,4},{12,8},{5,1},{9,5},{13,9},{6,2},{10,6},{14,10},{7,3},{... | collective-permute-start | bytes 2359304 | tf_op jit(solution)/shard_map/ppermute | solution.py:39
  1058.4 50.9 %collective-permute-start.8 = (bf16[1,1024,3,128]{1,3,2,0:T(8,128)(2,1)}, bf16[1,1024,3,128]{1,3,2,0:T(8,128)(2,1)}, u32[]{:S(2)}, u32[]{:S(2)}) collective-permute-start(bf16[1,1024,3,128]{1,3,2,0:T(8,128)(2,1)} %slice.636), channel_id=1, source_target_pairs={{8,0},{12,4},{9,1},{13,5},{10,2},{14,6},{11,3},{15,7},{24,16},{28,... | collective-permute-start | bytes 2359304 | tf_op jit(solution)/shard_map/ppermute | solution.py:39
  1060.1 19.2 slice-start
  1100.7 14.0 collective-permute-start.5
  1102.0 31.2 %collective-permute-start.6 = (bf16[1,1024,3,128]{1,3,2,0:T(8,128)(2,1)}, bf16[1,1024,3,128]{1,3,2,0:T(8,128)(2,1)}, u32[]{:S(2)}, u32[]{:S(2)}) collective-permute-start(bf16[1,1024,3,128]{1,3,2,0:T(8,128)(2,1)} %slice.638), channel_id=1, source_target_pairs={{8,0},{12,4},{9,1},{13,5},{10,2},{14,6},{11,3},{15,7},{24,16},{28,... | collective-permute-start | bytes 2359304 | tf_op jit(solution)/shard_map/ppermute | solution.py:39
  1146.0 58.2 %copy-start.25 = (f32[1,256,1536]{2,1,0:T(8,128)S(1)}, f32[1,256,1536]{2,1,0:T(8,128)}, u32[]{:S(2)}) copy-start(f32[1,256,1536]{2,1,0:T(8,128)} %copy-done.23) | copy-start | bytes 4718596
  1146.0 58.2 %copy-start.39 = (bf16[1,256,1536]{2,1,0:T(8,128)(2,1)S(1)}, bf16[1,256,1536]{2,1,0:T(8,128)(2,1)}, u32[]{:S(2)}) copy-start(bf16[1,256,1536]{2,1,0:T(8,128)(2,1)} %reduce-scatter.19.cloned.1.call-done) | copy-start | bytes 2359300
  1146.0 58.2 %copy-start.69 = (f32[1536]{0:T(1024)S(1)}, f32[1536]{0:T(1024)}, u32[]{:S(2)}) copy-start(f32[1536]{0:T(1024)} %copy-done.68) | copy-start | bytes 18436
  1146.0 58.2 %copy-start.101 = (f32[256]{0:T(256)S(1)}, f32[256]{0:T(256)}, u32[]{:S(2)}) copy-start(f32[256]{0:T(256)} %copy-done.100) | copy-start | bytes 3076
  1146.0 125.9 %all-gather.24.cloned.1.call-start = ((), (), s32[]{:S(2)}) async-start(), calls=%async_computation.29 | async-start | bytes 3932160 | tf_op jit(solution)/shard_map/all_gather | solution.py:47
  1208.2 145.0 %reduce-scatter.29.cloned.1.call-start = ((), (), s32[]{:S(2)}) async-start(), calls=%async_computation.30 | async-start | bytes 3932160 | tf_op jit(solution)/shard_map/reduce_scatter | solution.py:52
  1294.1 59.1 %copy-start.77 = (f32[1536]{0:T(1024)S(1)}, f32[1536]{0:T(1024)}, u32[]{:S(2)}) copy-start(f32[1536]{0:T(1024)} %copy-done.76) | copy-start | bytes 18436
  1294.1 59.1 %copy-start.107 = (f32[256]{0:T(256)S(1)}, f32[256]{0:T(256)}, u32[]{:S(2)}) copy-start(f32[256]{0:T(256)} %copy-done.106) | copy-start | bytes 3076
  1294.1 128.1 %all-gather.26.cloned.1.call-start = ((), (), s32[]{:S(2)}) async-start(), calls=%async_computation.31 | async-start | bytes 3932160 | tf_op jit(solution)/shard_map/all_gather | solution.py:47
  1358.5 311.0 %reduce-scatter.47.cloned.1.call-start = ((), (), s32[]{:S(2)}) async-start(), calls=%async_computation.40 | async-start | bytes 3538944 | tf_op jit(solution)/shard_map/reduce_scatter | solution.py:784
  1368.2 303.3 %reduce-scatter.45.cloned.1.call-start = ((), (), s32[]{:S(2)}) async-start(), calls=%async_computation.39 | async-start | bytes 7077888 | tf_op jit(solution)/shard_map/reduce_scatter | solution.py:781
  1381.0 293.6 %reduce-scatter.43.cloned.1.call-start = ((), (), s32[]{:S(2)}) async-start(), calls=%async_computation.38 | async-start | bytes 1327104 | tf_op jit(solution)/shard_map/reduce_scatter | solution.py:778
  1386.9 289.4 %reduce-scatter.41.cloned.1.call-start = ((), (), s32[]{:S(2)}) async-start(), calls=%async_computation.37 | async-start | bytes 3981312 | tf_op jit(solution)/shard_map/reduce_scatter | solution.py:775
  1395.5 283.0 %reduce-scatter.39.cloned.1.call-start = ((), (), s32[]{:S(2)}) async-start(), calls=%async_computation.36 | async-start | bytes 3538944 | tf_op jit(solution)/shard_map/reduce_scatter | solution.py:772
  1406.1 337.6 %reduce-scatter.37.cloned.1.call-start = ((), (), s32[]{:S(2)}) async-start(), calls=%async_computation.35 | async-start | bytes 7077888 | tf_op jit(solution)/shard_map/reduce_scatter | solution.py:769
  1418.9 381.8 %all-reduce.12.cloned.1.call-start = ((), (), s32[]{:S(2)}) async-start(), calls=%async_computation.41 | async-start | bytes 688128 | tf_op jit(solution)/shard_map/psum | solution.py:791
  1470.5 85.7 %copy-start.32 = (bf16[1,1024,768]{2,1,0:T(8,128)(2,1)S(1)}, bf16[1,1024,768]{2,1,0:T(8,128)(2,1)}, u32[]{:S(2)}) copy-start(bf16[1,1024,768]{2,1,0:T(8,128)(2,1)} %copy-done.30) | copy-start | bytes 4718596
  1470.6 85.7 %copy-start.51 = (f32[1024,768]{1,0:T(8,128)S(1)}, f32[1024,768]{1,0:T(8,128)}, u32[]{:S(2)}) copy-start(f32[1024,768]{1,0:T(8,128)} %copy-done.50) | copy-start | bytes 9437188
  1470.6 85.7 %copy-start.103 = (f32[768]{0:T(1024)S(1)}, f32[768]{0:T(1024)}, u32[]{:S(2)}) copy-start(f32[768]{0:T(1024)} %param.49) | copy-start | bytes 9220
  1559.5 32.0 %copy-start.33 = (bf16[1,1024,768]{2,1,0:T(8,128)(2,1)S(1)}, bf16[1,1024,768]{2,1,0:T(8,128)(2,1)}, u32[]{:S(2)}) copy-start(bf16[1,1024,768]{2,1,0:T(8,128)(2,1)} %copy-done.30) | copy-start | bytes 4718596
  1561.4 32.3 %copy-start.46 = (bf16[1,1024,768]{2,1,0:T(8,128)(2,1)S(1)}, bf16[1,1024,768]{2,1,0:T(8,128)(2,1)}, u32[]{:S(2)}) copy-start(bf16[1,1024,768]{2,1,0:T(8,128)(2,1)} %copy-done.45) | copy-start | bytes 4718596
  1595.9 251.7 %reduce-scatter.35.cloned.1.call-start = ((), (), s32[]{:S(2)}) async-start(), calls=%async_computation.34 | async-start | bytes 2654208 | tf_op jit(solution)/shard_map/reduce_scatter | solution.py:766
  1602.7 307.4 %reduce-scatter.31.cloned.1.call-start = ((), (), s32[]{:S(2)}) async-start(), calls=%async_computation.32 | async-start | bytes 3932160 | tf_op jit(solution)/shard_map/reduce_scatter | solution.py:52
  1641.9 3.3 collective-permute-start.9
  1658.7 309.2 %reduce-scatter.33.cloned.1.call-start = ((), (), s32[]{:S(2)}) async-start(), calls=%async_computation.33 | async-start | bytes 5308416 | tf_op jit(solution)/shard_map/reduce_scatter | solution.py:763
  1674.6 72.2 %copy-start.18 = (f32[16,768]{1,0:T(8,128)S(1)}, f32[16,768]{1,0:T(8,128)}, u32[]{:S(2)}) copy-start(f32[16,768]{1,0:T(8,128)} %copy-done.17) | copy-start | bytes 147460
  1674.6 72.2 %copy-start.72 = (f32[16,768]{1,0:T(8,128)S(1)}, f32[16,768]{1,0:T(8,128)}, u32[]{:S(2)}) copy-start(f32[16,768]{1,0:T(8,128)} %param.50) | copy-start | bytes 147460
  1678.3 231.8 %copy-start.34 = (f32[1,256,1536]{2,1,0:T(8,128)S(1)}, f32[1,256,1536]{2,1,0:T(8,128)}, u32[]{:S(2)}) copy-start(f32[1,256,1536]{2,1,0:T(8,128)} %param.41) | copy-start | bytes 4718596
  1678.3 231.8 %copy-start.75 = (f32[1536]{0:T(1024)S(1)}, f32[1536]{0:T(1024)}, u32[]{:S(2)}) copy-start(f32[1536]{0:T(1024)} %copy-done.74) | copy-start | bytes 18436
  1678.3 231.8 %copy-start.105 = (f32[256]{0:T(256)S(1)}, f32[256]{0:T(256)}, u32[]{:S(2)}) copy-start(f32[256]{0:T(256)} %copy-done.104) | copy-start | bytes 3076
  (108 other events, 523.7 us)
Sparse Core Ops, SparseCore 0:
  13.8 66.1 all-gather.11
  98.4 39.3 all-reduce.9
  234.0 60.2 reduce-scatter.16
  298.5 63.5 all-gather.13
  380.6 58.8 reduce-scatter.18
  444.6 63.5 all-gather.15
  589.5 71.3 reduce-scatter.20
  665.6 63.5 all-gather.17
  731.3 62.1 all-gather.19
  815.8 58.8 reduce-scatter.24
  877.0 60.2 reduce-scatter.22
  942.4 63.5 all-gather.21
  1146.1 58.0 reduce-scatter.26
  1208.3 63.5 all-gather.23
  1294.2 58.9 reduce-scatter.28
  1358.6 63.5 all-gather.25
  1425.4 45.0 reduce-scatter.46
  1474.1 61.7 reduce-scatter.44
  1539.8 36.8 reduce-scatter.42
  1580.4 48.0 reduce-scatter.40
  1632.3 46.2 reduce-scatter.38
  1681.9 61.7 reduce-scatter.36
  1747.8 52.7 all-reduce.11
  1804.2 43.2 reduce-scatter.34
  1849.8 60.2 reduce-scatter.30
  1913.4 54.4 reduce-scatter.32

commit v2 on v1

v2 whole, which is shorter than its diff:
```python
import jax
import jax.numpy as jnp
from jax import lax
from jax.experimental import pallas as pl
from jax.experimental.pallas import tpu as pltpu
from jax.sharding import PartitionSpec as P

HDIM = 128
WINDOW = 2048
f32 = jnp.float32
LOG2E = 1.4426950408889634
FAR = 1e30
QBLOCK = 256


epsilon = 1e-05
masked_score = -1e30


def carried_in(state, span, rate, axis, backward):
    count, mine = (lax.axis_size(axis), lax.axis_index(axis))
    both = jnp.concatenate([state, span[:, None, :]], axis=1)
    pieces = lax.all_gather(both, axis)
    if backward:
        mine = count - 1 - mine
    total = jnp.zeros_like(state)
    for position in range(count - 1):
        piece = pieces[count - 1 - position if backward else position]
        longer = jnp.exp(rate[None] * piece[:, -1:, :]) * total + piece[:, :-1]
        total = jnp.where(position < mine, longer, total)
    return total


def from_behind(x, axis, by):
    peers = lax.axis_size(axis)
    pairs = [(i, i + by) for i in range(peers) if 0 <= i + by < peers]
    return lax.ppermute(x, axis, pairs)


def gather_rows(local):
    return lax.all_gather(local, "tp", axis=1, tiled=True)


def reduce_rows(partial_value, event=()):
    low = after(partial_value.astype(jnp.bfloat16), event)
    return lax.psum_scatter(low, "tp", scatter_dimension=1, tiled=True).astype(jnp.float32)


def after(value, *events):
    marks = [event[(0,) * event.ndim].astype(jnp.float32) for event in jax.tree.leaves(events)]
    if not marks:
        return value
    return value + (sum(marks) * 0.0).astype(value.dtype)


def spread_sum(value, axes, kind):
    for axis in axes:
        flip = 1
        while flip < lax.axis_size(axis):
            other = partner(value.astype(kind), axis, flip)
            value = value + other.astype(value.dtype)
            flip *= 2
    return value


def partner(x, axis, flip):
    return lax.ppermute(x, axis, [(i, i ^ flip) for i in range(lax.axis_size(axis))])


def channel_total(partial_value):
    rows, count = (partial_value.shape[0], lax.axis_size("tp"))
    low = partial_value.astype(jnp.bfloat16)
    parts = lax.all_to_all(low, "tp", split_axis=1, concat_axis=0, tiled=True)
    parts = parts.reshape((count, rows) + parts.shape[1:]).astype(jnp.float32)
    total = jnp.sum(parts, axis=0).astype(jnp.bfloat16)
    return lax.all_gather(total, "tp", axis=1, tiled=True)


def plane_first(grad):
    if lax.axis_size("row") != 2:
        return (grad.astype(jnp.bfloat16),)
    held = grad.reshape((2, 2, 2, grad.shape[0] // 8) + grad.shape[1:])
    place = lax.axis_index("seq") % 2
    given = lax.dynamic_slice_in_dim(held, 1 - place, 1, axis=2).astype(jnp.bfloat16)
    kept = lax.dynamic_slice_in_dim(held, place, 1, axis=2).astype(jnp.bfloat16)
    return (given, kept)


def joined(given, kept, name, flip):
    other = partner(given, name, flip).astype(jnp.float32)
    return kept.astype(jnp.float32) + other


def plane_second(given, kept=None):
    if kept is None:
        return lax.psum_scatter(given, ("row", "seq"), scatter_dimension=0, tiled=True)
    row = lax.axis_index("row")
    held = joined(given, kept, "seq", 1).astype(jnp.bfloat16)
    given = lax.dynamic_slice_in_dim(held, 1 - row, 1, axis=0)
    held = joined(given, lax.dynamic_slice_in_dim(held, row, 1, axis=0), "row", 1)
    return held.astype(jnp.bfloat16)


def plane_third(held, event=()):
    if lax.axis_size("row") != 2:
        return held.astype(jnp.float32)
    seq = lax.axis_index("seq")
    given = after(lax.dynamic_slice_in_dim(held, 1 - seq // 2, 1, axis=1), event)
    held = joined(given, lax.dynamic_slice_in_dim(held, seq // 2, 1, axis=1), "seq", 2)
    return held.reshape(held.shape[3:])


def doc_numbers(positions, starts):
    return jnp.sum((starts[:, None, :] <= positions[None, :, None]).astype(jnp.int32), axis=-1)


def norm_forward(stream, gain):
    scale = lax.rsqrt(jnp.mean(stream * stream, axis=-1, keepdims=True) + epsilon)
    return (stream * scale * gain, scale)


def norm_backward(stream, scale, gain, grad_normed):
    unit = stream * scale
    scaled = grad_normed * gain
    return scale * (scaled - unit * jnp.mean(scaled * unit, axis=-1, keepdims=True))


def gain_share(partial_value, normed, gain):
    product = partial_value.astype(jnp.float32) * normed.astype(jnp.float32)
    return jnp.sum(product, axis=(0, 1)) / gain


def silu_slope(value):
    logistic = jax.nn.sigmoid(value)
    return logistic * (1.0 + value * (1.0 - logistic))


TB = 128
UNROLL = 64
UNROLL_BACK = 32
VM = 48 * 1024 * 1024

def cost(microseconds):
    return pl.CostEstimate(
        flops=int(microseconds * 1e9), bytes_accessed=int(microseconds * 3e6), transcendentals=0
    )


def params():
    return pltpu.CompilerParams(vmem_limit_bytes=VM, dimension_semantics=("arbitrary",))

def turned(ref, b, base, tb):
    return pltpu.roll(ref[b], lax.rem(tb - base, tb), axis=1)

def ends_kernel(step_ref, push_ref, write_ref, rate_ref, end_ref):
    rows, tb = step_ref.shape[0], step_ref.shape[1]
    @pl.when(pl.program_id(0) == 0)
    def _():
        end_ref[...] = jnp.zeros_like(end_ref)
    def group(j, held):
        base = pl.multiple_of(j * UNROLL, UNROLL)
        held = list(held)
        for b in range(rows):
            steps = step_ref[b, pl.ds(base, UNROLL), :]
            pushes = push_ref[b, pl.ds(base, UNROLL), :]
            writes = turned(write_ref, b, base, tb)
            for k in range(UNROLL):
                factor = jnp.exp2(steps[k:k+1] * rate_ref[...])
                held[b] = factor * held[b] + writes[:, k:k+1] * pushes[k:k+1]
        return tuple(held)
    held = lax.fori_loop(0, tb // UNROLL, group, tuple(end_ref[b] for b in range(rows)))
    for b in range(rows):
        end_ref[b] = held[b]

def scan_ends(step, push, write, rate):
    rows, length, chans = step.shape
    states = rate.shape[0]
    tb = min(TB, length)
    big = pl.BlockSpec((rows, tb, chans), lambda i: (0, i, 0))
    thin = pl.BlockSpec((rows, states, tb), lambda i: (0, 0, i))
    return pl.pallas_call(ends_kernel, grid=(length // tb,),
        in_specs=[big, big, thin, pl.BlockSpec((states, chans), lambda i: (0, 0))],
        out_specs=pl.BlockSpec((rows, states, chans), lambda i: (0, 0, 0)),
        out_shape=jax.ShapeDtypeStruct((rows, states, chans), f32),
        cost_estimate=cost(12), compiler_params=params())(step, push, write, rate)

def picker(tb):
    row = lax.broadcasted_iota(jnp.int32, (tb, tb * 8), 0)
    column = lax.broadcasted_iota(jnp.int32, (tb, tb * 8), 1)
    inside = (column >= row * 8) & (column < row * 8 + 8)
    return jnp.where(inside, 1.0, 0.0).astype(jnp.bfloat16)


def folded(value):
    return sum(value[i : i + 8] for i in range(0, value.shape[0], 8))


def across(value):
    return sum(value[:, i : i + 128] for i in range(0, value.shape[1], 128))


def mat(left, right, dims):
    return lax.dot_general(left, right, (dims, ((), ())), preferred_element_type=f32)


def outputs_kernel(step_ref, push_ref, write_ref, read_ref, rate_ref, first_ref, out_ref, start_ref, held_ref, part_ref):
    rows, tb = step_ref.shape[0], step_ref.shape[1]
    @pl.when(pl.program_id(0) == 0)
    def _():
        held_ref[...] = first_ref[...]
    start_ref[:, 0] = held_ref[...]
    for b in range(rows):
        def group(j, held):
            base = pl.multiple_of(j * UNROLL, UNROLL)
            steps = step_ref[b, pl.ds(base, UNROLL), :]
            pushes = push_ref[b, pl.ds(base, UNROLL), :]
            writes = turned(write_ref, b, base, tb)
            reads = turned(read_ref, b, base, tb)
            for k in range(UNROLL):
                factor = jnp.exp2(steps[k:k+1] * rate_ref[...])
                held = factor * held + writes[:, k:k+1] * pushes[k:k+1]
                part_ref[pl.ds(pl.multiple_of((base + k) * 8, 8), 8), :] = folded(held * reads[:, k:k+1])
            return held
        held_ref[b] = lax.fori_loop(0, tb // UNROLL, group, held_ref[b])
        high = part_ref[...].astype(jnp.bfloat16)
        low = (part_ref[...] - high.astype(f32)).astype(jnp.bfloat16)
        out_ref[b] = mat(picker(tb), high, ((1,), (0,))) + mat(picker(tb), low, ((1,), (0,)))

def scan_outputs(step, push, write, read, rate, first):
    rows, length, chans = step.shape
    states = rate.shape[0]
    tb = min(TB, length)
    big = pl.BlockSpec((rows, tb, chans), lambda i: (0, i, 0))
    thin = pl.BlockSpec((rows, states, tb), lambda i: (0, 0, i))
    whole = pl.BlockSpec((rows, states, chans), lambda i: (0, 0, 0))
    return pl.pallas_call(outputs_kernel, grid=(length // tb,),
        in_specs=[big, big, thin, thin, pl.BlockSpec((states, chans), lambda i: (0, 0)), whole],
        out_specs=[big, pl.BlockSpec((rows, 1, states, chans), lambda i: (0, i, 0, 0))],
        out_shape=[jax.ShapeDtypeStruct((rows, length, chans), f32),
                   jax.ShapeDtypeStruct((rows, length // tb, states, chans), f32)],
        scratch_shapes=[pltpu.VMEM((rows, states, chans), f32), pltpu.VMEM((tb * 8, chans), f32)],
        cost_estimate=cost(21), compiler_params=params())(step, push, write, read, rate, first)

def tail_kernel(step_ref, grad_ref, read_ref, rate_ref, end_ref):
    rows, tb = step_ref.shape[0], step_ref.shape[1]
    @pl.when(pl.program_id(0) == 0)
    def _():
        end_ref[...] = jnp.zeros_like(end_ref)
    def group(j, held):
        base = pl.multiple_of(tb - UNROLL - j * UNROLL, UNROLL)
        held = list(held)
        for b in range(rows):
            steps = step_ref[b, pl.ds(base, UNROLL), :]
            grads = grad_ref[b, pl.ds(base, UNROLL), :]
            reads = turned(read_ref, b, base, tb)
            for k in range(UNROLL - 1, -1, -1):
                factor = jnp.exp2(steps[k:k+1] * rate_ref[...])
                held[b] = factor * (held[b] + reads[:, k:k+1] * grads[k:k+1])
        return tuple(held)
    held = lax.fori_loop(0, tb // UNROLL, group, tuple(end_ref[b] for b in range(rows)))
    for b in range(rows):
        end_ref[b] = held[b]

def scan_tail(step, grad, read, rate):
    rows, length, chans = step.shape
    states = rate.shape[0]
    tb = min(TB, length)
    n = length // tb
    big = pl.BlockSpec((rows, tb, chans), lambda i: (0, n - 1 - i, 0))
    thin = pl.BlockSpec((rows, states, tb), lambda i: (0, 0, n - 1 - i))
    return pl.pallas_call(tail_kernel, grid=(n,),
        in_specs=[big, big, thin, pl.BlockSpec((states, chans), lambda i: (0, 0))],
        out_specs=pl.BlockSpec((rows, states, chans), lambda i: (0, 0, 0)),
        out_shape=jax.ShapeDtypeStruct((rows, states, chans), f32),
        cost_estimate=cost(12), compiler_params=params())(step, grad, read, rate)

def back_kernel(step_ref, push_ref, grad_ref, write_ref, read_ref, rate_ref, start_ref, later_ref,
                decay_ref, weight_ref, gwrite_ref, gread_ref, grate_ref,
                carry_ref, factor_sc, kept_sc, decay_sc, weight_sc, gwrite_sc, gread_sc):
    rows, tb = step_ref.shape[0], step_ref.shape[1]
    states = rate_ref.shape[0]
    @pl.when(pl.program_id(0) == 0)
    def _():
        carry_ref[...] = later_ref[...]
        grate_ref[...] = jnp.zeros_like(grate_ref)
    for b in range(rows):
        def redo(j, held):
            base = pl.multiple_of(j * UNROLL, UNROLL)
            steps = step_ref[b, pl.ds(base, UNROLL), :]
            pushes = push_ref[b, pl.ds(base, UNROLL), :]
            writes = turned(write_ref, b, base, tb)
            for k in range(UNROLL):
                factor = jnp.exp2(steps[k:k+1] * rate_ref[...])
                kept = factor * held
                factor_sc[base + k] = factor
                kept_sc[base + k] = kept
                held = kept + writes[:, k:k+1] * pushes[k:k+1]
            return held
        lax.fori_loop(0, tb // UNROLL, redo, start_ref[b, 0])
        def group(j, carried):
            carry, total = carried
            base = pl.multiple_of(tb - UNROLL_BACK - j * UNROLL_BACK, UNROLL_BACK)
            steps = step_ref[b, pl.ds(base, UNROLL_BACK), :]
            pushes = push_ref[b, pl.ds(base, UNROLL_BACK), :]
            grads = grad_ref[b, pl.ds(base, UNROLL_BACK), :]
            writes = turned(write_ref, b, base, tb)
            reads = turned(read_ref, b, base, tb)
            for k in range(UNROLL_BACK - 1, -1, -1):
                kept = kept_sc[base + k]
                adjoint = reads[:, k:k+1] * grads[k:k+1] + carry
                carry = factor_sc[base + k] * adjoint
                weighted = adjoint * kept
                total = total + weighted * steps[k:k+1]
                eight = pl.ds(pl.multiple_of((base + k) * 8, 8), 8)
                decay_sc[eight, :] = folded(weighted * rate_ref[...])
                weight_sc[eight, :] = folded(adjoint * writes[:, k:k+1])
                wide = pl.ds(pl.multiple_of((base + k) * states, states), states)
                gwrite_sc[wide, :] = across(adjoint * pushes[k:k+1])
                gread_sc[wide, :] = across(kept * grads[k:k+1])
            return (carry, total)
        carry, total = lax.fori_loop(0, tb // UNROLL_BACK, group, (carry_ref[b], grate_ref[...]))
        grate_ref[...] = total
        carry_ref[b] = carry
        pick = picker(tb)
        decay_ref[b] = mat(pick, decay_sc[...].astype(jnp.bfloat16), ((1,), (0,)))
        weight_ref[b] = mat(pick, weight_sc[...].astype(jnp.bfloat16), ((1,), (0,)))
        ones = jnp.ones((8, 128), jnp.bfloat16)
        gwrite_ref[b] = mat(ones, gwrite_sc[...].astype(jnp.bfloat16), ((1,), (1,)))[:1]
        gread_ref[b] = mat(ones, gread_sc[...].astype(jnp.bfloat16), ((1,), (1,)))[:1]

def scan_back(step, push, grad, write, read, rate, starts, later):
    rows, length, chans = step.shape
    states = rate.shape[0]
    tb = min(TB, length)
    n = length // tb
    big = pl.BlockSpec((rows, tb, chans), lambda i: (0, n - 1 - i, 0))
    thin = pl.BlockSpec((rows, states, tb), lambda i: (0, 0, n - 1 - i))
    line = pl.BlockSpec((rows, 1, tb * states), lambda i: (0, 0, n - 1 - i))
    whole = pl.BlockSpec((rows, states, chans), lambda i: (0, 0, 0))
    flat = pl.BlockSpec((states, chans), lambda i: (0, 0))
    return pl.pallas_call(back_kernel, grid=(n,),
        in_specs=[big, big, big, thin, thin, flat, pl.BlockSpec((rows, 1, states, chans), lambda i: (0, n - 1 - i, 0, 0)), whole],
        out_specs=[big, big, line, line, flat],
        out_shape=[jax.ShapeDtypeStruct((rows, length, chans), f32)] * 2
                 + [jax.ShapeDtypeStruct((rows, 1, length * states), f32)] * 2
                 + [jax.ShapeDtypeStruct((states, chans), f32)],
        scratch_shapes=[pltpu.VMEM((rows, states, chans), f32),
                        pltpu.VMEM((tb, states, chans), f32),
                        pltpu.VMEM((tb, states, chans), f32),
                        pltpu.VMEM((tb * 8, chans), f32),
                        pltpu.VMEM((tb * 8, chans), f32),
                        pltpu.VMEM((tb * states, 128), f32),
                        pltpu.VMEM((tb * states, 128), f32)],
        cost_estimate=cost(46), compiler_params=params())(step, push, grad, write, read, rate, starts, later)


def mixer_forward(normed, weights, same, flags):
    (
        mixer_in,
        conv_taps,
        conv_bias,
        state_proj,
        step_proj,
        step_bias,
        decay_log,
        skip_gain,
        mixer_out,
    ) = weights
    both = jnp.einsum("rtd,dce->rtce", normed, mixer_in, preferred_element_type=jnp.float32)
    signal = both[:, :, 0].astype(jnp.bfloat16)
    gate = both[:, :, 1]
    taps = conv_taps.shape[0]
    length = signal.shape[1]
    rows = signal.shape[0]
    tail = from_behind(signal[:, length - (taps - 1) :], "seq", 1)
    widened = jnp.concatenate([tail, signal], axis=1).astype(jnp.float32)
    conv_sum = conv_bias + jnp.zeros_like(gate)
    for tap in range(taps):
        conv_sum = (
            conv_sum + conv_taps[tap] * widened[:, tap : tap + length] * same[:, :, tap : tap + 1]
        )
    inner = jax.nn.silu(conv_sum).astype(jnp.bfloat16)
    source = inner.astype(jnp.float32)
    mixed = channel_total(
        jnp.einsum("rte,ec->rtc", inner, state_proj, preferred_element_type=jnp.float32)
    )
    rank = step_proj.shape[0]
    states = decay_log.shape[0]
    step_low = mixed[:, :, :rank]
    write_in = mixed[:, :, rank : rank + states].astype(jnp.float32)
    read_out = mixed[:, :, rank + states :].astype(jnp.float32)
    step_raw = (
        jnp.einsum("rtk,ke->rte", step_low, step_proj, preferred_element_type=jnp.float32)
        + step_bias
    )
    step = jax.nn.softplus(step_raw)
    rate = -jnp.exp(decay_log)
    step_far = jnp.where(flags[:, :, None] > 0, FAR, step)
    push = step * source
    write_cols = jnp.swapaxes(write_in, 1, 2)
    read_cols = jnp.swapaxes(read_out, 1, 2)
    ends = scan_ends(step_far, push, write_cols, rate * LOG2E)
    span = jnp.where(jnp.max(flags, axis=1)[:, None] > 0, FAR, jnp.sum(step, axis=1))
    incoming = carried_in(ends, span, rate, "seq", False)
    scanned, firsts = scan_outputs(
        step_far, push, write_cols, read_cols, rate * LOG2E, incoming
    )
    result = scanned + skip_gain * source
    gated = (result * jax.nn.silu(gate)).astype(jnp.bfloat16)
    partial_value = jnp.einsum("rte,ed->rtd", gated, mixer_out, preferred_element_type=jnp.float32)
    cache = (
        normed,
        widened,
        gate,
        conv_sum,
        inner,
        source,
        step_low,
        step_raw,
        step,
        step_far,
        push,
        write_in,
        write_cols,
        read_cols,
        result,
        gated,
        firsts,
        span,
    )
    return (partial_value, cache)


def mixer_backward(grad_branch, cache, weights, same, flags, first):
    (
        mixer_in,
        conv_taps,
        conv_bias,
        state_proj,
        step_proj,
        step_bias,
        decay_log,
        skip_gain,
        mixer_out,
    ) = weights
    (
        normed,
        widened,
        gate,
        conv_sum,
        inner,
        source,
        step_low,
        step_raw,
        step,
        step_far,
        push,
        write_in,
        write_cols,
        read_cols,
        result,
        gated,
        firsts,
        span,
    ) = cache
    grad_gated = jnp.einsum(
        "rtd,ed->rte", grad_branch, mixer_out, preferred_element_type=jnp.float32
    )
    grad_mixer_out = jnp.einsum(
        "rtd,rte->de", grad_branch, gated, preferred_element_type=jnp.float32
    )
    first_out = plane_first(grad_mixer_out)
    grad_gated = after(grad_gated, first)
    grad_result = grad_gated * jax.nn.silu(gate)
    grad_gate = grad_gated * result * silu_slope(gate)
    grad_skip = jnp.sum(grad_result * source, axis=(0, 1))
    rate = -jnp.exp(decay_log)
    early = after(rate * LOG2E, first_out[0])
    tail = scan_tail(step_far, grad_result, read_cols, early)
    second_out = plane_second(*first_out)
    first = [plane_third(held, tail) for held in first]
    later = carried_in(tail, span, rate, "seq", True)
    early = after(rate * LOG2E, second_out)
    decays, weights_back, write_back, read_back, grad_rate = scan_back(
        step_far, push, grad_result, write_cols, read_cols, early, firsts, later
    )
    grad_mixer_out = plane_third(second_out, grad_rate)
    grad_step = decays * (1.0 / LOG2E) + weights_back * source
    grad_source = weights_back * step
    grad_write = write_back.reshape(write_in.shape)
    grad_read = read_back.reshape(write_in.shape) + write_in * jnp.sum(
        push * grad_result, axis=2, keepdims=True
    )
    grad_source = grad_source + skip_gain * grad_result
    grad_step_raw = (grad_step * jax.nn.sigmoid(step_raw)).astype(jnp.bfloat16)
    grad_step_bias = jnp.sum(grad_step_raw.astype(jnp.float32), axis=(0, 1))
    grad_step_proj = jnp.einsum(
        "rtk,rte->ke", step_low, grad_step_raw, preferred_element_type=jnp.float32
    )
    grad_low = jnp.einsum(
        "rte,ke->rtk", grad_step_raw, step_proj, preferred_element_type=jnp.float32
    )
    grad_mixed = channel_total(
        jnp.concatenate([after(grad_low, first), grad_write, grad_read], axis=-1)
    )
    grad_state_proj = jnp.einsum(
        "rte,rtc->ce", inner, grad_mixed, preferred_element_type=jnp.float32
    )
    grad_source = grad_source + jnp.einsum(
        "rtc,ec->rte", grad_mixed, state_proj, preferred_element_type=jnp.float32
    )
    grad_conv = grad_source * silu_slope(conv_sum)
    length = grad_conv.shape[1]
    taps = conv_taps.shape[0]
    reach = taps - 1
    terms = [grad_conv * same[:, :, tap : tap + 1] for tap in range(taps)]
    grad_taps = [
        jnp.sum(widened[:, tap : tap + length] * terms[tap], axis=(0, 1)) for tap in range(taps)
    ]
    grad_conv_bias = jnp.sum(grad_conv, axis=(0, 1))
    heads = [conv_taps[tap] * terms[tap][:, :reach] for tap in range(taps)]
    head = sum(
        jnp.pad(heads[tap][:, : reach - tap], ((0, 0), (tap, 0), (0, 0))) for tap in range(reach)
    )
    returned = from_behind(head, "seq", -1)
    grad_signal = jnp.pad(returned, ((0, 0), (length - reach, 0), (0, 0)))
    for tap in range(taps):
        shift = reach - tap
        grad_signal = grad_signal + conv_taps[tap] * jnp.pad(
            terms[tap][:, shift:], ((0, 0), (0, shift), (0, 0))
        )
    grad_both = jnp.stack([grad_signal, grad_gate], axis=2).astype(jnp.bfloat16)
    grad_mixer_in = jnp.einsum(
        "rtd,rtce->dce", normed, grad_both, preferred_element_type=jnp.float32
    )
    grad_normed = jnp.einsum(
        "rtce,dce->rtd", grad_both, mixer_in, preferred_element_type=jnp.float32
    )
    small = (
        jnp.stack(grad_taps),
        grad_conv_bias[None],
        grad_state_proj,
        grad_step_proj,
        grad_step_bias[None],
        grad_rate * rate,
        grad_skip[None],
    )
    return (grad_normed, grad_mixer_in, grad_mixer_out, small, first)


def dense_forward(normed, dense_in, dense_out):
    both = jnp.einsum("rtd,dcf->rtcf", normed, dense_in, preferred_element_type=jnp.float32)
    gate = both[:, :, 0]
    upper = both[:, :, 1]
    hidden = (jax.nn.silu(gate) * upper).astype(jnp.bfloat16)
    partial_value = jnp.einsum("rtf,fd->rtd", hidden, dense_out, preferred_element_type=jnp.float32)
    return (partial_value, (normed, gate, upper, hidden))


def dense_backward(grad_branch, cache, dense_in, dense_out, event=()):
    normed, gate, upper, hidden = cache
    grad_hidden = jnp.einsum(
        "rtd,fd->rtf", grad_branch, dense_out, preferred_element_type=jnp.float32
    )
    grad_hidden = after(grad_hidden, event)
    grad_gate = grad_hidden * upper * silu_slope(gate)
    grad_upper = grad_hidden * jax.nn.silu(gate)
    grad_both = jnp.stack([grad_gate, grad_upper], axis=2).astype(jnp.bfloat16)
    grad_normed = jnp.einsum(
        "rtcf,dcf->rtd", grad_both, dense_in, preferred_element_type=jnp.float32
    )
    grad_dense_out = jnp.einsum(
        "rtd,rtf->df", grad_branch, hidden, preferred_element_type=jnp.float32
    )
    grad_dense_in = jnp.einsum(
        "rtd,rtcf->dcf", normed, grad_both, preferred_element_type=jnp.float32
    )
    return (grad_normed, [plane_first(grad_dense_in), plane_first(grad_dense_out)])


def plan_of(length):
    block = min(QBLOCK, length)
    return (block, (WINDOW + block) // block)


def lower_edge(info_ref, row, first, block):
    lane = lax.broadcasted_iota(jnp.int32, (1, block), 1)
    place = info_ref[row, 0] + first + lane
    start = jnp.zeros((1, block), jnp.int32)
    for index in range(1, info_ref.shape[1]):
        entry = info_ref[row, index]
        start = jnp.maximum(start, jnp.where(entry <= place, entry, 0))
    return (jnp.maximum(lane + 1, start - (info_ref[row, 0] + first - WINDOW)), lane)


def piece_mask(low, lane, piece, block, pieces):
    index = piece * block + lax.broadcasted_iota(jnp.int32, (block, block), 0)
    allowed = index >= low
    if piece == pieces - 1:
        allowed = allowed & (index <= lane + WINDOW)
    return allowed


NT = (((1,), (1,)), ((), ()))
TN = (((0,), (0,)), ((), ()))
NN = (((1,), (0,)), ((), ()))


def dot(left, right, dims):
    return lax.dot_general(left, right, dims, preferred_element_type=f32)


def attend_kernel(heads, pieces, skip, info_ref, query_ref, key_ref, value_ref, out_ref, total_ref, held):
    block = query_ref.shape[1]
    first = pl.multiple_of(pl.program_id(1) * block, block)
    low, lane = lower_edge(info_ref, pl.program_id(0) // heads, first, block)
    query = query_ref[0]
    top = jnp.full((1, block), masked_score, f32)
    for piece in range(pieces):
        at = pl.ds(pl.multiple_of(first + skip + piece * block, block), block)
        scores = dot(key_ref[0, at, :], query, NT)
        scores = jnp.where(piece_mask(low, lane, piece, block, pieces), scores, masked_score)
        held[piece] = scores
        top = jnp.maximum(top, jnp.max(scores, axis=0, keepdims=True))
    slope = HDIM ** (-0.5) * LOG2E
    total = jnp.zeros((1, block), f32)
    summed = jnp.zeros((HDIM, block), f32)
    for piece in range(pieces):
        at = pl.ds(pl.multiple_of(first + skip + piece * block, block), block)
        soft = jnp.exp2((held[piece] - top) * slope)
        total = total + jnp.sum(soft, axis=0, keepdims=True)
        summed = summed + dot(value_ref[0, at, :], soft.astype(jnp.bfloat16), TN)
    out_ref[0] = (summed / total).T.astype(jnp.bfloat16)
    total_ref[0] = top * slope + jnp.log2(total)


def attend(info, query, wide, head):
    rows, length, reach = (query.shape[0], query.shape[1], wide.shape[1])
    block, pieces = plan_of(length)
    skip = reach - length - WINDOW
    body = lambda *refs: attend_kernel(1, pieces, skip, *refs)
    return pl.pallas_call(
        body,
        grid=(rows, length // block),
        in_specs=[
            pl.BlockSpec(memory_space=pltpu.SMEM),
            pl.BlockSpec((1, block, HDIM), lambda i, j: (i, j, head)),
            pl.BlockSpec((1, reach, HDIM), lambda i, j: (i, 0, 0)),
            pl.BlockSpec((1, reach, HDIM), lambda i, j: (i, 0, 1)),
        ],
        out_specs=[
            pl.BlockSpec((1, block, HDIM), lambda i, j: (i, j, 0)),
            pl.BlockSpec((1, 1, block), lambda i, j: (i, 0, j)),
        ],
        out_shape=[
            jax.ShapeDtypeStruct((rows, length, HDIM), jnp.bfloat16),
            jax.ShapeDtypeStruct((rows, 1, length), f32),
        ],
        scratch_shapes=[pltpu.VMEM((pieces, block, block), f32)],
        cost_estimate=cost(7),
        compiler_params=pltpu.CompilerParams(vmem_limit_bytes=VM),
    )(info, query, wide, wide)


def attend_back_kernel(
    heads, pieces, skip, info_ref, query_ref, grad_ref, key_ref, value_ref, total_ref, delta_ref,
    gquery_ref, gkey_ref, gvalue_ref,
):
    block = query_ref.shape[1]
    first = pl.multiple_of(pl.program_id(1) * block, block)
    low, lane = lower_edge(info_ref, pl.program_id(0) // heads, first, block)

    @pl.when(pl.program_id(1) == 0)
    def _():
        gkey_ref[...] = jnp.zeros_like(gkey_ref)
        gvalue_ref[...] = jnp.zeros_like(gvalue_ref)

    query, grad = (query_ref[0], grad_ref[0])
    total, delta = (total_ref[0], delta_ref[0])
    slope = HDIM ** (-0.5) * LOG2E
    summed = jnp.zeros((HDIM, block), f32)
    for piece in range(pieces):
        at = pl.ds(pl.multiple_of(first + skip + piece * block, block), block)
        keys = key_ref[0, at, :]
        scores = dot(keys, query, NT)
        allowed = piece_mask(low, lane, piece, block, pieces)
        soft = jnp.exp2(jnp.where(allowed, scores * slope - total, masked_score))
        gvalue_ref[0, at, :] += dot(soft.astype(jnp.bfloat16), grad, NN)
        spread = soft * (dot(value_ref[0, at, :], grad, NT) - delta)
        spread = spread.astype(jnp.bfloat16)
        gkey_ref[0, at, :] += dot(spread, query, NN)
        summed = summed + dot(keys, spread, TN)
    gquery_ref[0] = (summed * HDIM ** (-0.5)).T


def attend_back(info, query, grad, wide, total, delta, head):
    rows, length, reach = (query.shape[0], query.shape[1], wide.shape[1])
    block, pieces = plan_of(length)
    skip = reach - length - WINDOW
    body = lambda *refs: attend_back_kernel(1, pieces, skip, *refs)
    narrow = pl.BlockSpec((1, block, HDIM), lambda i, j: (i, j, head))
    line = pl.BlockSpec((1, 1, block), lambda i, j: (i, 0, j))
    tall = pl.BlockSpec((1, reach, HDIM), lambda i, j: (i, 0, 0))
    return pl.pallas_call(
        body,
        grid=(rows, length // block),
        in_specs=[
            pl.BlockSpec(memory_space=pltpu.SMEM),
            narrow,
            narrow,
            tall,
            pl.BlockSpec((1, reach, HDIM), lambda i, j: (i, 0, 1)),
            line,
            line,
        ],
        out_specs=[pl.BlockSpec((1, block, HDIM), lambda i, j: (i, j, 0)), tall, tall],
        out_shape=[
            jax.ShapeDtypeStruct((rows, length, HDIM), f32),
            jax.ShapeDtypeStruct((rows, reach, HDIM), f32),
            jax.ShapeDtypeStruct((rows, reach, HDIM), f32),
        ],
        cost_estimate=cost(12),
        compiler_params=pltpu.CompilerParams(vmem_limit_bytes=VM),
    )(info, query, grad, wide, wide, total, delta)


def by_head(attend_in):
    features, heads = (attend_in.shape[0], attend_in.shape[2] // HDIM)
    split = attend_in.reshape(features, 3, heads, HDIM)
    pairs = jnp.swapaxes(split[:, 1:], 1, 2).reshape(features, 2 * heads * HDIM)
    return (attend_in[:, 0], pairs)


def attention_forward(normed, attend_in, attend_out, info):
    heads = attend_in.shape[2] // HDIM
    weight_query, weight_pairs = by_head(attend_in)
    pairs = jnp.einsum(
        "rtd,dh->rth", normed, weight_pairs, preferred_element_type=jnp.float32
    ).astype(jnp.bfloat16)
    query = jnp.einsum(
        "rtd,dh->rth", normed, weight_query, preferred_element_type=jnp.float32
    ).astype(jnp.bfloat16)
    odd = lax.axis_index("seq") % 2 == 1
    wides, results = ([], [])
    for head in range(heads):
        own = pairs[:, :, 2 * head * HDIM : 2 * (head + 1) * HDIM]
        seconds = from_behind(own, "seq", 2)
        firsts = partner(jnp.where(odd, seconds, own), "seq", 1)
        wides.append(jnp.concatenate([seconds, firsts, own], axis=1))
        results.append(attend(info, query, wides[head], head))
    attended = jnp.concatenate([result[0] for result in results], axis=2)
    totals = [result[1] for result in results]
    partial_value = jnp.einsum(
        "rth,hd->rtd", attended, attend_out, preferred_element_type=jnp.float32
    )
    return (partial_value, (normed, query, wides, attended, totals, weight_query, weight_pairs))


def attention_backward(grad_branch, cache, attend_in, attend_out, info, event):
    normed, query, wides, attended, totals, weight_query, weight_pairs = cache
    rows, length = (query.shape[0], query.shape[1])
    heads = query.shape[2] // HDIM
    grad_attended = jnp.einsum(
        "rtd,hd->rth", grad_branch, attend_out, preferred_element_type=jnp.float32
    )
    grad_attended = after(grad_attended, event).astype(jnp.bfloat16)
    grad_attend_out = jnp.einsum(
        "rtd,rth->dh", grad_branch, attended, preferred_element_type=jnp.float32
    )
    both = grad_attended.astype(jnp.float32) * attended.astype(jnp.float32)
    delta = jnp.sum(both.reshape(rows, length, heads, HDIM), axis=-1)
    odd = lax.axis_index("seq") % 2 == 1
    queries, pairs, marks = ([], [], [[], []])
    for head in range(heads):
        grad_query, grad_keys, grad_values = attend_back(
            after(info, marks[head]),
            query,
            grad_attended,
            wides[head],
            totals[head],
            delta[:, :, head].reshape(rows, 1, length),
            head,
        )
        queries.append(grad_query)
        scaled = jnp.concatenate([grad_keys * HDIM ** (-0.5), grad_values], axis=2)
        seconds, firsts, own = (scaled[:, i * length : (i + 1) * length] for i in range(3))
        given = partner(firsts.astype(jnp.bfloat16), "seq", 1).astype(jnp.float32)
        sent = (seconds + jnp.where(odd, given, 0.0)).astype(jnp.bfloat16)
        marks.append(sent)
        back = from_behind(sent, "seq", -2)
        pairs.append(own + jnp.where(odd, 0.0, given) + back.astype(jnp.float32))
    grad_projected = jnp.concatenate(queries + pairs, axis=2).astype(jnp.bfloat16)
    grad_weight = jnp.einsum(
        "rtd,rth->dh", normed, grad_projected, preferred_element_type=jnp.float32
    )
    flat = jnp.concatenate([weight_query, weight_pairs], axis=1)
    grad_normed = jnp.einsum(
        "rth,dh->rtd", grad_projected, flat, preferred_element_type=jnp.float32
    )
    return (grad_normed, [plane_first(grad_weight), plane_first(grad_attend_out)])


def in_order(grad_weight, heads):
    features = grad_weight.shape[0]
    query = grad_weight[:, : heads * HDIM].reshape(features, 1, heads, HDIM)
    pairs = grad_weight[:, heads * HDIM :].reshape(features, heads, 2, HDIM)
    both = jnp.concatenate([query, jnp.swapaxes(pairs, 1, 2)], axis=1)
    return both.reshape(features, 3, heads * HDIM)


def shards(
    block_in,
    block_grad,
    norm_gains,
    mixer_in,
    conv_taps,
    conv_bias,
    state_proj,
    step_proj,
    step_bias,
    decay_log,
    skip_gain,
    mixer_out,
    first_in,
    first_out,
    attend_in,
    attend_out,
    second_in,
    second_out,
    row_counts,
    doc_starts,
    row_mask,
):
    local_len = block_in.shape[1]
    length = local_len * lax.axis_size("tp")
    anchor = lax.axis_index("seq") * length
    positions = anchor + jnp.arange(length, dtype=jnp.int32)
    own_place = anchor + lax.axis_index("tp") * local_len + jnp.arange(local_len, dtype=jnp.int32)
    valid = ((own_place[None, :] < row_counts[:, None]) & (row_mask[:, None] == 1)).astype(
        jnp.float32
    )[:, :, None]
    documents = doc_numbers(positions, doc_starts)
    flags = jnp.any(doc_starts[:, None, :] == positions[None, :, None], axis=-1).astype(jnp.float32)
    taps = conv_taps.shape[0]
    same = jnp.stack(
        [
            (
                (positions - (taps - 1 - tap) >= 0)[None, :]
                & (doc_numbers(positions - (taps - 1 - tap), doc_starts) == documents)
            ).astype(jnp.float32)
            for tap in range(taps)
        ],
        axis=-1,
    )
    here = jnp.broadcast_to(anchor, (doc_starts.shape[0], 1)).astype(jnp.int32)
    info = jnp.concatenate([here, doc_starts], axis=1)
    mixer_weights = (
        mixer_in,
        conv_taps,
        conv_bias,
        state_proj,
        step_proj,
        step_bias,
        decay_log,
        skip_gain,
        mixer_out,
    )
    normed_mix, scale_mix = norm_forward(block_in, norm_gains[0])
    partial_value, cache_mix = mixer_forward(
        gather_rows(normed_mix.astype(jnp.bfloat16)), mixer_weights, same, flags
    )
    stream_mix = block_in + reduce_rows(partial_value)
    normed_first, scale_first = norm_forward(stream_mix, norm_gains[1])
    partial_value, cache_first = dense_forward(
        gather_rows(normed_first.astype(jnp.bfloat16)), first_in, first_out
    )
    stream_first = stream_mix + reduce_rows(partial_value)
    grad_stream = block_grad * valid
    grad_second = gather_rows(grad_stream.astype(jnp.bfloat16))
    normed_attend, scale_attend = norm_forward(stream_first, norm_gains[2])
    partial_value, cache_attend = attention_forward(
        gather_rows(normed_attend.astype(jnp.bfloat16)), attend_in, attend_out, info
    )
    stream_attend = stream_first + reduce_rows(partial_value, grad_second)
    normed_second, scale_second = norm_forward(stream_attend, norm_gains[3])
    partial_out, cache_second = dense_forward(
        gather_rows(normed_second.astype(jnp.bfloat16)), second_in, second_out
    )
    partial_out = partial_out.astype(jnp.bfloat16)

    def gain_of(which, low, cache):
        return gain_share(low, cache[0], norm_gains[which])

    grad_normed, firsts = dense_backward(grad_second, cache_second, second_in, second_out)
    low = grad_normed.astype(jnp.bfloat16)
    gain_four = gain_of(3, low, cache_second)
    grad_back = norm_backward(
        stream_attend,
        scale_second,
        after(norm_gains[3], firsts[0][0], firsts[1][0], gain_four, partial_out),
        reduce_rows(low),
    )
    grad_stream = grad_stream + grad_back
    second = [plane_second(*pair) for pair in firsts]
    gathered = gather_rows(grad_stream.astype(jnp.bfloat16))
    stream_out = stream_attend + reduce_rows(partial_out, gathered)
    block_out = stream_out * valid
    grad_normed, firsts = attention_backward(
        gathered, cache_attend, attend_in, attend_out, info, second
    )
    low = grad_normed.astype(jnp.bfloat16)
    gain_three = gain_of(2, low, cache_attend)
    second = [plane_third(held, grad_normed) for held in second]
    grad_back = norm_backward(
        stream_first,
        scale_attend,
        after(norm_gains[2], firsts[0][0], firsts[1][0], second, gain_three),
        reduce_rows(low),
    )
    grad_stream = grad_stream + grad_back
    middle = [plane_second(*pair) for pair in firsts]
    grad_normed, firsts = dense_backward(
        gather_rows(grad_stream.astype(jnp.bfloat16)), cache_first, first_in, first_out, middle
    )
    middle = [plane_third(held) for held in middle]
    low = grad_normed.astype(jnp.bfloat16)
    gain_two = gain_of(1, low, cache_first)
    grad_back = norm_backward(
        stream_mix,
        scale_first,
        after(norm_gains[1], firsts[0][0], firsts[1][0], middle, gain_two),
        reduce_rows(low),
    )
    grad_stream = grad_stream + grad_back
    firsts = [plane_second(*pair) for pair in firsts]
    grad_normed, grad_mixer_in, grad_mixer_out, small, first = mixer_backward(
        gather_rows(grad_stream.astype(jnp.bfloat16)),
        cache_mix,
        mixer_weights,
        same,
        flags,
        firsts,
    )
    low = grad_normed.astype(jnp.bfloat16)
    gains = jnp.stack([gain_of(0, low, cache_mix), gain_two, gain_three, gain_four])
    grad_mixer_in = plane_third(plane_second(*plane_first(grad_mixer_in)))
    grad_normed = reduce_rows(low)
    wide = small[0].shape[1]
    small = small + (gains.reshape(-1, wide),)
    counts = [member.shape[0] for member in small]
    packed = spread_sum(jnp.concatenate(small), ("seq", "row"), jnp.bfloat16)
    small, place = ([], 0)
    for count in counts:
        small.append(packed[place : place + count])
        place += count
    gains = jnp.sum(lax.all_gather(small.pop(), "tp"), axis=0).reshape(gains.shape)
    grad_back = norm_backward(
        block_in, scale_mix, norm_gains[0], grad_normed
    )
    grad_stream = grad_stream + grad_back
    middle[0] = in_order(middle[0], attend_in.shape[2] // HDIM)
    pairs = ((grad_mixer_in, grad_mixer_out), first, middle, second)
    flat = [member for pair in pairs for member in (pair[0], pair[1].T)]
    return (
        block_out,
        grad_stream,
        gains,
        flat[0],
        small[0],
        small[1][0],
        small[2].T,
        small[3],
        small[4][0],
        small[5],
        small[6][0],
        flat[1],
        flat[2],
        flat[3],
        flat[4],
        flat[5],
        flat[6],
        flat[7],
    )


def solution(mesh):
    in_specs = (
        P("row", ("seq", "tp"), None),
        P("row", ("seq", "tp"), None),
        P(),
        P(None, None, "tp"),
        P(None, "tp"),
        P("tp"),
        P("tp", None),
        P(None, "tp"),
        P("tp"),
        P(None, "tp"),
        P("tp"),
        P("tp", None),
        P(None, None, "tp"),
        P("tp", None),
        P(None, None, "tp"),
        P("tp", None),
        P(None, None, "tp"),
        P("tp", None),
        P("row"),
        P("row", None),
        P("row"),
    )
    out_specs = (
        P("row", ("seq", "tp"), None),
        P("row", ("seq", "tp"), None),
        P(),
        P(("row", "seq"), None, "tp"),
        P(None, "tp"),
        P("tp"),
        P("tp", None),
        P(None, "tp"),
        P("tp"),
        P(None, "tp"),
        P("tp"),
        P("tp", ("row", "seq")),
        P(("row", "seq"), None, "tp"),
        P("tp", ("row", "seq")),
        P(("row", "seq"), None, "tp"),
        P("tp", ("row", "seq")),
        P(("row", "seq"), None, "tp"),
        P("tp", ("row", "seq")),
    )
    return jax.shard_map(shards, mesh=mesh, in_specs=in_specs, out_specs=out_specs, check_vma=False)
```

time: 1990 us -> 1550 us (0.78)
  waiting for transfers between devices: 1110 us -> 732 us
  matrix products: 299 us -> 196 us
  local copies, waits for them, and re-layouts: 104 us -> 168 us
  blocking collectives: 112 us -> 68.1 us
  starting transfers between devices: 22.4 us -> 50.3 us
  between operations: 17.9 us -> 41 us
  Pallas kernels: 168 us -> 145 us
    reduce_scatter x8, waiting for transfers between devices: 477 us -> 207 us  [reduce_rows(): lax.psum_scatter(low, 'tp', scatter_dimension=1, tiled=True)]
    ppermute x0 -> x33, waiting for transfers between devices: none -> 127 us  [partner(): lax.ppermute(x, axis, [(i, i ^ flip) for i in range(lax.axis_size(axis))])]
    reduce_scatter x8 -> x0, waiting for transfers between devices: 118 us -> none  [the longest x1 63.1 us: shards(): lax.psum_scatter(flat[2].astype(jnp.bfloat16), ('row', 'seq'), scatter_di...]
    psum x3 -> x0, blocking collectives: 93.8 us -> none  [the longest x1 41 us: shards(): lax.psum(jnp.stack([gain_one, gain_two, gain_three, gain_four]), ('row',...]
    dot_general x20 -> x9, matrix products: 136 us -> 43.5 us  [the longest x2 15.5 us: dense_backward(): jnp.einsum('rtd,rtf->df', grad_branch, hidden, preferred_element_type=jnp...]
    all_gather x8, waiting for transfers between devices: 426 us -> 345 us  [gather_rows(): return lax.all_gather(local, 'tp', axis=1, tiled=True)]
    psum x2 -> x0, waiting for transfers between devices: 62.9 us -> none  [the longest x1 35.6 us: channel_total(): return lax.psum(partial_value, 'tp')]
    pallas_call x0 -> x6, Pallas kernels: none -> 56.1 us  [the longest x3 36.3 us: attend_back(): pl.pallas_call(body, grid=(rows, length // block), in_specs=[pl.BlockSpec...]
  transfers between devices with their start and end apart: 36 -> 58, of which waited for: 26 -> 28; matrix products, arithmetic and copies ran while one was open for 14% -> 19% of each run, Pallas kernels for 6% -> 6%
where the time goes in v2:
time: 1550 us; the launch traced here: 1540 us
  waiting for transfers between devices  732 us (47%)
  matrix products  196 us (13%)
  local copies, waits for them, and re-layouts  168 us (11%)
  Pallas kernels  145 us (9%)
  other arithmetic  144 us (9%)
  blocking collectives  68.1 us (4%)
  starting transfers between devices  50.3 us (3%)
  between operations  41 us (3%)
    all_gather x8, waiting for transfers between devices, gather_rows(): return lax.all_gather(local, 'tp', axis=1, tiled=True)  345 us
    reduce_scatter x8, waiting for transfers between devices, reduce_rows(): lax.psum_scatter(low, 'tp', scatter_dimension=1, tiled=True)  207 us
    ppermute x33, waiting for transfers between devices, partner(): lax.ppermute(x, axis, [(i, i ^ flip) for i in range(lax.axis_size(axis))])  127 us
    unnamed x353, local copies, waits for them, and re-layouts  67.1 us
    pallas_call x1, Pallas kernels, scan_back(): pl.pallas_call(back_kernel, grid=(n,), in_specs=[big, big, big, thin, thi...  45.7 us
    ppermute x8, waiting for transfers between devices, from_behind(): return lax.ppermute(x, axis, pairs)  43.8 us
    pallas_call x3, Pallas kernels, attend_back(): pl.pallas_call(body, grid=(rows, length // block), in_specs=[pl.BlockSpec...  36.3 us
  transfers between devices with their start and end apart: 58, of which 28 were waited for; matrix products, arithmetic and copies ran while one was open for 19% of the time, Pallas kernels for 6%

profile of v2, /device:TPU:0, one launch (start us, length us, event | category | flops | bytes accessed | tf_op | source)
XLA Modules:
  0.0 1544.1 jit_solution(9850301236438649154)
XLA Ops:
  12.9 65.9 %all-gather.14.cloned.1.call-done = bf16[1,1024,1536]{2,1,0:T(8,128)(2,1)} async-done(((bf16[1,256,1536]{2,1,0:T(8,128)(2,1)}), bf16[1,1024,1536]{2,1,0:T(8,128)(2,1)}) %all-gather.14.cloned.1.call-update) | async-done | bytes 3145744 | tf_op jit(solution)/shard_map/all_gather | solution.py:41
  78.8 8.3 fusion.94
  110.7 8.4 all-to-all-done
  122.8 15.0 all-gather
  137.8 5.4 convert_multiply_fusion.3
  145.3 11.5 shard_map.340
  156.9 5.9 all-gather.1
  162.9 20.5 %shard_map.341 = (f32[1,1024,768]{2,1,0:T(8,128)S(1)}, f32[1,8,16,768]{3,2,1,0:T(8,128)S(1)}) custom-call(f32[1,1024,768]{2,1,0:T(8,128)} %copy-done.2, f32[1,1024,768]{2,1,0:T(8,128)} %get-tuple-element.230.push_ref, f32[1,16,1024]{2,1,0:T(8,128)S(1)} %get-tuple-element.217.write_ref, f32[1,16,1024]{2,1,0:T(8,128)S(1)} %get-tuple-element.216.read_ref, ...), custom_call_target="tpu_custom_call" | custom-call | flops 20999999488 | bytes 63000000 | tf_op jit(solution)/shard_map/pallas_call | solution.py:236
  193.3 59.7 %reduce-scatter.9.cloned.1.call-done = bf16[1,256,1536]{2,1,0:T(8,128)(2,1)} async-done(((bf16[1,1024,1536]{2,1,0:T(8,128)(2,1)}), bf16[1,256,1536]{2,1,0:T(8,128)(2,1)}) %reduce-scatter.9.cloned.1.call-update) | async-done | bytes 786448 | tf_op jit(solution)/shard_map/reduce_scatter | solution.py:46
  258.7 63.5 %all-gather.16.cloned.1.call-done = bf16[1,1024,1536]{2,1,0:T(8,128)(2,1)} async-done(((bf16[1,256,1536]{2,1,0:T(8,128)(2,1)}), bf16[1,1024,1536]{2,1,0:T(8,128)(2,1)}) %all-gather.16.cloned.1.call-update) | async-done | bytes 3145744 | tf_op jit(solution)/shard_map/all_gather | solution.py:41
  322.2 10.2 fusion.52
  335.7 4.9 fusion.43
  340.7 59.0 %reduce-scatter.11.cloned.1.call-done = bf16[1,256,1536]{2,1,0:T(8,128)(2,1)} async-done(((bf16[1,1024,1536]{2,1,0:T(8,128)(2,1)}), bf16[1,256,1536]{2,1,0:T(8,128)(2,1)}) %reduce-scatter.11.cloned.1.call-update) | async-done | bytes 786448 | tf_op jit(solution)/shard_map/reduce_scatter | solution.py:46
  408.3 6.1 copy.150
  417.9 50.2 %all-gather.18.cloned.1.call-done = bf16[1,1024,1536]{2,1,0:T(8,128)(2,1)} async-done(((bf16[1,256,1536]{2,1,0:T(8,128)(2,1)}), bf16[1,1024,1536]{2,1,0:T(8,128)(2,1)}) %all-gather.18.cloned.1.call-update) | async-done | bytes 3145744 | tf_op jit(solution)/shard_map/all_gather | solution.py:41
  468.1 5.3 fusion.128
  479.5 10.7 collective-permute-done.5
  492.7 5.2 collective-permute-start.3
  500.2 32.0 %all-gather.20.cloned.1.call-done = bf16[1,1024,1536]{2,1,0:T(8,128)(2,1)} async-done(((bf16[1,256,1536]{2,1,0:T(8,128)(2,1)}), bf16[1,1024,1536]{2,1,0:T(8,128)(2,1)}) %all-gather.20.cloned.1.call-update) | async-done | bytes 3145744 | tf_op jit(solution)/shard_map/all_gather | solution.py:41
  541.8 6.6 shard_map.344
  549.8 6.6 shard_map.342
  558.5 6.6 shard_map.343
  570.4 59.1 %reduce-scatter.13.cloned.1.call-done = bf16[1,256,1536]{2,1,0:T(8,128)(2,1)} async-done(((bf16[1,1024,1536]{2,1,0:T(8,128)(2,1)}), bf16[1,256,1536]{2,1,0:T(8,128)(2,1)}) %reduce-scatter.13.cloned.1.call-update) | async-done | bytes 786448 | tf_op jit(solution)/shard_map/reduce_scatter | solution.py:46
  635.6 63.4 %all-gather.22.cloned.1.call-done = bf16[1,1024,1536]{2,1,0:T(8,128)(2,1)} async-done(((bf16[1,256,1536]{2,1,0:T(8,128)(2,1)}), bf16[1,1024,1536]{2,1,0:T(8,128)(2,1)}) %all-gather.22.cloned.1.call-update) | async-done | bytes 3145744 | tf_op jit(solution)/shard_map/all_gather | solution.py:41
  699.0 10.2 fusion.55
  709.2 6.2 fusion.109
  715.4 10.3 multiply_reduce_fusion.3
  726.8 4.7 copy.156
  736.1 9.6 fusion.10
  752.4 7.5 fusion.107
  772.0 12.8 reduce-scatter.15.cloned.1.call-done
  805.3 45.2 %collective-permute-done.10 = bf16[1,2,1,192,1024]{4,3,2,1,0:T(8,128)(2,1)} collective-permute-done((bf16[1,2,1,192,1024]{4,3,2,1,0:T(8,128)(2,1)S(1)}, bf16[1,2,1,192,1024]{4,3,2,1,0:T(8,128)(2,1)}, u32[]{:S(2)}, u32[]{:S(2)}) %collective-permute-start.10) | collective-permute-done | bytes 786464 | tf_op jit(solution)/shard_map/ppermute | solution.py:67
  856.4 5.2 convert_multiply_fusion.7
  866.3 12.2 shard_map.345
  878.8 12.0 shard_map.346
  893.8 12.0 shard_map.347
  912.2 12.1 collective-permute-done.12
  924.5 11.0 collective-permute-done.14
  935.7 10.1 collective-permute-done.16
  980.0 16.6 %collective-permute-done.18 = bf16[1,1,1,192,1024]{4,3,2,1,0:T(8,128)(2,1)S(1)} collective-permute-done((bf16[1,1,1,192,1024]{4,3,2,1,0:T(8,128)(2,1)S(1)}, bf16[1,1,1,192,1024]{4,3,2,1,0:T(8,128)(2,1)S(1)}, u32[]{:S(2)}, u32[]{:S(2)}) %collective-permute-start.18) | collective-permute-done | bytes 393248 | tf_op jit(solution)/shard_map/ppermute | solution.py:67
  1001.5 13.4 reduce-scatter.19.cloned.1.call-done
  1028.8 25.7 %collective-permute-done.22 = bf16[1,2,1,192,384]{4,3,2,1,0:T(8,128)(2,1)S(1)} collective-permute-done((bf16[1,2,1,192,384]{4,3,2,1,0:T(8,128)(2,1)S(1)}, bf16[1,2,1,192,384]{4,3,2,1,0:T(8,128)(2,1)S(1)}, u32[]{:S(2)}, u32[]{:S(2)}) %collective-permute-start.22) | collective-permute-done | bytes 294944 | tf_op jit(solution)/shard_map/ppermute | solution.py:67
  1058.0 25.6 %all-gather.26.cloned.1.call-done = bf16[1,1024,1536]{2,1,0:T(8,128)(2,1)} async-done(((bf16[1,256,1536]{2,1,0:T(8,128)(2,1)}), bf16[1,1024,1536]{2,1,0:T(8,128)(2,1)}) %all-gather.26.cloned.1.call-update) | async-done | bytes 3145744 | tf_op jit(solution)/shard_map/all_gather | solution.py:41
  1083.6 10.1 fusion.110
  1093.7 11.8 multiply_reduce_fusion.1
  1115.4 7.5 collective-permute-done.24
  1127.2 9.6 fusion.8
  1145.7 7.9 fusion.105
  1173.2 5.4 collective-permute-done.27
  1189.6 44.6 %all-gather.28.cloned.1.call-done = bf16[1,1024,1536]{2,1,0:T(8,128)(2,1)} async-done(((bf16[1,256,1536]{2,1,0:T(8,128)(2,1)}), bf16[1,1024,1536]{2,1,0:T(8,128)(2,1)}) %all-gather.28.cloned.1.call-update) | async-done | bytes 3145744 | tf_op jit(solution)/shard_map/all_gather | solution.py:41
  1238.9 5.1 fusion.115
  1260.1 11.5 fusion.62
  1275.9 11.4 shard_map.348
  1290.2 6.3 all-gather.2
  1298.7 45.7 %shard_map.349 = (f32[1,1024,768]{2,1,0:T(8,128)S(1)}, f32[1,1024,768]{2,1,0:T(8,128)}, f32[1,1,16384]{2,1,0:T(1,128)S(1)}, f32[1,1,16384]{2,1,0:T(1,128)S(1)}, f32[16,768]{1,0:T(8,128)S(1)}) custom-call(f32[1,1024,768]{2,1,0:T(8,128)} %copy-done.2, f32[1,1024,768]{2,1,0:T(8,128)} %get-tuple-element.230.push_ref, f32[1,1024,768]{2,1,0:T(8,128)} %bitcast.598, ...), custom_call_target="tpu_custom_call" | custom-call | flops 46000001024 | bytes 138000000 | tf_op jit(solution)/shard_map/pallas_call | solution.py:341
  1372.2 13.2 all_to_all.24
  1390.2 14.4 all-gather.3
  1404.7 10.0 multiply_reduce_fusion.4
  1418.8 4.8 copy.170
  1432.6 6.6 multiply_reduce_fusion
  1441.1 7.1 fusion.63
  1488.2 13.7 collective-permute-done.38
  1504.2 5.4 collective-permute-done.36
  1512.8 13.3 all-gather.4
  (706 shorter events, 385.4 us)
Async XLA Ops:
  7.2 702.0 %copy-start = (bf16[1024,1536]{1,0:T(8,128)(2,1)S(1)}, bf16[1024,1536]{1,0:T(8,128)(2,1)}, u32[]{:S(2)}) copy-start(bf16[1024,1536]{1,0:T(8,128)(2,1)} %param.38) | copy-start | bytes 9437188
  7.2 71.6 %all-gather.14.cloned.1.call-start = ((), (), s32[]{:S(2)}) async-start(), calls=%async_computation.10 | async-start | bytes 3932160 | tf_op jit(solution)/shard_map/all_gather | solution.py:41
  8.3 247.7 %copy-start.105 = (f32[1536]{0:T(1024)}, f32[1536]{0:T(1024)S(1)}, u32[]{:S(2)}) copy-start(f32[1536]{0:T(1024)S(1)} %get-tuple-element.169) | copy-start | bytes 18436
  8.3 393.3 %copy-start.107 = (f32[1536]{0:T(1024)}, f32[1536]{0:T(1024)S(1)}, u32[]{:S(2)}) copy-start(f32[1536]{0:T(1024)S(1)} %get-tuple-element.171) | copy-start | bytes 18436
  12.5 82.6 %copy-start.117 = (f32[1024]{0:T(1024)}, f32[1024]{0:T(1024)S(1)}, u32[]{:S(2)}) copy-start(f32[1024]{0:T(1024)S(1)} %fusion.208) | copy-start | bytes 12292
  12.7 82.4 %copy-start.109 = (f32[768]{0:T(1024)}, f32[768]{0:T(1024)S(1)}, u32[]{:S(2)}) copy-start(f32[768]{0:T(1024)S(1)} %get-tuple-element.172) | copy-start | bytes 9220
  90.4 3.0 collective-permute-start
  107.2 12.0 all-to-all-start
  110.6 142.5 %reduce-scatter.9.cloned.1.call-start = ((), (), s32[]{:S(2)}) async-start(), calls=%async_computation.11 | async-start | bytes 3932160 | tf_op jit(solution)/shard_map/reduce_scatter | solution.py:46
  193.3 128.9 %all-gather.16.cloned.1.call-start = ((), (), s32[]{:S(2)}) async-start(), calls=%async_computation.12 | async-start | bytes 3932160 | tf_op jit(solution)/shard_map/all_gather | solution.py:41
  258.5 141.2 %reduce-scatter.11.cloned.1.call-start = ((), (), s32[]{:S(2)}) async-start(), calls=%async_computation.13 | async-start | bytes 3932160 | tf_op jit(solution)/shard_map/reduce_scatter | solution.py:46
  340.7 127.4 %all-gather.18.cloned.1.call-start = ((), (), s32[]{:S(2)}) async-start(), calls=%async_computation.14 | async-start | bytes 3932160 | tf_op jit(solution)/shard_map/all_gather | solution.py:41
  404.4 127.9 %all-gather.20.cloned.1.call-start = ((), (), s32[]{:S(2)}) async-start(), calls=%async_computation.15 | async-start | bytes 3932160 | tf_op jit(solution)/shard_map/all_gather | solution.py:41
  405.8 381.1 %copy-start.130 = (f32[256]{0:T(256)}, f32[256]{0:T(256)S(1)}, u32[]{:S(2)}) copy-start(f32[256]{0:T(256)S(1)} %and_convert_fusion.3) | copy-start | bytes 3076
  408.2 221.3 %reduce-scatter.13.cloned.1.call-start = ((), (), s32[]{:S(2)}) async-start(), calls=%async_computation.16 | async-start | bytes 3932160 | tf_op jit(solution)/shard_map/reduce_scatter | solution.py:46
  475.3 14.8 collective-permute-start.5
  492.7 45.7 %collective-permute-start.3 = (bf16[1,1024,256]{2,1,0:T(8,128)(2,1)}, bf16[1,1024,256]{2,1,0:T(8,128)(2,1)}, u32[]{:S(2)}, u32[]{:S(2)}) collective-permute-start(bf16[1,1024,256]{2,1,0:T(8,128)(2,1)} %get-tuple-element.206), channel_id=1, source_target_pairs={{0,8},{4,12},{1,9},{5,13},{2,10},{6,14},{3,11},{7,15},{16,24},{20,... | collective-permute-start | bytes 1572872 | tf_op jit(solution)/shard_map/ppermute | solution.py:37
  497.9 40.5 %collective-permute-start.1 = (bf16[1,1024,256]{2,1,0:T(8,128)(2,1)}, bf16[1,1024,256]{2,1,0:T(8,128)(2,1)}, u32[]{:S(2)}, u32[]{:S(2)}) collective-permute-start(bf16[1,1024,256]{2,1,0:T(8,128)(2,1)} %get-tuple-element.207), channel_id=1, source_target_pairs={{0,8},{4,12},{1,9},{5,13},{2,10},{6,14},{3,11},{7,15},{16,24},{20,... | collective-permute-start | bytes 1572872 | tf_op jit(solution)/shard_map/ppermute | solution.py:37
  534.1 6.4 collective-permute-start.6
  538.5 9.9 collective-permute-start.2
  540.4 16.7 %collective-permute-start.4 = (bf16[1,1024,256]{2,1,0:T(8,128)(2,1)S(1)}, bf16[1,1024,256]{2,1,0:T(8,128)(2,1)S(1)}, u32[]{:S(2)}, u32[]{:S(2)}) collective-permute-start(bf16[1,1024,256]{2,1,0:T(8,128)(2,1)S(1)} %get-tuple-element.208), channel_id=1, source_target_pairs={{0,4},{4,0},{8,12},{12,8},{1,5},{5,1},{9,13},{13,9},{2,6},{6,2},{1... | collective-permute-start | bytes 1572872 | tf_op jit(solution)/shard_map/ppermute | solution.py:67
  570.4 128.6 %all-gather.22.cloned.1.call-start = ((), (), s32[]{:S(2)}) async-start(), calls=%async_computation.17 | async-start | bytes 3932160 | tf_op jit(solution)/shard_map/all_gather | solution.py:41
  635.3 149.5 %reduce-scatter.15.cloned.1.call-start = ((), (), s32[]{:S(2)}) async-start(), calls=%async_computation.18 | async-start | bytes 3932160 | tf_op jit(solution)/shard_map/reduce_scatter | solution.py:46
  725.7 130.6 %all-gather.24.cloned.1.call-start = ((), (), s32[]{:S(2)}) async-start(), calls=%async_computation.19 | async-start | bytes 3932160 | tf_op jit(solution)/shard_map/all_gather | solution.py:41
  752.4 38.5 %collective-permute-start.7 = (bf16[2,2,1,192,2,1024]{5,3,4,2,1,0:T(8,128)(2,1)}, bf16[2,2,1,192,2,1024]{5,3,4,2,1,0:T(8,128)(2,1)}, u32[]{:S(2)}, u32[]{:S(2)}) collective-permute-start(bf16[2,2,1,192,2,1024]{5,3,4,2,1,0:T(8,128)(2,1)} %dynamic-slice_convert_fusion.3), channel_id=1, source_target_pairs={{0,4},{4,0},{8,12},{12,8},{1,5},{5,1},{9,13},{13,9},{2,6},{6,2},{1... | collective-permute-start | bytes 9437192 | tf_op jit(solution)/shard_map/ppermute | solution.py:67
  790.5 224.3 %reduce-scatter.19.cloned.1.call-start = ((), (), s32[]{:S(2)}) async-start(), calls=%async_computation.21 | async-start | bytes 3932160 | tf_op jit(solution)/shard_map/reduce_scatter | solution.py:46
  790.8 7.3 collective-permute-start.9
  796.6 55.9 %collective-permute-start.8 = (bf16[1,2,1,192,2,1024]{5,3,4,2,1,0:T(8,128)(2,1)}, bf16[1,2,1,192,2,1024]{5,3,4,2,1,0:T(8,128)(2,1)}, u32[]{:S(2)}, u32[]{:S(2)}) collective-permute-start(bf16[1,2,1,192,2,1024]{5,3,4,2,1,0:T(8,128)(2,1)} %constant_dynamic-slice_fusion.10), channel_id=1, source_target_pairs={{0,16},{16,0},{1,17},{17,1},{2,18},{18,2},{3,19},{19,3},{4,20},{20... | collective-permute-start | bytes 4718600 | tf_op jit(solution)/shard_map/ppermute | solution.py:67
  801.4 49.1 %collective-permute-start.10 = (bf16[1,2,1,192,1024]{4,3,2,1,0:T(8,128)(2,1)S(1)}, bf16[1,2,1,192,1024]{4,3,2,1,0:T(8,128)(2,1)}, u32[]{:S(2)}, u32[]{:S(2)}) collective-permute-start(bf16[1,2,1,192,1024]{4,3,2,1,0:T(8,128)(2,1)S(1)} %constant_dynamic-slice_fusion.9), channel_id=1, source_target_pairs={{0,16},{16,0},{1,17},{17,1},{2,18},{18,2},{3,19},{19,3},{4,20},{20... | collective-permute-start | bytes 2359304 | tf_op jit(solution)/shard_map/ppermute | solution.py:67
  878.8 13.6 collective-permute-start.11
  891.1 17.8 %collective-permute-start.13 = (bf16[1,1024,256]{2,1,0:T(8,128)(2,1)S(1)}, bf16[1,1024,256]{2,1,0:T(8,128)(2,1)S(1)}, u32[]{:S(2)}, u32[]{:S(2)}) collective-permute-start(bf16[1,1024,256]{2,1,0:T(8,128)(2,1)S(1)} %fusion.173), channel_id=1, source_target_pairs={{0,4},{4,0},{8,12},{12,8},{1,5},{5,1},{9,13},{13,9},{2,6},{6,2},{1... | collective-permute-start | bytes 1572872 | tf_op jit(solution)/shard_map/ppermute | solution.py:67
  906.0 4.4 collective-permute-start.15
  907.6 16.7 %collective-permute-start.12 = (bf16[1,1024,256]{2,1,0:T(8,128)(2,1)S(1)}, bf16[1,1024,256]{2,1,0:T(8,128)(2,1)S(1)}, u32[]{:S(2)}, u32[]{:S(2)}) collective-permute-start(bf16[1,1024,256]{2,1,0:T(8,128)(2,1)S(1)} %fusion.155), channel_id=1, source_target_pairs={{8,0},{12,4},{9,1},{13,5},{10,2},{14,6},{11,3},{15,7},{24,16},{28,... | collective-permute-start | bytes 1572872 | tf_op jit(solution)/shard_map/ppermute | solution.py:37
  909.0 26.4 %collective-permute-start.14 = (bf16[1,1024,256]{2,1,0:T(8,128)(2,1)S(1)}, bf16[1,1024,256]{2,1,0:T(8,128)(2,1)S(1)}, u32[]{:S(2)}, u32[]{:S(2)}) collective-permute-start(bf16[1,1024,256]{2,1,0:T(8,128)(2,1)S(1)} %fusion.163), channel_id=1, source_target_pairs={{8,0},{12,4},{9,1},{13,5},{10,2},{14,6},{11,3},{15,7},{24,16},{28,... | collective-permute-start | bytes 1572872 | tf_op jit(solution)/shard_map/ppermute | solution.py:37
  910.6 35.2 %collective-permute-start.16 = (bf16[1,1024,256]{2,1,0:T(8,128)(2,1)S(1)}, bf16[1,1024,256]{2,1,0:T(8,128)(2,1)S(1)}, u32[]{:S(2)}, u32[]{:S(2)}) collective-permute-start(bf16[1,1024,256]{2,1,0:T(8,128)(2,1)S(1)} %fusion.168), channel_id=1, source_target_pairs={{8,0},{12,4},{9,1},{13,5},{10,2},{14,6},{11,3},{15,7},{24,16},{28,... | collective-permute-start | bytes 1572872 | tf_op jit(solution)/shard_map/ppermute | solution.py:37
  955.3 128.3 %all-gather.26.cloned.1.call-start = ((), (), s32[]{:S(2)}) async-start(), calls=%async_computation.22 | async-start | bytes 3932160 | tf_op jit(solution)/shard_map/all_gather | solution.py:41
  969.4 28.7 %collective-permute-start.17 = (bf16[1,1,1,192,2,1024]{5,3,4,2,1,0:T(8,128)(2,1)S(1)}, bf16[1,1,1,192,2,1024]{5,3,4,2,1,0:T(8,128)(2,1)S(1)}, u32[]{:S(2)}, u32[]{:S(2)}) collective-permute-start(bf16[1,1,1,192,2,1024]{5,3,4,2,1,0:T(8,128)(2,1)S(1)} %dynamic-slice_add_fusion.1), channel_id=1, source_target_pairs={{0,8},{4,12},{8,0},{12,4},{1,9},{5,13},{9,1},{13,5},{2,10},{6,14},... | collective-permute-start | bytes 2359304 | tf_op jit(solution)/shard_map/ppermute | solution.py:67
  969.6 27.1 %collective-permute-start.18 = (bf16[1,1,1,192,1024]{4,3,2,1,0:T(8,128)(2,1)S(1)}, bf16[1,1,1,192,1024]{4,3,2,1,0:T(8,128)(2,1)S(1)}, u32[]{:S(2)}, u32[]{:S(2)}) collective-permute-start(bf16[1,1,1,192,1024]{4,3,2,1,0:T(8,128)(2,1)S(1)} %dynamic-slice_add_fusion.3), channel_id=1, source_target_pairs={{0,8},{4,12},{8,0},{12,4},{1,9},{5,13},{9,1},{13,5},{2,10},{6,14},... | collective-permute-start | bytes 1179656 | tf_op jit(solution)/shard_map/ppermute | solution.py:67
  1019.9 144.7 %reduce-scatter.21.cloned.1.call-start = ((), (), s32[]{:S(2)}) async-start(), calls=%async_computation.23 | async-start | bytes 3932160 | tf_op jit(solution)/shard_map/reduce_scatter | solution.py:46
  1020.4 4.0 collective-permute-start.19
  1020.5 7.5 collective-permute-start.21
  1026.4 28.7 %collective-permute-start.20 = (bf16[1,2,1,192,1152]{4,3,2,1,0:T(8,128)(2,1)S(1)}, bf16[1,2,1,192,1152]{4,3,2,1,0:T(8,128)(2,1)S(1)}, u32[]{:S(2)}, u32[]{:S(2)}) collective-permute-start(bf16[1,2,1,192,1152]{4,3,2,1,0:T(8,128)(2,1)S(1)} %constant_dynamic-slice_fusion.8), channel_id=1, source_target_pairs={{0,16},{16,0},{1,17},{17,1},{2,18},{18,2},{3,19},{19,3},{4,20},{20... | collective-permute-start | bytes 2654216 | tf_op jit(solution)/shard_map/ppermute | solution.py:67
  1028.1 26.3 %collective-permute-start.22 = (bf16[1,2,1,192,384]{4,3,2,1,0:T(8,128)(2,1)S(1)}, bf16[1,2,1,192,384]{4,3,2,1,0:T(8,128)(2,1)S(1)}, u32[]{:S(2)}, u32[]{:S(2)}) collective-permute-start(bf16[1,2,1,192,384]{4,3,2,1,0:T(8,128)(2,1)S(1)} %constant_dynamic-slice_fusion.7), channel_id=1, source_target_pairs={{0,16},{16,0},{1,17},{17,1},{2,18},{18,2},{3,19},{19,3},{4,20},{20... | collective-permute-start | bytes 884744 | tf_op jit(solution)/shard_map/ppermute | solution.py:67
  1105.5 128.7 %all-gather.28.cloned.1.call-start = ((), (), s32[]{:S(2)}) async-start(), calls=%async_computation.24 | async-start | bytes 3932160 | tf_op jit(solution)/shard_map/all_gather | solution.py:41
  1107.5 17.5 %collective-permute-start.23 = (bf16[1,1,1,192,1152]{4,3,2,1,0:T(8,128)(2,1)}, bf16[1,1,1,192,1152]{4,3,2,1,0:T(8,128)(2,1)}, u32[]{:S(2)}, u32[]{:S(2)}) collective-permute-start(bf16[1,1,1,192,1152]{4,3,2,1,0:T(8,128)(2,1)} %constant_dynamic-slice_fusion.6), channel_id=1, source_target_pairs={{0,8},{4,12},{8,0},{12,4},{1,9},{5,13},{9,1},{13,5},{2,10},{6,14},... | collective-permute-start | bytes 1327112 | tf_op jit(solution)/shard_map/ppermute | solution.py:67
  1109.7 13.2 collective-permute-start.24
  1170.5 305.2 %reduce-scatter.17.cloned.1.call-start = ((), (), s32[]{:S(2)}) async-start(), calls=%async_computation.20 | async-start | bytes 3932160 | tf_op jit(solution)/shard_map/reduce_scatter | solution.py:46
  1170.8 12.5 collective-permute-start.25
  1170.9 7.7 collective-permute-start.27
  1181.8 66.9 %collective-permute-start.28 = (bf16[1,2,1,192,1024]{4,3,2,1,0:T(8,128)(2,1)}, bf16[1,2,1,192,1024]{4,3,2,1,0:T(8,128)(2,1)}, u32[]{:S(2)}, u32[]{:S(2)}) collective-permute-start(bf16[1,2,1,192,1024]{4,3,2,1,0:T(8,128)(2,1)} %constant_dynamic-slice_fusion.3), channel_id=1, source_target_pairs={{0,16},{16,0},{1,17},{17,1},{2,18},{18,2},{3,19},{19,3},{4,20},{20... | collective-permute-start | bytes 2359304 | tf_op jit(solution)/shard_map/ppermute | solution.py:67
  1189.0 62.2 %collective-permute-start.26 = (bf16[1,2,1,192,2,1024]{5,3,4,2,1,0:T(8,128)(2,1)}, bf16[1,2,1,192,2,1024]{5,3,4,2,1,0:T(8,128)(2,1)}, u32[]{:S(2)}, u32[]{:S(2)}) collective-permute-start(bf16[1,2,1,192,2,1024]{5,3,4,2,1,0:T(8,128)(2,1)} %constant_dynamic-slice_fusion.4), channel_id=1, source_target_pairs={{0,16},{16,0},{1,17},{17,1},{2,18},{18,2},{3,19},{19,3},{4,20},{20... | collective-permute-start | bytes 4718600 | tf_op jit(solution)/shard_map/ppermute | solution.py:67
  1246.6 9.9 collective-permute-start.29
  1248.6 282.8 %reduce-scatter.23.cloned.1.call-start = ((), (), s32[]{:S(2)}) async-start(), calls=%async_computation.25 | async-start | bytes 3932160 | tf_op jit(solution)/shard_map/reduce_scatter | solution.py:46
  1258.6 15.8 %collective-permute-start.30 = (bf16[1,2,1,192,768]{4,3,2,1,0:T(8,128)(2,1)S(1)}, bf16[1,2,1,192,768]{4,3,2,1,0:T(8,128)(2,1)S(1)}, u32[]{:S(2)}, u32[]{:S(2)}) collective-permute-start(bf16[1,2,1,192,768]{4,3,2,1,0:T(8,128)(2,1)S(1)} %constant_dynamic-slice_fusion.2), channel_id=1, source_target_pairs={{0,16},{16,0},{1,17},{17,1},{2,18},{18,2},{3,19},{19,3},{4,20},{20... | collective-permute-start | bytes 1769480 | tf_op jit(solution)/shard_map/ppermute | solution.py:67
  1296.6 62.1 %collective-permute-start.31 = (bf16[1,1,1,192,2,1024]{5,3,4,2,1,0:T(8,128)(2,1)}, bf16[1,1,1,192,2,1024]{5,3,4,2,1,0:T(8,128)(2,1)}, u32[]{:S(2)}, u32[]{:S(2)}) collective-permute-start(bf16[1,1,1,192,2,1024]{5,3,4,2,1,0:T(8,128)(2,1)} %dynamic-slice_add_fusion), channel_id=1, source_target_pairs={{0,8},{4,12},{8,0},{12,4},{1,9},{5,13},{9,1},{13,5},{2,10},{6,14},... | collective-permute-start | bytes 2359304 | tf_op jit(solution)/shard_map/ppermute | solution.py:67
  1298.1 57.8 %collective-permute-start.32 = (bf16[1,1,1,192,1024]{4,3,2,1,0:T(8,128)(2,1)}, bf16[1,1,1,192,1024]{4,3,2,1,0:T(8,128)(2,1)}, u32[]{:S(2)}, u32[]{:S(2)}) collective-permute-start(bf16[1,1,1,192,1024]{4,3,2,1,0:T(8,128)(2,1)} %dynamic-slice_add_fusion.2), channel_id=1, source_target_pairs={{0,8},{4,12},{8,0},{12,4},{1,9},{5,13},{9,1},{13,5},{2,10},{6,14},... | collective-permute-start | bytes 1179656 | tf_op jit(solution)/shard_map/ppermute | solution.py:67
  1417.4 10.3 collective-permute-start.33
  1449.9 18.9 %collective-permute-start.37 = (bf16[2,2,1,192,2,768]{5,3,4,2,1,0:T(8,128)(2,1)}, bf16[2,2,1,192,2,768]{5,3,4,2,1,0:T(8,128)(2,1)}, u32[]{:S(2)}, u32[]{:S(2)}) collective-permute-start(bf16[2,2,1,192,2,768]{5,3,4,2,1,0:T(8,128)(2,1)} %dynamic-slice_convert_fusion.4), channel_id=1, source_target_pairs={{0,4},{4,0},{8,12},{12,8},{1,5},{5,1},{9,13},{13,9},{2,6},{6,2},{1... | collective-permute-start | bytes 7077896 | tf_op jit(solution)/shard_map/ppermute | solution.py:67
  1462.2 16.6 %collective-permute-start.40 = (bf16[1,1,1,192,768]{4,3,2,1,0:T(8,128)(2,1)}, bf16[1,1,1,192,768]{4,3,2,1,0:T(8,128)(2,1)}, u32[]{:S(2)}, u32[]{:S(2)}) collective-permute-start(bf16[1,1,1,192,768]{4,3,2,1,0:T(8,128)(2,1)} %dynamic-slice_add_fusion.4), channel_id=1, source_target_pairs={{0,8},{4,12},{8,0},{12,4},{1,9},{5,13},{9,1},{13,5},{2,10},{6,14},... | collective-permute-start | bytes 884744 | tf_op jit(solution)/shard_map/ppermute | solution.py:67
  1468.5 5.8 collective-permute-start.34
  1472.8 29.1 %collective-permute-start.38 = (bf16[1,2,1,192,2,768]{5,3,4,2,1,0:T(8,128)(2,1)}, bf16[1,2,1,192,2,768]{5,3,4,2,1,0:T(8,128)(2,1)}, u32[]{:S(2)}, u32[]{:S(2)}) collective-permute-start(bf16[1,2,1,192,2,768]{5,3,4,2,1,0:T(8,128)(2,1)} %constant_dynamic-slice_fusion.1), channel_id=1, source_target_pairs={{0,16},{16,0},{1,17},{17,1},{2,18},{18,2},{3,19},{19,3},{4,20},{20... | collective-permute-start | bytes 3538952 | tf_op jit(solution)/shard_map/ppermute | solution.py:67
  1475.1 11.4 collective-permute-start.35
  1487.6 22.0 %collective-permute-start.36 = (bf16[255,768]{1,0:T(8,128)(2,1)S(1)}, bf16[255,768]{1,0:T(8,128)(2,1)S(1)}, u32[]{:S(2)}, u32[]{:S(2)}) collective-permute-start(bf16[255,768]{1,0:T(8,128)(2,1)S(1)} %fusion.188), channel_id=1, source_target_pairs={{0,16},{16,0},{1,17},{17,1},{2,18},{18,2},{3,19},{19,3},{4,20},{20... | collective-permute-start | bytes 1175048 | tf_op jit(solution)/shard_map/ppermute | solution.py:67
  1503.6 24.8 %collective-permute-start.39 = (bf16[1,1,1,192,2,768]{5,3,4,2,1,0:T(8,128)(2,1)S(1)}, bf16[1,1,1,192,2,768]{5,3,4,2,1,0:T(8,128)(2,1)S(1)}, u32[]{:S(2)}, u32[]{:S(2)}) collective-permute-start(bf16[1,1,1,192,2,768]{5,3,4,2,1,0:T(8,128)(2,1)S(1)} %constant_dynamic-slice_fusion), channel_id=1, source_target_pairs={{0,8},{4,12},{8,0},{12,4},{1,9},{5,13},{9,1},{13,5},{2,10},{6,14},... | collective-permute-start | bytes 1769480 | tf_op jit(solution)/shard_map/ppermute | solution.py:67
  (164 other events, 2244.7 us)
Sparse Core Ops, SparseCore 0:
  12.6 66.1 all-gather.13
  193.4 59.5 reduce-scatter.8
  258.6 63.5 all-gather.15
  340.8 58.8 reduce-scatter.10
  404.5 63.5 all-gather.17
  470.1 62.1 all-gather.19
  570.5 58.9 reduce-scatter.12
  635.4 63.5 all-gather.21
  725.9 58.8 reduce-scatter.14
  790.6 63.5 all-gather.23
  955.4 59.3 reduce-scatter.18
  1020.0 63.5 all-gather.25
  1105.6 58.8 reduce-scatter.20
  1170.6 63.5 all-gather.27
  1248.7 59.0 reduce-scatter.16
  1439.4 60.1 reduce-scatter.22

commit v3 on v2

--- a/solution.py
+++ b/solution.py
@@ -2,6 +2,7 @@
 import jax.numpy as jnp
 from jax import lax
 from jax.experimental import pallas as pl
+from jax.experimental.layout import Layout, with_layout_constraint
 from jax.experimental.pallas import tpu as pltpu
 from jax.sharding import PartitionSpec as P
 
@@ -43,7 +44,7 @@
 
 def reduce_rows(partial_value, event=()):
     low = after(partial_value.astype(jnp.bfloat16), event)
-    return lax.psum_scatter(low, "tp", scatter_dimension=1, tiled=True).astype(jnp.float32)
+    return lax.psum_scatter(low, "tp", scatter_dimension=1, tiled=True)
 
 
 def after(value, *events):
@@ -51,6 +52,10 @@
     if not marks:
         return value
     return value + (sum(marks) * 0.0).astype(value.dtype)
+
+
+def rowwise(value):
+    return with_layout_constraint(value, Layout(tuple(range(value.ndim))))
 
 
 def spread_sum(value, axes, kind):
@@ -68,12 +73,13 @@
 
 
 def channel_total(partial_value):
-    rows, count = (partial_value.shape[0], lax.axis_size("tp"))
-    low = partial_value.astype(jnp.bfloat16)
-    parts = lax.all_to_all(low, "tp", split_axis=1, concat_axis=0, tiled=True)
-    parts = parts.reshape((count, rows) + parts.shape[1:]).astype(jnp.float32)
-    total = jnp.sum(parts, axis=0).astype(jnp.bfloat16)
-    return lax.all_gather(total, "tp", axis=1, tiled=True)
+    low = partial_value.astype(jnp.bfloat16).astype(jnp.float32)
+    flip = 1
+    while flip < lax.axis_size("tp"):
+        other = partner(low.astype(jnp.bfloat16), "tp", flip)
+        low = (low + other.astype(jnp.float32)).astype(jnp.bfloat16).astype(jnp.float32)
+        flip *= 2
+    return low.astype(jnp.bfloat16)
 
 
 def plane_first(grad):
@@ -114,15 +120,59 @@
     return jnp.sum((starts[:, None, :] <= positions[None, :, None]).astype(jnp.int32), axis=-1)
 
 
-def norm_forward(stream, gain):
+def norm_kernel(stream_ref, part_ref, gain_ref, out_ref, normed_ref):
+    stream = stream_ref[0] + part_ref[0].astype(f32)
     scale = lax.rsqrt(jnp.mean(stream * stream, axis=-1, keepdims=True) + epsilon)
-    return (stream * scale * gain, scale)
-
-
-def norm_backward(stream, scale, gain, grad_normed):
+    out_ref[0] = stream
+    normed_ref[0] = (stream * scale * gain_ref[...]).astype(jnp.bfloat16)
+
+
+def norm_specs(stream):
+    rows, length, features = stream.shape
+    block = min(128, length)
+    tile = pl.BlockSpec((1, block, features), lambda i, j: (i, j, 0))
+    return ((rows, length // block), tile, pl.BlockSpec((1, features), lambda i, j: (0, 0)))
+
+
+def norm_forward(stream, part, gain):
+    grid, tile, line = norm_specs(stream)
+    return pl.pallas_call(
+        norm_kernel,
+        grid=grid,
+        in_specs=[tile, tile, line],
+        out_specs=[tile, tile],
+        out_shape=[
+            jax.ShapeDtypeStruct(stream.shape, f32),
+            jax.ShapeDtypeStruct(stream.shape, jnp.bfloat16),
+        ],
+        cost_estimate=cost(2),
+    )(stream, part, gain[None])
+
+
+def norm_back_kernel(stream_ref, grad_ref, part_ref, gain_ref, out_ref, low_ref):
+    stream = stream_ref[0]
+    scale = lax.rsqrt(jnp.mean(stream * stream, axis=-1, keepdims=True) + epsilon)
     unit = stream * scale
-    scaled = grad_normed * gain
-    return scale * (scaled - unit * jnp.mean(scaled * unit, axis=-1, keepdims=True))
+    scaled = part_ref[0].astype(f32) * gain_ref[...]
+    mean = jnp.mean(scaled * unit, axis=-1, keepdims=True)
+    grad = grad_ref[0] + scale * (scaled - unit * mean)
+    out_ref[0] = grad
+    low_ref[0] = grad.astype(jnp.bfloat16)
+
+
+def norm_backward(stream, grad, part, gain):
+    grid, tile, line = norm_specs(stream)
+    return pl.pallas_call(
+        norm_back_kernel,
+        grid=grid,
+        in_specs=[tile, tile, tile, line],
+        out_specs=[tile, tile],
+        out_shape=[
+            jax.ShapeDtypeStruct(stream.shape, f32),
+            jax.ShapeDtypeStruct(stream.shape, jnp.bfloat16),
+        ],
+        cost_estimate=cost(2),
+    )(stream, grad, part, gain[None])
 
 
 def gain_share(partial_value, normed, gain):
@@ -354,7 +404,7 @@
         cost_estimate=cost(46), compiler_params=params())(step, push, grad, write, read, rate, starts, later)
 
 
-def mixer_forward(normed, weights, same, flags):
+def mixer_forward(normed, weights, same, flags, late):
     (
         mixer_in,
         conv_taps,
@@ -384,6 +434,7 @@
     mixed = channel_total(
         jnp.einsum("rte,ec->rtc", inner, state_proj, preferred_element_type=jnp.float32)
     )
+    late = gather_rows(after(late, mixed))
     rank = step_proj.shape[0]
     states = decay_log.shape[0]
     step_low = mixed[:, :, :rank]
@@ -428,10 +479,10 @@
         firsts,
         span,
     )
-    return (partial_value, cache)
-
-
-def mixer_backward(grad_branch, cache, weights, same, flags, first):
+    return (partial_value, cache, late)
+
+
+def mixer_backward(grad_branch, cache, weights, same, flags, first, branch):
     (
         mixer_in,
         conv_taps,
@@ -501,7 +552,7 @@
         "rte,ke->rtk", grad_step_raw, step_proj, preferred_element_type=jnp.float32
     )
     grad_mixed = channel_total(
-        jnp.concatenate([after(grad_low, first), grad_write, grad_read], axis=-1)
+        jnp.concatenate([after(grad_low, first, branch), grad_write, grad_read], axis=-1)
     )
     grad_state_proj = jnp.einsum(
         "rte,rtc->ce", inner, grad_mixed, preferred_element_type=jnp.float32
@@ -610,15 +661,28 @@
     return lax.dot_general(left, right, dims, preferred_element_type=f32)
 
 
-def attend_kernel(heads, pieces, skip, info_ref, query_ref, key_ref, value_ref, out_ref, total_ref, held):
+def gathered_pieces(refs, wide):
+    length = refs[0].shape[1]
+    for index, ref in enumerate(refs):
+        wide[pl.ds(index * length, length), :] = ref[0]
+
+
+def attend_kernel(
+    pieces, skip, info_ref, query_ref, second_ref, first_ref, own_ref, out_ref, total_ref, wide, held
+):
     block = query_ref.shape[1]
+
+    @pl.when(pl.program_id(1) == 0)
+    def _():
+        gathered_pieces((second_ref, first_ref, own_ref), wide)
+
     first = pl.multiple_of(pl.program_id(1) * block, block)
-    low, lane = lower_edge(info_ref, pl.program_id(0) // heads, first, block)
+    low, lane = lower_edge(info_ref, pl.program_id(0), first, block)
     query = query_ref[0]
     top = jnp.full((1, block), masked_score, f32)
     for piece in range(pieces):
         at = pl.ds(pl.multiple_of(first + skip + piece * block, block), block)
-        scores = dot(key_ref[0, at, :], query, NT)
+        scores = dot(wide[at, :HDIM], query, NT)
         scores = jnp.where(piece_mask(low, lane, piece, block, pieces), scores, masked_score)
         held[piece] = scores
         top = jnp.maximum(top, jnp.max(scores, axis=0, keepdims=True))
@@ -629,51 +693,57 @@
         at = pl.ds(pl.multiple_of(first + skip + piece * block, block), block)
         soft = jnp.exp2((held[piece] - top) * slope)
         total = total + jnp.sum(soft, axis=0, keepdims=True)
-        summed = summed + dot(value_ref[0, at, :], soft.astype(jnp.bfloat16), TN)
+        summed = summed + dot(wide[at, HDIM:], soft.astype(jnp.bfloat16), TN)
     out_ref[0] = (summed / total).T.astype(jnp.bfloat16)
     total_ref[0] = top * slope + jnp.log2(total)
 
 
-def attend(info, query, wide, head):
-    rows, length, reach = (query.shape[0], query.shape[1], wide.shape[1])
+def head_specs(query, head):
+    rows, length = (query.shape[0], query.shape[1])
     block, pieces = plan_of(length)
-    skip = reach - length - WINDOW
-    body = lambda *refs: attend_kernel(1, pieces, skip, *refs)
+    halo = pl.BlockSpec((1, length, 2 * HDIM), lambda i, j: (i, 0, 0))
+    own = pl.BlockSpec((1, length, 2 * HDIM), lambda i, j: (i, 0, head))
+    narrow = pl.BlockSpec((1, block, HDIM), lambda i, j: (i, j, head))
+    plain = pl.BlockSpec((1, block, HDIM), lambda i, j: (i, j, 0))
+    line = pl.BlockSpec((1, 1, block), lambda i, j: (i, 0, j))
+    skip = 2 * length - WINDOW
+    return (rows, length, block, pieces, skip, halo, own, narrow, plain, line)
+
+
+def attend(info, query, seconds, firsts, pairs, head):
+    rows, length, block, pieces, skip, halo, own, narrow, plain, line = head_specs(query, head)
+    body = lambda *refs: attend_kernel(pieces, skip, *refs)
     return pl.pallas_call(
         body,
         grid=(rows, length // block),
-        in_specs=[
-            pl.BlockSpec(memory_space=pltpu.SMEM),
-            pl.BlockSpec((1, block, HDIM), lambda i, j: (i, j, head)),
-            pl.BlockSpec((1, reach, HDIM), lambda i, j: (i, 0, 0)),
-            pl.BlockSpec((1, reach, HDIM), lambda i, j: (i, 0, 1)),
-        ],
-        out_specs=[
-            pl.BlockSpec((1, block, HDIM), lambda i, j: (i, j, 0)),
-            pl.BlockSpec((1, 1, block), lambda i, j: (i, 0, j)),
-        ],
+        in_specs=[pl.BlockSpec(memory_space=pltpu.SMEM), narrow, halo, halo, own],
+        out_specs=[plain, line],
         out_shape=[
             jax.ShapeDtypeStruct((rows, length, HDIM), jnp.bfloat16),
             jax.ShapeDtypeStruct((rows, 1, length), f32),
         ],
-        scratch_shapes=[pltpu.VMEM((pieces, block, block), f32)],
+        scratch_shapes=[
+            pltpu.VMEM((3 * length, 2 * HDIM), jnp.bfloat16),
+            pltpu.VMEM((pieces, block, block), f32),
+        ],
         cost_estimate=cost(7),
         compiler_params=pltpu.CompilerParams(vmem_limit_bytes=VM),
-    )(info, query, wide, wide)
+    )(info, query, seconds, firsts, pairs)
 
 
 def attend_back_kernel(
-    heads, pieces, skip, info_ref, query_ref, grad_ref, key_ref, value_ref, total_ref, delta_ref,
-    gquery_ref, gkey_ref, gvalue_ref,
+    pieces, skip, info_ref, query_ref, grad_ref, second_ref, first_ref, own_ref, total_ref, delta_ref,
+    gquery_ref, gsecond_ref, gfirst_ref, gown_ref, wide, gkeys, gvalues,
 ):
-    block = query_ref.shape[1]
+    block, length = (query_ref.shape[1], own_ref.shape[1])
     first = pl.multiple_of(pl.program_id(1) * block, block)
-    low, lane = lower_edge(info_ref, pl.program_id(0) // heads, first, block)
+    low, lane = lower_edge(info_ref, pl.program_id(0), first, block)
 
     @pl.when(pl.program_id(1) == 0)
     def _():
-        gkey_ref[...] = jnp.zeros_like(gkey_ref)
-        gvalue_ref[...] = jnp.zeros_like(gvalue_ref)
+        gathered_pieces((second_ref, first_ref, own_ref), wide)
+        gkeys[...] = jnp.zeros_like(gkeys)
+        gvalues[...] = jnp.zeros_like(gvalues)
 
     query, grad = (query_ref[0], grad_ref[0])
     total, delta = (total_ref[0], delta_ref[0])
@@ -681,26 +751,29 @@
     summed = jnp.zeros((HDIM, block), f32)
     for piece in range(pieces):
         at = pl.ds(pl.multiple_of(first + skip + piece * block, block), block)
-        keys = key_ref[0, at, :]
+        keys = wide[at, :HDIM]
         scores = dot(keys, query, NT)
         allowed = piece_mask(low, lane, piece, block, pieces)
         soft = jnp.exp2(jnp.where(allowed, scores * slope - total, masked_score))
-        gvalue_ref[0, at, :] += dot(soft.astype(jnp.bfloat16), grad, NN)
-        spread = soft * (dot(value_ref[0, at, :], grad, NT) - delta)
+        gvalues[at, :] += dot(soft.astype(jnp.bfloat16), grad, NN)
+        spread = soft * (dot(wide[at, HDIM:], grad, NT) - delta)
         spread = spread.astype(jnp.bfloat16)
-        gkey_ref[0, at, :] += dot(spread, query, NN)
+        gkeys[at, :] += dot(spread, query, NN)
         summed = summed + dot(keys, spread, TN)
-    gquery_ref[0] = (summed * HDIM ** (-0.5)).T
-
-
-def attend_back(info, query, grad, wide, total, delta, head):
-    rows, length, reach = (query.shape[0], query.shape[1], wide.shape[1])
-    block, pieces = plan_of(length)
-    skip = reach - length - WINDOW
-    body = lambda *refs: attend_back_kernel(1, pieces, skip, *refs)
-    narrow = pl.BlockSpec((1, block, HDIM), lambda i, j: (i, j, head))
-    line = pl.BlockSpec((1, 1, block), lambda i, j: (i, 0, j))
-    tall = pl.BlockSpec((1, reach, HDIM), lambda i, j: (i, 0, 0))
+    gquery_ref[0] = (summed * HDIM ** (-0.5)).T.astype(jnp.bfloat16)
+
+    @pl.when(pl.program_id(1) == pl.num_programs(1) - 1)
+    def _():
+        for index, ref in enumerate((gsecond_ref, gfirst_ref, gown_ref)):
+            at = pl.ds(index * length, length)
+            ref[0, :, :HDIM] = (gkeys[at, :] * HDIM ** (-0.5)).astype(ref.dtype)
+            ref[0, :, HDIM:] = gvalues[at, :].astype(ref.dtype)
+
+
+def attend_back(info, query, grad, seconds, firsts, pairs, total, delta, head):
+    rows, length, block, pieces, skip, halo, own, narrow, plain, line = head_specs(query, head)
+    body = lambda *refs: attend_back_kernel(pieces, skip, *refs)
+    double = (rows, length, 2 * HDIM)
     return pl.pallas_call(
         body,
         grid=(rows, length // block),
@@ -708,20 +781,27 @@
             pl.BlockSpec(memory_space=pltpu.SMEM),
             narrow,
             narrow,
-            tall,
-            pl.BlockSpec((1, reach, HDIM), lambda i, j: (i, 0, 1)),
+            halo,
+            halo,
+            own,
             line,
             line,
         ],
-        out_specs=[pl.BlockSpec((1, block, HDIM), lambda i, j: (i, j, 0)), tall, tall],
+        out_specs=[plain, halo, halo, halo],
         out_shape=[
-            jax.ShapeDtypeStruct((rows, length, HDIM), f32),
-            jax.ShapeDtypeStruct((rows, reach, HDIM), f32),
-            jax.ShapeDtypeStruct((rows, reach, HDIM), f32),
+            jax.ShapeDtypeStruct((rows, length, HDIM), jnp.bfloat16),
+            jax.ShapeDtypeStruct(double, f32),
+            jax.ShapeDtypeStruct(double, jnp.bfloat16),
+            jax.ShapeDtypeStruct(double, f32),
+        ],
+        scratch_shapes=[
+            pltpu.VMEM((3 * length, 2 * HDIM), jnp.bfloat16),
+            pltpu.VMEM((3 * length, HDIM), f32),
+            pltpu.VMEM((3 * length, HDIM), f32),
         ],
         cost_estimate=cost(12),
         compiler_params=pltpu.CompilerParams(vmem_limit_bytes=VM),
-    )(info, query, grad, wide, wide, total, delta)
+    )(info, query, grad, seconds, firsts, pairs, total, delta)
 
 
 def by_head(attend_in):
@@ -734,36 +814,40 @@
 def attention_forward(normed, attend_in, attend_out, info):
     heads = attend_in.shape[2] // HDIM
     weight_query, weight_pairs = by_head(attend_in)
-    pairs = jnp.einsum(
-        "rtd,dh->rth", normed, weight_pairs, preferred_element_type=jnp.float32
-    ).astype(jnp.bfloat16)
-    query = jnp.einsum(
-        "rtd,dh->rth", normed, weight_query, preferred_element_type=jnp.float32
-    ).astype(jnp.bfloat16)
+    pairs = rowwise(
+        jnp.einsum(
+            "rtd,dh->rth", normed, weight_pairs, preferred_element_type=jnp.float32
+        ).astype(jnp.bfloat16)
+    )
+    query = rowwise(
+        jnp.einsum(
+            "rtd,dh->rth", normed, weight_query, preferred_element_type=jnp.float32
+        ).astype(jnp.bfloat16)
+    )
     odd = lax.axis_index("seq") % 2 == 1
-    wides, results = ([], [])
+    halos, results = ([], [])
     for head in range(heads):
-        own = pairs[:, :, 2 * head * HDIM : 2 * (head + 1) * HDIM]
-        seconds = from_behind(own, "seq", 2)
-        firsts = partner(jnp.where(odd, seconds, own), "seq", 1)
-        wides.append(jnp.concatenate([seconds, firsts, own], axis=1))
-        results.append(attend(info, query, wides[head], head))
+        own = rowwise(pairs[:, :, 2 * head * HDIM : 2 * (head + 1) * HDIM])
+        seconds = rowwise(from_behind(own, "seq", 2))
+        firsts = rowwise(partner(rowwise(jnp.where(odd, seconds, own)), "seq", 1))
+        halos.append((seconds, firsts))
+        results.append(attend(info, query, seconds, firsts, pairs, head))
     attended = jnp.concatenate([result[0] for result in results], axis=2)
     totals = [result[1] for result in results]
     partial_value = jnp.einsum(
         "rth,hd->rtd", attended, attend_out, preferred_element_type=jnp.float32
     )
-    return (partial_value, (normed, query, wides, attended, totals, weight_query, weight_pairs))
+    return (partial_value, (normed, query, pairs, halos, attended, totals, weight_query, weight_pairs))
 
 
 def attention_backward(grad_branch, cache, attend_in, attend_out, info, event):
-    normed, query, wides, attended, totals, weight_query, weight_pairs = cache
+    normed, query, own_pairs, halos, attended, totals, weight_query, weight_pairs = cache
     rows, length = (query.shape[0], query.shape[1])
     heads = query.shape[2] // HDIM
     grad_attended = jnp.einsum(
         "rtd,hd->rth", grad_branch, attend_out, preferred_element_type=jnp.float32
     )
-    grad_attended = after(grad_attended, event).astype(jnp.bfloat16)
+    grad_attended = rowwise(after(grad_attended, event).astype(jnp.bfloat16))
     grad_attend_out = jnp.einsum(
         "rtd,rth->dh", grad_branch, attended, preferred_element_type=jnp.float32
     )
@@ -772,24 +856,23 @@
     odd = lax.axis_index("seq") % 2 == 1
     queries, pairs, marks = ([], [], [[], []])
     for head in range(heads):
-        grad_query, grad_keys, grad_values = attend_back(
+        grad_query, second, given, own = attend_back(
             after(info, marks[head]),
             query,
             grad_attended,
-            wides[head],
+            *halos[head],
+            own_pairs,
             totals[head],
             delta[:, :, head].reshape(rows, 1, length),
             head,
         )
         queries.append(grad_query)
-        scaled = jnp.concatenate([grad_keys * HDIM ** (-0.5), grad_values], axis=2)
-        seconds, firsts, own = (scaled[:, i * length : (i + 1) * length] for i in range(3))
-        given = partner(firsts.astype(jnp.bfloat16), "seq", 1).astype(jnp.float32)
-        sent = (seconds + jnp.where(odd, given, 0.0)).astype(jnp.bfloat16)
+        given = rowwise(partner(given, "seq", 1)).astype(jnp.float32)
+        sent = rowwise((second + jnp.where(odd, given, 0.0)).astype(jnp.bfloat16))
         marks.append(sent)
-        back = from_behind(sent, "seq", -2)
-        pairs.append(own + jnp.where(odd, 0.0, given) + back.astype(jnp.float32))
-    grad_projected = jnp.concatenate(queries + pairs, axis=2).astype(jnp.bfloat16)
+        back = rowwise(from_behind(sent, "seq", -2))
+        pairs.append((own + jnp.where(odd, 0.0, given) + back.astype(jnp.float32)).astype(jnp.bfloat16))
+    grad_projected = rowwise(jnp.concatenate(queries + pairs, axis=2))
     grad_weight = jnp.einsum(
         "rtd,rth->dh", normed, grad_projected, preferred_element_type=jnp.float32
     )
@@ -865,26 +948,24 @@
         skip_gain,
         mixer_out,
     )
-    normed_mix, scale_mix = norm_forward(block_in, norm_gains[0])
-    partial_value, cache_mix = mixer_forward(
-        gather_rows(normed_mix.astype(jnp.bfloat16)), mixer_weights, same, flags
-    )
-    stream_mix = block_in + reduce_rows(partial_value)
-    normed_first, scale_first = norm_forward(stream_mix, norm_gains[1])
-    partial_value, cache_first = dense_forward(
-        gather_rows(normed_first.astype(jnp.bfloat16)), first_in, first_out
-    )
-    stream_first = stream_mix + reduce_rows(partial_value)
-    grad_stream = block_grad * valid
-    grad_second = gather_rows(grad_stream.astype(jnp.bfloat16))
-    normed_attend, scale_attend = norm_forward(stream_first, norm_gains[2])
+    grad_stream = rowwise(block_grad * valid)
+    unit = block_in * lax.rsqrt(jnp.mean(block_in * block_in, axis=-1, keepdims=True) + epsilon)
+    normed = (unit * norm_gains[0]).astype(jnp.bfloat16)
+    gathered = gather_rows(normed)
+    partial_value, cache_mix, grad_second = mixer_forward(
+        gathered, mixer_weights, same, flags, grad_stream.astype(jnp.bfloat16)
+    )
+    stream_mix, normed = norm_forward(
+        block_in, reduce_rows(partial_value, grad_second), norm_gains[1]
+    )
+    partial_value, cache_first = dense_forward(gather_rows(normed), first_in, first_out)
+    stream_first, normed = norm_forward(stream_mix, reduce_rows(partial_value), norm_gains[2])
     partial_value, cache_attend = attention_forward(
-        gather_rows(normed_attend.astype(jnp.bfloat16)), attend_in, attend_out, info
-    )
-    stream_attend = stream_first + reduce_rows(partial_value, grad_second)
-    normed_second, scale_second = norm_forward(stream_attend, norm_gains[3])
+        gather_rows(normed), attend_in, attend_out, info
+    )
+    stream_attend, normed = norm_forward(stream_first, reduce_rows(partial_value), norm_gains[3])
     partial_out, cache_second = dense_forward(
-        gather_rows(normed_second.astype(jnp.bfloat16)), second_in, second_out
+        gather_rows(normed), second_in, second_out
     )
     partial_out = partial_out.astype(jnp.bfloat16)
 
@@ -894,70 +975,68 @@
     grad_normed, firsts = dense_backward(grad_second, cache_second, second_in, second_out)
     low = grad_normed.astype(jnp.bfloat16)
     gain_four = gain_of(3, low, cache_second)
-    grad_back = norm_backward(
+    grad_stream, grad_low = norm_backward(
         stream_attend,
-        scale_second,
+        grad_stream,
+        reduce_rows(low),
         after(norm_gains[3], firsts[0][0], firsts[1][0], gain_four, partial_out),
-        reduce_rows(low),
-    )
-    grad_stream = grad_stream + grad_back
+    )
     second = [plane_second(*pair) for pair in firsts]
-    gathered = gather_rows(grad_stream.astype(jnp.bfloat16))
-    stream_out = stream_attend + reduce_rows(partial_out, gathered)
-    block_out = stream_out * valid
+    gathered = gather_rows(grad_low)
     grad_normed, firsts = attention_backward(
         gathered, cache_attend, attend_in, attend_out, info, second
     )
     low = grad_normed.astype(jnp.bfloat16)
     gain_three = gain_of(2, low, cache_attend)
     second = [plane_third(held, grad_normed) for held in second]
-    grad_back = norm_backward(
+    grad_stream, grad_low = norm_backward(
         stream_first,
-        scale_attend,
-        after(norm_gains[2], firsts[0][0], firsts[1][0], second, gain_three),
+        grad_stream,
         reduce_rows(low),
-    )
-    grad_stream = grad_stream + grad_back
+        after(norm_gains[2], firsts[0][0], firsts[1][0], second[0], second[1], gain_three),
+    )
     middle = [plane_second(*pair) for pair in firsts]
     grad_normed, firsts = dense_backward(
-        gather_rows(grad_stream.astype(jnp.bfloat16)), cache_first, first_in, first_out, middle
+        gather_rows(grad_low), cache_first, first_in, first_out, middle
     )
     middle = [plane_third(held) for held in middle]
     low = grad_normed.astype(jnp.bfloat16)
     gain_two = gain_of(1, low, cache_first)
-    grad_back = norm_backward(
+    grad_stream, grad_low = norm_backward(
         stream_mix,
-        scale_first,
-        after(norm_gains[1], firsts[0][0], firsts[1][0], middle, gain_two),
+        grad_stream,
         reduce_rows(low),
-    )
-    grad_stream = grad_stream + grad_back
+        after(norm_gains[1], firsts[0][0], firsts[1][0], middle[0], middle[1], gain_two),
+    )
     firsts = [plane_second(*pair) for pair in firsts]
+    gathered = gather_rows(grad_low)
+    branch = reduce_rows(partial_out, gathered)
+    block_out = (stream_attend + branch.astype(jnp.float32)) * valid
     grad_normed, grad_mixer_in, grad_mixer_out, small, first = mixer_backward(
-        gather_rows(grad_stream.astype(jnp.bfloat16)),
+        gathered,
         cache_mix,
         mixer_weights,
         same,
         flags,
         firsts,
+        branch,
     )
     low = grad_normed.astype(jnp.bfloat16)
     gains = jnp.stack([gain_of(0, low, cache_mix), gain_two, gain_three, gain_four])
-    grad_mixer_in = plane_third(plane_second(*plane_first(grad_mixer_in)))
+    parted = plane_first(grad_mixer_in)
     grad_normed = reduce_rows(low)
     wide = small[0].shape[1]
     small = small + (gains.reshape(-1, wide),)
     counts = [member.shape[0] for member in small]
     packed = spread_sum(jnp.concatenate(small), ("seq", "row"), jnp.bfloat16)
+    parted = (after(parted[0], packed),) + parted[1:]
+    grad_mixer_in = plane_third(plane_second(*parted))
     small, place = ([], 0)
     for count in counts:
         small.append(packed[place : place + count])
         place += count
-    gains = jnp.sum(lax.all_gather(small.pop(), "tp"), axis=0).reshape(gains.shape)
-    grad_back = norm_backward(
-        block_in, scale_mix, norm_gains[0], grad_normed
-    )
-    grad_stream = grad_stream + grad_back
+    gains = spread_sum(small.pop(), ("tp",), jnp.float32).reshape(gains.shape)
+    grad_stream, _ = norm_backward(block_in, grad_stream, grad_normed, norm_gains[0])
     middle[0] = in_order(middle[0], attend_in.shape[2] // HDIM)
     pairs = ((grad_mixer_in, grad_mixer_out), first, middle, second)
     flat = [member for pair in pairs for member in (pair[0], pair[1].T)]

time: 1550 us -> 1480 us (0.955)
  other arithmetic: 144 us -> 85.3 us
  blocking collectives: 68.1 us -> 12.3 us
  waiting for transfers between devices: 732 us -> 764 us
  local copies, waits for them, and re-layouts: 168 us -> 141 us
  Pallas kernels: 145 us -> 169 us
    ppermute x33 -> x39, waiting for transfers between devices: 127 us -> 171 us  [partner(): lax.ppermute(x, axis, [(i, i ^ flip) for i in range(lax.axis_size(axis))])]
    all_gather x3 -> x0, blocking collectives: 42.7 us -> none  [the longest x2 29.4 us: channel_total(): return lax.all_gather(total, 'tp', axis=1, tiled=True)]
    all_gather x8, waiting for transfers between devices: 345 us -> 322 us  [gather_rows(): return lax.all_gather(local, 'tp', axis=1, tiled=True)]
    pallas_call x0 -> x7, Pallas kernels: none -> 22.4 us  [the longest x4 14.2 us: norm_backward(): pl.pallas_call(norm_back_kernel, grid=grid, in_specs=[tile, tile, tile, l...]
    unnamed x353 -> x304, local copies, waits for them, and re-layouts: 67.1 us -> 44.9 us
    convert_element_type x11 -> x7, other arithmetic: 23.5 us -> 4.14 us  [the longest x1 2.49 us: shards(): normed = (unit * norm_gains[0]).astype(jnp.bfloat16)]
    reduce_sum x11 -> x1, other arithmetic: 19.7 us -> 1.59 us  [shards(): jnp.mean(block_in * block_in, axis=-1, keepdims=True) + epsilon]
    ppermute x8, waiting for transfers between devices: 43.8 us -> 61.3 us  [from_behind(): return lax.ppermute(x, axis, pairs)]
  transfers between devices with their start and end apart: 58 -> 63, of which waited for: 28 -> 40; matrix products, arithmetic and copies ran while one was open for 19% -> 17% of each run, Pallas kernels for 6% -> 9%
where the time goes in v3:
time: 1480 us; the launch traced here: 1470 us
  waiting for transfers between devices  764 us (52%)
  matrix products  203 us (14%)
  Pallas kernels  169 us (11%)
  local copies, waits for them, and re-layouts  141 us (10%)
  other arithmetic  85.3 us (6%)
  starting transfers between devices  48.5 us (3%)
  between operations  42.6 us (3%)
    all_gather x8, waiting for transfers between devices, gather_rows(): return lax.all_gather(local, 'tp', axis=1, tiled=True)  322 us
    reduce_scatter x8, waiting for transfers between devices, reduce_rows(): return lax.psum_scatter(low, 'tp', scatter_dimension=1, tiled=True)  209 us
    ppermute x39, waiting for transfers between devices, partner(): lax.ppermute(x, axis, [(i, i ^ flip) for i in range(lax.axis_size(axis))])  171 us
    ppermute x8, waiting for transfers between devices, from_behind(): return lax.ppermute(x, axis, pairs)  61.3 us
    pallas_call x1, Pallas kernels, scan_back(): pl.pallas_call(back_kernel, grid=(n,), in_specs=[big, big, big, thin, thi...  45.6 us
    unnamed x304, local copies, waits for them, and re-layouts  44.9 us
    pallas_call x3, Pallas kernels, attend_back(): pl.pallas_call(body, grid=(rows, length // block), in_specs=[pl.BlockSpec...  36.7 us
  transfers between devices with their start and end apart: 63, of which 40 were waited for; matrix products, arithmetic and copies ran while one was open for 17% of the time, Pallas kernels for 9%

profile of v3, /device:TPU:0, one launch (start us, length us, event | category | flops | bytes accessed | tf_op | source)
XLA Modules:
  0.0 1466.0 jit_solution(1908851019960635117)
XLA Ops:
  18.2 61.7 %all-gather.11.cloned.1.call-done = bf16[1,1024,1536]{2,1,0:T(8,128)(2,1)} async-done(((bf16[1,256,1536]{2,1,0:T(8,128)(2,1)}), bf16[1,1024,1536]{2,1,0:T(8,128)(2,1)}) %all-gather.11.cloned.1.call-update) | async-done | bytes 3145744 | tf_op jit(solution)/shard_map/all_gather | solution.py:42
  79.9 8.3 fusion.92
  96.8 8.0 collective-permute-done.1
  109.9 9.8 collective-permute-done.2
  124.2 5.3 convert_multiply_fusion.3
  131.7 11.5 shard_map.340
  143.2 6.0 all-gather
  149.4 20.6 %shard_map.341 = (f32[1,1024,768]{2,1,0:T(8,128)S(1)}, f32[1,8,16,768]{3,2,1,0:T(8,128)S(1)}) custom-call(f32[1,1024,768]{2,1,0:T(8,128)} %copy-done.4, f32[1,1024,768]{2,1,0:T(8,128)} %get-tuple-element.240.push_ref, f32[1,16,1024]{2,1,0:T(8,128)S(1)} %get-tuple-element.223.write_ref, f32[1,16,1024]{2,1,0:T(8,128)S(1)} %get-tuple-element.222.read_ref, ...), custom_call_target="tpu_custom_call" | custom-call | flops 20999999488 | bytes 63000000 | tf_op jit(solution)/shard_map/pallas_call | solution.py:286
  176.4 9.7 all-gather.13.cloned.1.call-done
  188.0 6.4 add_bitcast_fusion.1
  194.4 58.5 %reduce-scatter.9.cloned.1.call-done.part_ref = bf16[1,256,1536]{2,1,0:T(8,128)(2,1)} async-done(((bf16[1,1024,1536]{2,1,0:T(8,128)(2,1)}), bf16[1,256,1536]{2,1,0:T(8,128)(2,1)}) %reduce-scatter.9.cloned.1.call-update) | async-done | bytes 786448 | tf_op jit(solution)/shard_map/reduce_scatter | solution.py:47
  255.8 63.6 %all-gather.15.cloned.1.call-done = bf16[1,1024,1536]{2,1,0:T(8,128)(2,1)} async-done(((bf16[1,256,1536]{2,1,0:T(8,128)(2,1)}), bf16[1,1024,1536]{2,1,0:T(8,128)(2,1)}) %all-gather.15.cloned.1.call-update) | async-done | bytes 3145744 | tf_op jit(solution)/shard_map/all_gather | solution.py:42
  319.4 10.2 fusion.50
  337.8 59.0 %reduce-scatter.11.cloned.1.call-done.part_ref = bf16[1,256,1536]{2,1,0:T(8,128)(2,1)} async-done(((bf16[1,1024,1536]{2,1,0:T(8,128)(2,1)}), bf16[1,256,1536]{2,1,0:T(8,128)(2,1)}) %reduce-scatter.11.cloned.1.call-update) | async-done | bytes 786448 | tf_op jit(solution)/shard_map/reduce_scatter | solution.py:47
  399.6 6.1 copy.121
  409.2 54.0 %all-gather.17.cloned.1.call-done = bf16[1,1024,1536]{2,1,0:T(8,128)(2,1)} async-done(((bf16[1,256,1536]{2,1,0:T(8,128)(2,1)}), bf16[1,1024,1536]{2,1,0:T(8,128)(2,1)}) %all-gather.17.cloned.1.call-update) | async-done | bytes 3145744 | tf_op jit(solution)/shard_map/all_gather | solution.py:42
  463.2 5.2 fusion.128.refs_4_.refs_5_
  474.6 10.7 collective-permute-done.7.refs_2_.refs_3_
  496.0 7.5 collective-permute-done.3.refs_2_.refs_3_
  503.5 9.3 collective-permute-done.5.refs_2_.refs_3_
  513.5 7.4 shard_map.346
  520.9 6.7 shard_map.344
  527.8 6.7 shard_map.345
  539.1 60.4 %reduce-scatter.13.cloned.1.call-done.part_ref = bf16[1,256,1536]{2,1,0:T(8,128)(2,1)} async-done(((bf16[1,1024,1536]{2,1,0:T(8,128)(2,1)}), bf16[1,256,1536]{2,1,0:T(8,128)(2,1)}) %reduce-scatter.13.cloned.1.call-update) | async-done | bytes 786448 | tf_op jit(solution)/shard_map/reduce_scatter | solution.py:47
  602.6 63.4 %all-gather.19.cloned.1.call-done = bf16[1,1024,1536]{2,1,0:T(8,128)(2,1)} async-done(((bf16[1,256,1536]{2,1,0:T(8,128)(2,1)}), bf16[1,1024,1536]{2,1,0:T(8,128)(2,1)}) %all-gather.19.cloned.1.call-update) | async-done | bytes 3145744 | tf_op jit(solution)/shard_map/all_gather | solution.py:42
  666.0 10.2 fusion.53
  676.2 6.5 fusion.109
  682.8 10.0 multiply_reduce_fusion.3
  699.4 9.6 fusion.10
  713.7 8.2 fusion.107
  734.7 17.2 %reduce-scatter.15.cloned.1.call-done.part_ref = bf16[1,256,1536]{2,1,0:T(8,128)(2,1)} async-done(((bf16[1,1024,1536]{2,1,0:T(8,128)(2,1)}), bf16[1,256,1536]{2,1,0:T(8,128)(2,1)}) %reduce-scatter.15.cloned.1.call-update) | async-done | bytes 786448 | tf_op jit(solution)/shard_map/reduce_scatter | solution.py:47
  771.1 44.4 %collective-permute-done.12 = bf16[1,2,1,192,1024]{4,3,2,1,0:T(8,128)(2,1)} collective-permute-done((bf16[1,2,1,192,1024]{4,3,2,1,0:T(8,128)(2,1)}, bf16[1,2,1,192,1024]{4,3,2,1,0:T(8,128)(2,1)}, u32[]{:S(2)}, u32[]{:S(2)}) %collective-permute-start.12) | collective-permute-done | bytes 786464 | tf_op jit(solution)/shard_map/ppermute | solution.py:72
  823.2 5.7 convert_multiply_fusion.4
  833.2 12.3 shard_map.349
  845.7 12.1 shard_map.350
  859.7 12.2 shard_map.351
  876.7 12.1 collective-permute-done.14
  889.0 11.0 collective-permute-done.16
  900.2 10.6 collective-permute-done.18
  933.5 6.8 copy.131
  944.5 6.9 fusion.98
  955.8 14.0 collective-permute-done.20
  974.1 6.0 reduce-scatter.17.cloned.1.call-done.part_ref
  993.5 25.7 %collective-permute-done.24 = bf16[1,2,1,192,384]{4,3,2,1,0:T(8,128)(2,1)S(1)} collective-permute-done((bf16[1,2,1,192,384]{4,3,2,1,0:T(8,128)(2,1)S(1)}, bf16[1,2,1,192,384]{4,3,2,1,0:T(8,128)(2,1)S(1)}, u32[]{:S(2)}, u32[]{:S(2)}) %collective-permute-start.24) | collective-permute-done | bytes 294944 | tf_op jit(solution)/shard_map/ppermute | solution.py:72
  1021.8 25.6 %all-gather.23.cloned.1.call-done = bf16[1,1024,1536]{2,1,0:T(8,128)(2,1)} async-done(((bf16[1,256,1536]{2,1,0:T(8,128)(2,1)}), bf16[1,1024,1536]{2,1,0:T(8,128)(2,1)}) %all-gather.23.cloned.1.call-update) | async-done | bytes 3145744 | tf_op jit(solution)/shard_map/all_gather | solution.py:42
  1047.4 10.1 fusion.110
  1057.5 11.7 multiply_reduce_fusion.1
  1077.7 6.9 collective-permute-done.26
  1086.6 9.6 fusion.8
  1105.2 8.0 fusion.105
  1120.2 8.2 reduce-scatter.19.cloned.1.call-done.part_ref
  1135.0 7.6 collective-permute-done.27
  1154.1 43.7 %all-gather.25.cloned.1.call-done = bf16[1,1024,1536]{1,2,0:T(8,128)(2,1)} async-done(((bf16[1,256,1536]{1,2,0:T(8,128)(2,1)}), bf16[1,1024,1536]{1,2,0:T(8,128)(2,1)}) %all-gather.25.cloned.1.call-update) | async-done | bytes 3145744 | tf_op jit(solution)/shard_map/all_gather | solution.py:42
  1220.9 11.5 fusion.60
  1236.6 11.4 shard_map.354
  1251.0 6.3 all-gather.1
  1259.5 45.6 %shard_map.355 = (f32[1,1024,768]{2,1,0:T(8,128)S(1)}, f32[1,1024,768]{2,1,0:T(8,128)}, f32[1,1,16384]{2,1,0:T(1,128)S(1)}, f32[1,1,16384]{2,1,0:T(1,128)S(1)}, f32[16,768]{1,0:T(8,128)S(1)}) custom-call(f32[1,1024,768]{2,1,0:T(8,128)} %copy-done.4, f32[1,1024,768]{2,1,0:T(8,128)} %get-tuple-element.240.push_ref, f32[1,1024,768]{2,1,0:T(8,128)} %bitcast.570, ...), custom_call_target="tpu_custom_call" | custom-call | flops 46000001024 | bytes 138000000 | tf_op jit(solution)/shard_map/pallas_call | solution.py:391
  1321.3 7.9 collective-permute-done.35
  1332.1 10.9 collective-permute-done.36
  1343.8 12.9 multiply_reduce_fusion.4
  1366.1 6.7 multiply_reduce_fusion
  1383.9 5.4 collective-permute-done.39
  1391.0 7.7 fusion.61
  1429.7 6.5 collective-permute-done.44
  (640 shorter events, 341.9 us)
Async XLA Ops:
  7.2 669.0 %copy-start = (bf16[1024,1536]{1,0:T(8,128)(2,1)S(1)}, bf16[1024,1536]{1,0:T(8,128)(2,1)}, u32[]{:S(2)}) copy-start(bf16[1024,1536]{1,0:T(8,128)(2,1)} %param.38) | copy-start | bytes 9437188
  7.2 72.7 %all-gather.11.cloned.1.call-start = ((), (), s32[]{:S(2)}) async-start(), calls=%async_computation.8 | async-start | bytes 3932160 | tf_op jit(solution)/shard_map/all_gather | solution.py:42
  13.6 172.6 %all-gather.13.cloned.1.call-start = ((), (), s32[]{:S(2)}) async-start(), calls=%async_computation.9 | async-start | bytes 3932160 | tf_op jit(solution)/shard_map/all_gather | solution.py:42
  88.5 2.7 collective-permute-start
  96.2 8.5 collective-permute-start.1
  104.8 14.9 %collective-permute-start.2 = (bf16[1,1024,128]{1,2,0:T(8,128)(2,1)S(1)}, bf16[1,1024,128]{1,2,0:T(8,128)(2,1)}, u32[]{:S(2)}, u32[]{:S(2)}) collective-permute-start(bf16[1,1024,128]{1,2,0:T(8,128)(2,1)S(1)} %add_convert_fusion.21), channel_id=1, source_target_pairs={{0,2},{1,3},{2,0},{3,1},{4,6},{5,7},{6,4},{7,5},{8,10},{9,11},{10,... | collective-permute-start | bytes 786440 | tf_op jit(solution)/shard_map/ppermute | solution.py:72
  124.1 128.9 %reduce-scatter.9.cloned.1.call-start = ((), (), s32[]{:S(2)}) async-start(), calls=%async_computation.10 | async-start | bytes 3932160 | tf_op jit(solution)/shard_map/reduce_scatter | solution.py:47
  194.4 125.0 %all-gather.15.cloned.1.call-start = ((), (), s32[]{:S(2)}) async-start(), calls=%async_computation.11 | async-start | bytes 3932160 | tf_op jit(solution)/shard_map/all_gather | solution.py:42
  255.7 141.0 %reduce-scatter.11.cloned.1.call-start = ((), (), s32[]{:S(2)}) async-start(), calls=%async_computation.12 | async-start | bytes 3932160 | tf_op jit(solution)/shard_map/reduce_scatter | solution.py:47
  337.8 125.4 %all-gather.17.cloned.1.call-start = ((), (), s32[]{:S(2)}) async-start(), calls=%async_computation.13 | async-start | bytes 3932160 | tf_op jit(solution)/shard_map/all_gather | solution.py:42
  399.5 200.0 %reduce-scatter.13.cloned.1.call-start = ((), (), s32[]{:S(2)}) async-start(), calls=%async_computation.14 | async-start | bytes 3932160 | tf_op jit(solution)/shard_map/reduce_scatter | solution.py:47
  470.4 14.8 %collective-permute-start.7 = (bf16[1,1024,256]{2,1,0:T(8,128)(2,1)}, bf16[1,1024,256]{2,1,0:T(8,128)(2,1)}, u32[]{:S(2)}, u32[]{:S(2)}) collective-permute-start(bf16[1,1024,256]{2,1,0:T(8,128)(2,1)} %slice.459), channel_id=1, source_target_pairs={{0,8},{4,12},{1,9},{5,13},{2,10},{6,14},{3,11},{7,15},{16,24},{20,... | collective-permute-start | bytes 1572872 | tf_op jit(solution)/shard_map/ppermute | solution.py:38
  486.7 16.8 %collective-permute-start.3 = (bf16[1,1024,256]{2,1,0:T(8,128)(2,1)S(1)}, bf16[1,1024,256]{2,1,0:T(8,128)(2,1)S(1)}, u32[]{:S(2)}, u32[]{:S(2)}) collective-permute-start(bf16[1,1024,256]{2,1,0:T(8,128)(2,1)S(1)} %get-tuple-element.213), channel_id=1, source_target_pairs={{0,8},{4,12},{1,9},{5,13},{2,10},{6,14},{3,11},{7,15},{16,24},{20,... | collective-permute-start | bytes 1572872 | tf_op jit(solution)/shard_map/ppermute | solution.py:38
  491.2 21.6 %collective-permute-start.5 = (bf16[1,1024,256]{2,1,0:T(8,128)(2,1)S(1)}, bf16[1,1024,256]{2,1,0:T(8,128)(2,1)S(1)}, u32[]{:S(2)}, u32[]{:S(2)}) collective-permute-start(bf16[1,1024,256]{2,1,0:T(8,128)(2,1)S(1)} %get-tuple-element.212), channel_id=1, source_target_pairs={{0,8},{4,12},{1,9},{5,13},{2,10},{6,14},{3,11},{7,15},{16,24},{20,... | collective-permute-start | bytes 1572872 | tf_op jit(solution)/shard_map/ppermute | solution.py:38
  492.8 20.7 %collective-permute-start.8 = (bf16[1,1024,256]{2,1,0:T(8,128)(2,1)S(1)}, bf16[1,1024,256]{2,1,0:T(8,128)(2,1)S(1)}, u32[]{:S(2)}, u32[]{:S(2)}) collective-permute-start(bf16[1,1024,256]{2,1,0:T(8,128)(2,1)S(1)} %get-tuple-element.211), channel_id=1, source_target_pairs={{0,4},{4,0},{8,12},{12,8},{1,5},{5,1},{9,13},{13,9},{2,6},{6,2},{1... | collective-permute-start | bytes 1572872 | tf_op jit(solution)/shard_map/ppermute | solution.py:72
  512.9 8.0 collective-permute-start.4
  513.0 14.8 %collective-permute-start.6 = (bf16[1,1024,256]{2,1,0:T(8,128)(2,1)S(1)}, bf16[1,1024,256]{2,1,0:T(8,128)(2,1)S(1)}, u32[]{:S(2)}, u32[]{:S(2)}) collective-permute-start(bf16[1,1024,256]{2,1,0:T(8,128)(2,1)S(1)} %get-tuple-element.214), channel_id=1, source_target_pairs={{0,4},{4,0},{8,12},{12,8},{1,5},{5,1},{9,13},{13,9},{2,6},{6,2},{1... | collective-permute-start | bytes 1572872 | tf_op jit(solution)/shard_map/ppermute | solution.py:72
  539.1 127.0 %all-gather.19.cloned.1.call-start = ((), (), s32[]{:S(2)}) async-start(), calls=%async_computation.15 | async-start | bytes 3932160 | tf_op jit(solution)/shard_map/all_gather | solution.py:42
  602.3 149.6 %reduce-scatter.15.cloned.1.call-start = ((), (), s32[]{:S(2)}) async-start(), calls=%async_computation.16 | async-start | bytes 3932160 | tf_op jit(solution)/shard_map/reduce_scatter | solution.py:47
  692.8 130.4 %all-gather.21.cloned.1.call-start = ((), (), s32[]{:S(2)}) async-start(), calls=%async_computation.17 | async-start | bytes 3932160 | tf_op jit(solution)/shard_map/all_gather | solution.py:42
  713.7 42.1 %collective-permute-start.9 = (bf16[2,2,1,192,2,1024]{5,3,4,2,1,0:T(8,128)(2,1)}, bf16[2,2,1,192,2,1024]{5,3,4,2,1,0:T(8,128)(2,1)}, u32[]{:S(2)}, u32[]{:S(2)}) collective-permute-start(bf16[2,2,1,192,2,1024]{5,3,4,2,1,0:T(8,128)(2,1)} %dynamic-slice_convert_fusion.3), channel_id=1, source_target_pairs={{0,4},{4,0},{8,12},{12,8},{1,5},{5,1},{9,13},{13,9},{2,6},{6,2},{1... | collective-permute-start | bytes 9437192 | tf_op jit(solution)/shard_map/ppermute | solution.py:72
  755.5 224.7 %reduce-scatter.17.cloned.1.call-start = ((), (), s32[]{:S(2)}) async-start(), calls=%async_computation.18 | async-start | bytes 3932160 | tf_op jit(solution)/shard_map/reduce_scatter | solution.py:47
  755.7 7.4 collective-permute-start.11
  761.6 56.5 %collective-permute-start.10 = (bf16[1,2,1,192,2,1024]{5,3,4,2,1,0:T(8,128)(2,1)}, bf16[1,2,1,192,2,1024]{5,3,4,2,1,0:T(8,128)(2,1)}, u32[]{:S(2)}, u32[]{:S(2)}) collective-permute-start(bf16[1,2,1,192,2,1024]{5,3,4,2,1,0:T(8,128)(2,1)} %constant_dynamic-slice_fusion.10), channel_id=1, source_target_pairs={{0,16},{16,0},{1,17},{17,1},{2,18},{18,2},{3,19},{19,3},{4,20},{20... | collective-permute-start | bytes 4718600 | tf_op jit(solution)/shard_map/ppermute | solution.py:72
  767.4 48.1 %collective-permute-start.12 = (bf16[1,2,1,192,1024]{4,3,2,1,0:T(8,128)(2,1)}, bf16[1,2,1,192,1024]{4,3,2,1,0:T(8,128)(2,1)}, u32[]{:S(2)}, u32[]{:S(2)}) collective-permute-start(bf16[1,2,1,192,1024]{4,3,2,1,0:T(8,128)(2,1)} %constant_dynamic-slice_fusion.9), channel_id=1, source_target_pairs={{0,16},{16,0},{1,17},{17,1},{2,18},{18,2},{3,19},{19,3},{4,20},{20... | collective-permute-start | bytes 2359304 | tf_op jit(solution)/shard_map/ppermute | solution.py:72
  845.5 12.8 collective-permute-start.13
  857.8 15.7 %collective-permute-start.15 = (bf16[1,1024,256]{2,1,0:T(8,128)(2,1)S(1)}, bf16[1,1024,256]{2,1,0:T(8,128)(2,1)S(1)}, u32[]{:S(2)}, u32[]{:S(2)}) collective-permute-start(bf16[1,1024,256]{2,1,0:T(8,128)(2,1)S(1)} %get-tuple-element.78), channel_id=1, source_target_pairs={{0,4},{4,0},{8,12},{12,8},{1,5},{5,1},{9,13},{13,9},{2,6},{6,2},{1... | collective-permute-start | bytes 1572872 | tf_op jit(solution)/shard_map/ppermute | solution.py:72
  872.0 3.1 collective-permute-start.17
  872.2 16.6 %collective-permute-start.14 = (bf16[1,1024,256]{2,1,0:T(8,128)(2,1)S(1)}, bf16[1,1024,256]{2,1,0:T(8,128)(2,1)S(1)}, u32[]{:S(2)}, u32[]{:S(2)}) collective-permute-start(bf16[1,1024,256]{2,1,0:T(8,128)(2,1)S(1)} %fusion.158), channel_id=1, source_target_pairs={{8,0},{12,4},{9,1},{13,5},{10,2},{14,6},{11,3},{15,7},{24,16},{28,... | collective-permute-start | bytes 1572872 | tf_op jit(solution)/shard_map/ppermute | solution.py:38
  873.6 26.4 %collective-permute-start.16 = (bf16[1,1024,256]{2,1,0:T(8,128)(2,1)S(1)}, bf16[1,1024,256]{2,1,0:T(8,128)(2,1)S(1)}, u32[]{:S(2)}, u32[]{:S(2)}) collective-permute-start(bf16[1,1024,256]{2,1,0:T(8,128)(2,1)S(1)} %fusion.166), channel_id=1, source_target_pairs={{8,0},{12,4},{9,1},{13,5},{10,2},{14,6},{11,3},{15,7},{24,16},{28,... | collective-permute-start | bytes 1572872 | tf_op jit(solution)/shard_map/ppermute | solution.py:38
  875.2 35.7 %collective-permute-start.18 = (bf16[1,1024,256]{2,1,0:T(8,128)(2,1)S(1)}, bf16[1,1024,256]{2,1,0:T(8,128)(2,1)S(1)}, u32[]{:S(2)}, u32[]{:S(2)}) collective-permute-start(bf16[1,1024,256]{2,1,0:T(8,128)(2,1)S(1)} %fusion.171), channel_id=1, source_target_pairs={{8,0},{12,4},{9,1},{13,5},{10,2},{14,6},{11,3},{15,7},{24,16},{28,... | collective-permute-start | bytes 1572872 | tf_op jit(solution)/shard_map/ppermute | solution.py:38
  920.6 126.8 %all-gather.23.cloned.1.call-start = ((), (), s32[]{:S(2)}) async-start(), calls=%async_computation.19 | async-start | bytes 3932160 | tf_op jit(solution)/shard_map/all_gather | solution.py:42
  942.3 29.1 %collective-permute-start.19 = (bf16[1,1,1,192,2,1024]{5,3,4,2,1,0:T(8,128)(2,1)S(1)}, bf16[1,1,1,192,2,1024]{5,3,4,2,1,0:T(8,128)(2,1)S(1)}, u32[]{:S(2)}, u32[]{:S(2)}) collective-permute-start(bf16[1,1,1,192,2,1024]{5,3,4,2,1,0:T(8,128)(2,1)S(1)} %dynamic-slice_add_fusion.1), channel_id=1, source_target_pairs={{0,8},{4,12},{8,0},{12,4},{1,9},{5,13},{9,1},{13,5},{2,10},{6,14},... | collective-permute-start | bytes 2359304 | tf_op jit(solution)/shard_map/ppermute | solution.py:72
  942.4 27.4 %collective-permute-start.20 = (bf16[1,1,1,192,1024]{4,3,2,1,0:T(8,128)(2,1)S(1)}, bf16[1,1,1,192,1024]{4,3,2,1,0:T(8,128)(2,1)S(1)}, u32[]{:S(2)}, u32[]{:S(2)}) collective-permute-start(bf16[1,1,1,192,1024]{4,3,2,1,0:T(8,128)(2,1)S(1)} %dynamic-slice_add_fusion.3), channel_id=1, source_target_pairs={{0,8},{4,12},{8,0},{12,4},{1,9},{5,13},{9,1},{13,5},{2,10},{6,14},... | collective-permute-start | bytes 1179656 | tf_op jit(solution)/shard_map/ppermute | solution.py:72
  983.7 144.7 %reduce-scatter.19.cloned.1.call-start = ((), (), s32[]{:S(2)}) async-start(), calls=%async_computation.20 | async-start | bytes 3932160 | tf_op jit(solution)/shard_map/reduce_scatter | solution.py:47
  984.2 4.8 collective-permute-start.21
  984.3 8.3 collective-permute-start.23
  991.1 28.6 %collective-permute-start.22 = (bf16[1,2,1,192,1152]{4,3,2,1,0:T(8,128)(2,1)S(1)}, bf16[1,2,1,192,1152]{4,3,2,1,0:T(8,128)(2,1)S(1)}, u32[]{:S(2)}, u32[]{:S(2)}) collective-permute-start(bf16[1,2,1,192,1152]{4,3,2,1,0:T(8,128)(2,1)S(1)} %constant_dynamic-slice_fusion.8), channel_id=1, source_target_pairs={{0,16},{16,0},{1,17},{17,1},{2,18},{18,2},{3,19},{19,3},{4,20},{20... | collective-permute-start | bytes 2654216 | tf_op jit(solution)/shard_map/ppermute | solution.py:72
  992.8 26.3 %collective-permute-start.24 = (bf16[1,2,1,192,384]{4,3,2,1,0:T(8,128)(2,1)S(1)}, bf16[1,2,1,192,384]{4,3,2,1,0:T(8,128)(2,1)S(1)}, u32[]{:S(2)}, u32[]{:S(2)}) collective-permute-start(bf16[1,2,1,192,384]{4,3,2,1,0:T(8,128)(2,1)S(1)} %constant_dynamic-slice_fusion.7), channel_id=1, source_target_pairs={{0,16},{16,0},{1,17},{17,1},{2,18},{18,2},{3,19},{19,3},{4,20},{20... | collective-permute-start | bytes 884744 | tf_op jit(solution)/shard_map/ppermute | solution.py:72
  1069.3 128.5 %all-gather.25.cloned.1.call-start = ((), (), s32[]{:S(2)}) async-start(), calls=%async_computation.21 | async-start | bytes 3932160 | tf_op jit(solution)/shard_map/all_gather | solution.py:42
  1069.6 16.4 %collective-permute-start.25 = (bf16[1,1,1,192,1152]{4,3,2,1,0:T(8,128)(2,1)S(1)}, bf16[1,1,1,192,1152]{4,3,2,1,0:T(8,128)(2,1)S(1)}, u32[]{:S(2)}, u32[]{:S(2)}) collective-permute-start(bf16[1,1,1,192,1152]{4,3,2,1,0:T(8,128)(2,1)S(1)} %constant_dynamic-slice_fusion.6), channel_id=1, source_target_pairs={{0,8},{4,12},{8,0},{12,4},{1,9},{5,13},{9,1},{13,5},{2,10},{6,14},... | collective-permute-start | bytes 1327112 | tf_op jit(solution)/shard_map/ppermute | solution.py:72
  1071.1 13.5 collective-permute-start.26
  1134.2 184.6 %reduce-scatter.21.cloned.1.call-start = ((), (), s32[]{:S(2)}) async-start(), calls=%async_computation.22 | async-start | bytes 3932160 | tf_op jit(solution)/shard_map/reduce_scatter | solution.py:47
  1134.4 8.2 collective-permute-start.27
  1134.5 14.4 collective-permute-start.29
  1147.4 59.0 %collective-permute-start.28 = (bf16[1,2,1,192,2,1024]{5,3,4,2,1,0:T(8,128)(2,1)}, bf16[1,2,1,192,2,1024]{5,3,4,2,1,0:T(8,128)(2,1)}, u32[]{:S(2)}, u32[]{:S(2)}) collective-permute-start(bf16[1,2,1,192,2,1024]{5,3,4,2,1,0:T(8,128)(2,1)} %constant_dynamic-slice_fusion.4), channel_id=1, source_target_pairs={{0,16},{16,0},{1,17},{17,1},{2,18},{18,2},{3,19},{19,3},{4,20},{20... | collective-permute-start | bytes 4718600 | tf_op jit(solution)/shard_map/ppermute | solution.py:72
  1153.5 50.5 %collective-permute-start.30 = (bf16[1,2,1,192,1024]{4,3,2,1,0:T(8,128)(2,1)}, bf16[1,2,1,192,1024]{4,3,2,1,0:T(8,128)(2,1)}, u32[]{:S(2)}, u32[]{:S(2)}) collective-permute-start(bf16[1,2,1,192,1024]{4,3,2,1,0:T(8,128)(2,1)} %constant_dynamic-slice_fusion.3), channel_id=1, source_target_pairs={{0,16},{16,0},{1,17},{17,1},{2,18},{18,2},{3,19},{19,3},{4,20},{20... | collective-permute-start | bytes 2359304 | tf_op jit(solution)/shard_map/ppermute | solution.py:72
  1204.0 13.1 collective-permute-start.31
  1217.1 238.5 %reduce-scatter.23.cloned.1.call-start = ((), (), s32[]{:S(2)}) async-start(), calls=%async_computation.23 | async-start | bytes 3932160 | tf_op jit(solution)/shard_map/reduce_scatter | solution.py:47
  1219.3 15.8 %collective-permute-start.32 = (bf16[1,2,1,192,768]{4,3,2,1,0:T(8,128)(2,1)S(1)}, bf16[1,2,1,192,768]{4,3,2,1,0:T(8,128)(2,1)S(1)}, u32[]{:S(2)}, u32[]{:S(2)}) collective-permute-start(bf16[1,2,1,192,768]{4,3,2,1,0:T(8,128)(2,1)S(1)} %constant_dynamic-slice_fusion.2), channel_id=1, source_target_pairs={{0,16},{16,0},{1,17},{17,1},{2,18},{18,2},{3,19},{19,3},{4,20},{20... | collective-permute-start | bytes 1769480 | tf_op jit(solution)/shard_map/ppermute | solution.py:72
  1257.3 57.9 %collective-permute-start.33 = (bf16[1,1,1,192,2,1024]{5,3,4,2,1,0:T(8,128)(2,1)}, bf16[1,1,1,192,2,1024]{5,3,4,2,1,0:T(8,128)(2,1)}, u32[]{:S(2)}, u32[]{:S(2)}) collective-permute-start(bf16[1,1,1,192,2,1024]{5,3,4,2,1,0:T(8,128)(2,1)} %dynamic-slice_add_fusion), channel_id=1, source_target_pairs={{0,8},{4,12},{8,0},{12,4},{1,9},{5,13},{9,1},{13,5},{2,10},{6,14},... | collective-permute-start | bytes 2359304 | tf_op jit(solution)/shard_map/ppermute | solution.py:72
  1258.8 53.7 %collective-permute-start.34 = (bf16[1,1,1,192,1024]{4,3,2,1,0:T(8,128)(2,1)}, bf16[1,1,1,192,1024]{4,3,2,1,0:T(8,128)(2,1)}, u32[]{:S(2)}, u32[]{:S(2)}) collective-permute-start(bf16[1,1,1,192,1024]{4,3,2,1,0:T(8,128)(2,1)} %dynamic-slice_add_fusion.2), channel_id=1, source_target_pairs={{0,8},{4,12},{8,0},{12,4},{1,9},{5,13},{9,1},{13,5},{2,10},{6,14},... | collective-permute-start | bytes 1179656 | tf_op jit(solution)/shard_map/ppermute | solution.py:72
  1321.2 8.1 collective-permute-start.35
  1329.4 13.7 collective-permute-start.36
  1356.8 4.4 collective-permute-start.37
  1374.3 2.6 collective-permute-start.38
  1377.7 11.6 collective-permute-start.39
  1389.4 10.6 collective-permute-start.40
  1401.6 4.6 collective-permute-start.43
  1407.9 28.3 %collective-permute-start.44 = (bf16[1,2,1,192,2,768]{5,3,4,2,1,0:T(8,128)(2,1)}, bf16[1,2,1,192,2,768]{5,3,4,2,1,0:T(8,128)(2,1)}, u32[]{:S(2)}, u32[]{:S(2)}) collective-permute-start(bf16[1,2,1,192,2,768]{5,3,4,2,1,0:T(8,128)(2,1)} %constant_dynamic-slice_fusion.1), channel_id=1, source_target_pairs={{0,16},{16,0},{1,17},{17,1},{2,18},{18,2},{3,19},{19,3},{4,20},{20... | collective-permute-start | bytes 3538952 | tf_op jit(solution)/shard_map/ppermute | solution.py:72
  1417.6 8.8 collective-permute-start.46
  1437.9 14.6 collective-permute-start.45
  1440.8 3.9 collective-permute-start.41
  1444.7 4.8 collective-permute-start.42
  (147 other events, 1742.3 us)
Sparse Core Ops, SparseCore 0:
  13.7 66.1 all-gather.10
  124.2 61.8 all-gather.12
  194.5 58.4 reduce-scatter.8
  255.9 63.5 all-gather.14
  337.9 58.8 reduce-scatter.10
  399.6 63.5 all-gather.16
  539.2 60.3 reduce-scatter.12
  602.4 63.5 all-gather.18
  693.0 58.8 reduce-scatter.14
  755.6 63.5 all-gather.20
  920.7 59.3 reduce-scatter.16
  983.8 63.5 all-gather.22
  1069.4 58.8 reduce-scatter.18
  1134.3 63.4 all-gather.24
  1217.2 58.5 reduce-scatter.20
  1384.0 57.5 reduce-scatter.22

commit v4 on v3

--- a/solution.py
+++ b/solution.py
@@ -43,8 +43,15 @@
 
 
 def reduce_rows(partial_value, event=()):
-    low = after(partial_value.astype(jnp.bfloat16), event)
+    low = partial_value.astype(jnp.bfloat16)
+    if jax.tree.leaves(event):
+        low = nudged(low, event)
     return lax.psum_scatter(low, "tp", scatter_dimension=1, tiled=True)
+
+
+def nudged(value, *events):
+    corner = lax.slice(value, (0,) * value.ndim, (1,) * value.ndim)
+    return lax.dynamic_update_slice(value, after(corner, *events), (0,) * value.ndim)
 
 
 def after(value, *events):
@@ -74,12 +81,12 @@
 
 def channel_total(partial_value):
     low = partial_value.astype(jnp.bfloat16).astype(jnp.float32)
-    flip = 1
+    flip, hops = (1, [])
     while flip < lax.axis_size("tp"):
-        other = partner(low.astype(jnp.bfloat16), "tp", flip)
-        low = (low + other.astype(jnp.float32)).astype(jnp.bfloat16).astype(jnp.float32)
+        hops.append(partner(low.astype(jnp.bfloat16), "tp", flip))
+        low = (low + hops[-1].astype(jnp.float32)).astype(jnp.bfloat16).astype(jnp.float32)
         flip *= 2
-    return low.astype(jnp.bfloat16)
+    return (low.astype(jnp.bfloat16), hops[0])
 
 
 def plane_first(grad):
@@ -109,11 +116,13 @@
 
 def plane_third(held, event=()):
     if lax.axis_size("row") != 2:
-        return held.astype(jnp.float32)
+        return (held.astype(jnp.float32), held)
     seq = lax.axis_index("seq")
     given = after(lax.dynamic_slice_in_dim(held, 1 - seq // 2, 1, axis=1), event)
-    held = joined(given, lax.dynamic_slice_in_dim(held, seq // 2, 1, axis=1), "seq", 2)
-    return held.reshape(held.shape[3:])
+    kept = lax.dynamic_slice_in_dim(held, seq // 2, 1, axis=1)
+    other = partner(given, "seq", 2)
+    total = kept.astype(jnp.float32) + other.astype(jnp.float32)
+    return (total.reshape(total.shape[3:]), other)
 
 
 def doc_numbers(positions, starts):
@@ -186,8 +195,8 @@
 
 
 TB = 128
-UNROLL = 64
-UNROLL_BACK = 32
+UNROLL = 128
+UNROLL_BACK = 64
 VM = 48 * 1024 * 1024
 
 def cost(microseconds):
@@ -431,10 +440,10 @@
         )
     inner = jax.nn.silu(conv_sum).astype(jnp.bfloat16)
     source = inner.astype(jnp.float32)
-    mixed = channel_total(
+    mixed, hop = channel_total(
         jnp.einsum("rte,ec->rtc", inner, state_proj, preferred_element_type=jnp.float32)
     )
-    late = gather_rows(after(late, mixed))
+    late = gather_rows(nudged(late, hop))
     rank = step_proj.shape[0]
     states = decay_log.shape[0]
     step_low = mixed[:, :, :rank]
@@ -526,16 +535,15 @@
     grad_gate = grad_gated * result * silu_slope(gate)
     grad_skip = jnp.sum(grad_result * source, axis=(0, 1))
     rate = -jnp.exp(decay_log)
-    early = after(rate * LOG2E, first_out[0])
-    tail = scan_tail(step_far, grad_result, read_cols, early)
+    tail = scan_tail(step_far, grad_result, read_cols, rate * LOG2E)
     second_out = plane_second(*first_out)
     first = [plane_third(held, tail) for held in first]
+    first, arrived = ([pair[0] for pair in first], [pair[1] for pair in first])
     later = carried_in(tail, span, rate, "seq", True)
-    early = after(rate * LOG2E, second_out)
     decays, weights_back, write_back, read_back, grad_rate = scan_back(
-        step_far, push, grad_result, write_cols, read_cols, early, firsts, later
-    )
-    grad_mixer_out = plane_third(second_out, grad_rate)
+        step_far, push, grad_result, write_cols, read_cols, rate * LOG2E, firsts, later
+    )
+    grad_mixer_out, _ = plane_third(second_out, grad_rate)
     grad_step = decays * (1.0 / LOG2E) + weights_back * source
     grad_source = weights_back * step
     grad_write = write_back.reshape(write_in.shape)
@@ -551,15 +559,14 @@
     grad_low = jnp.einsum(
         "rte,ke->rtk", grad_step_raw, step_proj, preferred_element_type=jnp.float32
     )
-    grad_mixed = channel_total(
-        jnp.concatenate([after(grad_low, first, branch), grad_write, grad_read], axis=-1)
+    grad_mixed, _ = channel_total(
+        jnp.concatenate([after(grad_low, arrived, branch), grad_write, grad_read], axis=-1)
     )
     grad_state_proj = jnp.einsum(
         "rte,rtc->ce", inner, grad_mixed, preferred_element_type=jnp.float32
     )
-    grad_source = grad_source + jnp.einsum(
-        "rtc,ec->rte", grad_mixed, state_proj, preferred_element_type=jnp.float32
-    )
+    spread = jnp.einsum("rtc,ec->rte", grad_mixed, state_proj, preferred_element_type=jnp.float32)
+    grad_source = grad_source + after(spread, first_out[0])
     grad_conv = grad_source * silu_slope(conv_sum)
     length = grad_conv.shape[1]
     taps = conv_taps.shape[0]
@@ -596,20 +603,24 @@
         grad_rate * rate,
         grad_skip[None],
     )
-    return (grad_normed, grad_mixer_in, grad_mixer_out, small, first)
+    return (grad_normed, grad_mixer_in, grad_mixer_out, small, first, second_out)
 
 
 def dense_forward(normed, dense_in, dense_out):
-    both = jnp.einsum("rtd,dcf->rtcf", normed, dense_in, preferred_element_type=jnp.float32)
+    both = jnp.einsum(
+        "rtd,dcf->rtcf", normed, dense_in, preferred_element_type=jnp.float32
+    ).astype(jnp.bfloat16)
     gate = both[:, :, 0]
     upper = both[:, :, 1]
-    hidden = (jax.nn.silu(gate) * upper).astype(jnp.bfloat16)
+    hidden = jax.nn.silu(gate.astype(jnp.float32)) * upper.astype(jnp.float32)
+    hidden = hidden.astype(jnp.bfloat16)
     partial_value = jnp.einsum("rtf,fd->rtd", hidden, dense_out, preferred_element_type=jnp.float32)
     return (partial_value, (normed, gate, upper, hidden))
 
 
 def dense_backward(grad_branch, cache, dense_in, dense_out, event=()):
     normed, gate, upper, hidden = cache
+    gate, upper = (gate.astype(jnp.float32), upper.astype(jnp.float32))
     grad_hidden = jnp.einsum(
         "rtd,fd->rtf", grad_branch, dense_out, preferred_element_type=jnp.float32
     )
@@ -732,7 +743,7 @@
 
 
 def attend_back_kernel(
-    pieces, skip, info_ref, query_ref, grad_ref, second_ref, first_ref, own_ref, total_ref, delta_ref,
+    pieces, skip, info_ref, query_ref, grad_ref, second_ref, first_ref, own_ref, total_ref, done_ref,
     gquery_ref, gsecond_ref, gfirst_ref, gown_ref, wide, gkeys, gvalues,
 ):
     block, length = (query_ref.shape[1], own_ref.shape[1])
@@ -746,7 +757,11 @@
         gvalues[...] = jnp.zeros_like(gvalues)
 
     query, grad = (query_ref[0], grad_ref[0])
-    total, delta = (total_ref[0], delta_ref[0])
+    total = total_ref[0]
+    both = grad.astype(f32) * done_ref[0].astype(f32)
+    delta = lax.dot_general(
+        jnp.ones((8, HDIM), f32), both, NT, precision=lax.Precision.HIGHEST
+    )[:1]
     slope = HDIM ** (-0.5) * LOG2E
     summed = jnp.zeros((HDIM, block), f32)
     for piece in range(pieces):
@@ -770,7 +785,7 @@
             ref[0, :, HDIM:] = gvalues[at, :].astype(ref.dtype)
 
 
-def attend_back(info, query, grad, seconds, firsts, pairs, total, delta, head):
+def attend_back(info, query, grad, seconds, firsts, pairs, total, attended, head):
     rows, length, block, pieces, skip, halo, own, narrow, plain, line = head_specs(query, head)
     body = lambda *refs: attend_back_kernel(pieces, skip, *refs)
     double = (rows, length, 2 * HDIM)
@@ -785,7 +800,7 @@
             halo,
             own,
             line,
-            line,
+            narrow,
         ],
         out_specs=[plain, halo, halo, halo],
         out_shape=[
@@ -801,7 +816,7 @@
         ],
         cost_estimate=cost(12),
         compiler_params=pltpu.CompilerParams(vmem_limit_bytes=VM),
-    )(info, query, grad, seconds, firsts, pairs, total, delta)
+    )(info, query, grad, seconds, firsts, pairs, total, attended)
 
 
 def by_head(attend_in):
@@ -832,7 +847,7 @@
         firsts = rowwise(partner(rowwise(jnp.where(odd, seconds, own)), "seq", 1))
         halos.append((seconds, firsts))
         results.append(attend(info, query, seconds, firsts, pairs, head))
-    attended = jnp.concatenate([result[0] for result in results], axis=2)
+    attended = rowwise(jnp.concatenate([result[0] for result in results], axis=2))
     totals = [result[1] for result in results]
     partial_value = jnp.einsum(
         "rth,hd->rtd", attended, attend_out, preferred_element_type=jnp.float32
@@ -851,8 +866,6 @@
     grad_attend_out = jnp.einsum(
         "rtd,rth->dh", grad_branch, attended, preferred_element_type=jnp.float32
     )
-    both = grad_attended.astype(jnp.float32) * attended.astype(jnp.float32)
-    delta = jnp.sum(both.reshape(rows, length, heads, HDIM), axis=-1)
     odd = lax.axis_index("seq") % 2 == 1
     queries, pairs, marks = ([], [], [[], []])
     for head in range(heads):
@@ -863,7 +876,7 @@
             *halos[head],
             own_pairs,
             totals[head],
-            delta[:, :, head].reshape(rows, 1, length),
+            attended,
             head,
         )
         queries.append(grad_query)
@@ -988,7 +1001,7 @@
     )
     low = grad_normed.astype(jnp.bfloat16)
     gain_three = gain_of(2, low, cache_attend)
-    second = [plane_third(held, grad_normed) for held in second]
+    second = [plane_third(held, grad_normed)[0] for held in second]
     grad_stream, grad_low = norm_backward(
         stream_first,
         grad_stream,
@@ -999,7 +1012,7 @@
     grad_normed, firsts = dense_backward(
         gather_rows(grad_low), cache_first, first_in, first_out, middle
     )
-    middle = [plane_third(held) for held in middle]
+    middle = [plane_third(held)[0] for held in middle]
     low = grad_normed.astype(jnp.bfloat16)
     gain_two = gain_of(1, low, cache_first)
     grad_stream, grad_low = norm_backward(
@@ -1012,7 +1025,7 @@
     gathered = gather_rows(grad_low)
     branch = reduce_rows(partial_out, gathered)
     block_out = (stream_attend + branch.astype(jnp.float32)) * valid
-    grad_normed, grad_mixer_in, grad_mixer_out, small, first = mixer_backward(
+    grad_normed, grad_mixer_in, grad_mixer_out, small, first, second_out = mixer_backward(
         gathered,
         cache_mix,
         mixer_weights,
@@ -1028,9 +1041,10 @@
     wide = small[0].shape[1]
     small = small + (gains.reshape(-1, wide),)
     counts = [member.shape[0] for member in small]
-    packed = spread_sum(jnp.concatenate(small), ("seq", "row"), jnp.bfloat16)
+    packed = after(jnp.concatenate(small), second_out)
+    packed = spread_sum(packed, ("seq", "row"), jnp.bfloat16)
     parted = (after(parted[0], packed),) + parted[1:]
-    grad_mixer_in = plane_third(plane_second(*parted))
+    grad_mixer_in, _ = plane_third(plane_second(*parted))
     small, place = ([], 0)
     for count in counts:
         small.append(packed[place : place + count])

time: 1480 us -> 1450 us (0.980)
  waiting for transfers between devices: 764 us -> 742 us
  local copies, waits for them, and re-layouts: 141 us -> 161 us
  matrix products: 203 us -> 187 us
    all_gather x8, waiting for transfers between devices: 322 us -> 268 us  [gather_rows(): return lax.all_gather(local, 'tp', axis=1, tiled=True)]
    ppermute x39, waiting for transfers between devices: 171 us -> 201 us  [partner(): lax.ppermute(x, axis, [(i, i ^ flip) for i in range(lax.axis_size(axis))])]
    unnamed x304 -> x332, local copies, waits for them, and re-layouts: 44.9 us -> 44.6 us
  transfers between devices with their start and end apart: 63 -> 63, of which waited for: 40 -> 35; matrix products, arithmetic and copies ran while one was open for 17% -> 18% of each run, Pallas kernels for 9% -> 8%
where the time goes in v4:
time: 1450 us; the launch traced here: 1440 us
  waiting for transfers between devices  742 us (51%)
  matrix products  187 us (13%)
  Pallas kernels  164 us (11%)
  local copies, waits for them, and re-layouts  161 us (11%)
  other arithmetic  79.7 us (5%)
  starting transfers between devices  50.7 us (3%)
  between operations  44.3 us (3%)
    all_gather x8, waiting for transfers between devices, gather_rows(): return lax.all_gather(local, 'tp', axis=1, tiled=True)  268 us
    reduce_scatter x8, waiting for transfers between devices, reduce_rows(): return lax.psum_scatter(low, 'tp', scatter_dimension=1, tiled=True)  212 us
    ppermute x39, waiting for transfers between devices, partner(): lax.ppermute(x, axis, [(i, i ^ flip) for i in range(lax.axis_size(axis))])  201 us
    ppermute x8, waiting for transfers between devices, from_behind(): return lax.ppermute(x, axis, pairs)  60.5 us
    unnamed x332, local copies, waits for them, and re-layouts  44.6 us
    pallas_call x1, Pallas kernels, scan_back(): pl.pallas_call(back_kernel, grid=(n,), in_specs=[big, big, big, thin, thi...  42.7 us
    pallas_call x3, Pallas kernels, attend_back(): pl.pallas_call(body, grid=(rows, length // block), in_specs=[pl.BlockSpec...  38.4 us
    ppermute x39, starting transfers between devices, partner(): lax.ppermute(x, axis, [(i, i ^ flip) for i in range(lax.axis_size(axis))])  29.9 us
  transfers between devices with their start and end apart: 63, of which 35 were waited for; matrix products, arithmetic and copies ran while one was open for 18% of the time, Pallas kernels for 8%

profile of v4, /device:TPU:0, one launch (start us, length us, event | category | flops | bytes accessed | tf_op | source)
XLA Modules:
  0.0 1440.4 jit_solution(14602766804145340314)
XLA Ops:
  21.5 58.4 %all-gather.11.cloned.1.call-done = bf16[1,1024,1536]{2,1,0:T(8,128)(2,1)} async-done(((bf16[1,256,1536]{2,1,0:T(8,128)(2,1)}), bf16[1,1024,1536]{2,1,0:T(8,128)(2,1)}) %all-gather.11.cloned.1.call-update) | async-done | bytes 3145744 | tf_op jit(solution)/shard_map/all_gather | solution.py:42
  79.9 8.3 fusion.106
  98.0 8.3 collective-permute-done.1
  114.8 7.1 collective-permute-done.2
  123.0 5.4 convert_multiply_fusion.5
  130.5 10.2 shard_map.340
  140.7 5.9 all-gather
  146.8 19.1 %shard_map.341 = (f32[1,1024,768]{2,1,0:T(8,128)S(1)}, f32[1,8,16,768]{3,2,1,0:T(8,128)S(1)}) custom-call(f32[1,1024,768]{2,1,0:T(8,128)} %copy-done.4, f32[1,1024,768]{2,1,0:T(8,128)} %get-tuple-element.235.push_ref, f32[1,16,1024]{2,1,0:T(8,128)S(1)} %get-tuple-element.223.write_ref, f32[1,16,1024]{2,1,0:T(8,128)S(1)} %get-tuple-element.222.read_ref, ...), custom_call_target="tpu_custom_call" | custom-call | flops 20999999488 | bytes 63000000 | tf_op jit(solution)/shard_map/pallas_call | solution.py:295
  181.7 58.5 %reduce-scatter.9.cloned.1.call-done = bf16[1,256,1536]{1,2,0:T(8,128)(2,1)} async-done(((bf16[1,1024,1536]{1,2,0:T(8,128)(2,1)}), bf16[1,256,1536]{1,2,0:T(8,128)(2,1)}) %reduce-scatter.9.cloned.1.call-update) | async-done | bytes 786448 | tf_op jit(solution)/shard_map/reduce_scatter | solution.py:49
  245.5 63.4 %all-gather.15.cloned.1.call-done = bf16[1,1024,1536]{2,1,0:T(8,128)(2,1)} async-done(((bf16[1,256,1536]{2,1,0:T(8,128)(2,1)}), bf16[1,1024,1536]{2,1,0:T(8,128)(2,1)}) %all-gather.15.cloned.1.call-update) | async-done | bytes 3145744 | tf_op jit(solution)/shard_map/all_gather | solution.py:42
  309.0 10.2 convert_bitcast_fusion.5
  321.2 5.0 fusion.61
  326.3 59.0 %reduce-scatter.11.cloned.1.call-done.part_ref = bf16[1,256,1536]{2,1,0:T(8,128)(2,1)} async-done(((bf16[1,1024,1536]{2,1,0:T(8,128)(2,1)}), bf16[1,256,1536]{2,1,0:T(8,128)(2,1)}) %reduce-scatter.11.cloned.1.call-update) | async-done | bytes 786448 | tf_op jit(solution)/shard_map/reduce_scatter | solution.py:49
  388.1 6.1 copy.144
  397.8 54.0 %all-gather.17.cloned.1.call-done = bf16[1,1024,1536]{2,1,0:T(8,128)(2,1)} async-done(((bf16[1,256,1536]{2,1,0:T(8,128)(2,1)}), bf16[1,1024,1536]{2,1,0:T(8,128)(2,1)}) %all-gather.17.cloned.1.call-update) | async-done | bytes 3145744 | tf_op jit(solution)/shard_map/all_gather | solution.py:42
  451.8 5.2 fusion.158.refs_4_.refs_5_
  463.2 10.6 collective-permute-done.7.refs_2_.refs_3_
  484.7 7.4 collective-permute-done.3.refs_2_.refs_3_
  492.1 9.3 collective-permute-done.5.refs_2_.refs_3_
  502.1 7.4 shard_map.346
  509.5 6.7 shard_map.344
  516.4 6.7 shard_map.345
  527.8 60.5 %reduce-scatter.13.cloned.1.call-done.part_ref = bf16[1,256,1536]{2,1,0:T(8,128)(2,1)} async-done(((bf16[1,1024,1536]{2,1,0:T(8,128)(2,1)}), bf16[1,256,1536]{2,1,0:T(8,128)(2,1)}) %reduce-scatter.13.cloned.1.call-update) | async-done | bytes 786448 | tf_op jit(solution)/shard_map/reduce_scatter | solution.py:49
  591.6 63.2 %all-gather.19.cloned.1.call-done = bf16[1,1024,1536]{2,1,0:T(8,128)(2,1)} async-done(((bf16[1,256,1536]{2,1,0:T(8,128)(2,1)}), bf16[1,1024,1536]{2,1,0:T(8,128)(2,1)}) %all-gather.19.cloned.1.call-update) | async-done | bytes 3145744 | tf_op jit(solution)/shard_map/all_gather | solution.py:42
  654.7 10.2 convert_bitcast_fusion.4
  665.0 5.1 fusion.133
  670.2 8.3 multiply_reduce_fusion.3
  683.0 4.9 copy.150
  687.8 9.7 fusion.44
  718.7 18.9 %reduce-scatter.15.cloned.1.call-done.part_ref = bf16[1,256,1536]{2,1,0:T(8,128)(2,1)} async-done(((bf16[1,1024,1536]{2,1,0:T(8,128)(2,1)}), bf16[1,256,1536]{2,1,0:T(8,128)(2,1)}) %reduce-scatter.15.cloned.1.call-update) | async-done | bytes 786448 | tf_op jit(solution)/shard_map/reduce_scatter | solution.py:49
  756.7 44.5 %collective-permute-done.12 = bf16[1,2,1,192,1024]{4,3,2,1,0:T(8,128)(2,1)} collective-permute-done((bf16[1,2,1,192,1024]{4,3,2,1,0:T(8,128)(2,1)}, bf16[1,2,1,192,1024]{4,3,2,1,0:T(8,128)(2,1)}, u32[]{:S(2)}, u32[]{:S(2)}) %collective-permute-start.12) | collective-permute-done | bytes 786464 | tf_op jit(solution)/shard_map/ppermute | solution.py:79
  813.1 12.9 shard_map.349
  826.1 12.7 shard_map.350
  840.7 12.8 shard_map.351
  858.9 11.6 collective-permute-done.14
  870.7 11.0 collective-permute-done.16
  881.9 10.4 collective-permute-done.18
  906.2 4.9 copy.153
  917.2 6.7 copy.154
  928.0 6.9 fusion.120
  939.4 13.8 collective-permute-done.20
  974.5 25.7 %collective-permute-done.24 = bf16[1,2,1,192,384]{4,3,2,1,0:T(8,128)(2,1)S(1)} collective-permute-done((bf16[1,2,1,192,384]{4,3,2,1,0:T(8,128)(2,1)S(1)}, bf16[1,2,1,192,384]{4,3,2,1,0:T(8,128)(2,1)S(1)}, u32[]{:S(2)}, u32[]{:S(2)}) %collective-permute-start.24) | collective-permute-done | bytes 294944 | tf_op jit(solution)/shard_map/ppermute | solution.py:79
  1002.9 25.9 %all-gather.23.cloned.1.call-done = bf16[1,1024,1536]{2,1,0:T(8,128)(2,1)} async-done(((bf16[1,256,1536]{2,1,0:T(8,128)(2,1)}), bf16[1,1024,1536]{2,1,0:T(8,128)(2,1)}) %all-gather.23.cloned.1.call-update) | async-done | bytes 3145744 | tf_op jit(solution)/shard_map/all_gather | solution.py:42
  1028.8 9.1 fusion.134
  1037.9 11.7 multiply_reduce_fusion.1
  1053.1 4.7 copy.156
  1057.8 7.0 collective-permute-done.26
  1066.7 4.8 copy.157
  1071.6 9.1 fusion.42
  1097.3 11.3 reduce-scatter.19.cloned.1.call-done.part_ref
  1126.4 48.4 %collective-permute-done.30 = bf16[1,2,1,192,1024]{4,3,2,1,0:T(8,128)(2,1)} collective-permute-done((bf16[1,2,1,192,1024]{4,3,2,1,0:T(8,128)(2,1)}, bf16[1,2,1,192,1024]{4,3,2,1,0:T(8,128)(2,1)}, u32[]{:S(2)}, u32[]{:S(2)}) %collective-permute-start.30) | collective-permute-done | bytes 786464 | tf_op jit(solution)/shard_map/ppermute | solution.py:79
  1182.5 12.0 fusion.74
  1194.5 9.9 shard_map.354
  1211.1 5.0 fusion.145
  1217.4 6.0 all-gather.1
  1225.6 42.7 %shard_map.355 = (f32[1,1024,768]{2,1,0:T(8,128)S(1)}, f32[1,1024,768]{2,1,0:T(8,128)}, f32[1,1,16384]{2,1,0:T(1,128)S(1)}, f32[1,1,16384]{2,1,0:T(1,128)S(1)}, f32[16,768]{1,0:T(8,128)S(1)}) custom-call(f32[1,1024,768]{2,1,0:T(8,128)} %copy-done.4, f32[1,1024,768]{2,1,0:T(8,128)} %get-tuple-element.235.push_ref, f32[1,1024,768]{2,1,0:T(8,128)} %bitcast.574, ...), custom_call_target="tpu_custom_call" | custom-call | flops 46000001024 | bytes 138000000 | tf_op jit(solution)/shard_map/pallas_call | solution.py:400
  1268.3 4.7 convert_reduce_fusion
  1289.8 5.3 collective-permute-done.33
  1301.9 7.5 collective-permute-done.34
  1310.2 10.5 multiply_reduce_fusion.4
  1332.5 6.6 multiply_reduce_fusion
  1350.1 5.5 collective-permute-done.39
  1356.3 7.7 fusion.75
  1393.2 15.0 %collective-permute-done.44 = bf16[1,2,1,192,2,768]{5,3,4,2,1,0:T(8,128)(2,1)S(1)} collective-permute-done((bf16[1,2,1,192,2,768]{5,3,4,2,1,0:T(8,128)(2,1)S(1)}, bf16[1,2,1,192,2,768]{5,3,4,2,1,0:T(8,128)(2,1)S(1)}, u32[]{:S(2)}, u32[]{:S(2)}) %collective-permute-start.44) | collective-permute-done | bytes 1179680 | tf_op jit(solution)/shard_map/ppermute | solution.py:79
  (669 shorter events, 338.7 us)
Async XLA Ops:
  7.2 657.7 %copy-start = (bf16[1024,1536]{1,0:T(8,128)(2,1)S(1)}, bf16[1024,1536]{1,0:T(8,128)(2,1)}, u32[]{:S(2)}) copy-start(bf16[1024,1536]{1,0:T(8,128)(2,1)} %param.38) | copy-start | bytes 9437188
  7.2 72.7 %all-gather.11.cloned.1.call-start = ((), (), s32[]{:S(2)}) async-start(), calls=%async_computation.8 | async-start | bytes 3932160 | tf_op jit(solution)/shard_map/all_gather | solution.py:42
  13.6 164.3 %all-gather.13.cloned.1.call-start = ((), (), s32[]{:S(2)}) async-start(), calls=%async_computation.9 | async-start | bytes 3932160 | tf_op jit(solution)/shard_map/all_gather | solution.py:42
  88.5 2.6 collective-permute-start
  97.9 8.5 collective-permute-start.1
  107.1 14.8 %collective-permute-start.2 = (bf16[1,1024,128]{1,2,0:T(8,128)(2,1)S(1)}, bf16[1,1024,128]{1,2,0:T(8,128)(2,1)}, u32[]{:S(2)}, u32[]{:S(2)}) collective-permute-start(bf16[1,1024,128]{1,2,0:T(8,128)(2,1)S(1)} %add_convert_fusion.22), channel_id=1, source_target_pairs={{0,2},{1,3},{2,0},{3,1},{4,6},{5,7},{6,4},{7,5},{8,10},{9,11},{10,... | collective-permute-start | bytes 786440 | tf_op jit(solution)/shard_map/ppermute | solution.py:79
  114.6 125.7 %reduce-scatter.9.cloned.1.call-start = ((), (), s32[]{:S(2)}) async-start(), calls=%async_computation.10 | async-start | bytes 3932160 | tf_op jit(solution)/shard_map/reduce_scatter | solution.py:49
  181.6 127.3 %all-gather.15.cloned.1.call-start = ((), (), s32[]{:S(2)}) async-start(), calls=%async_computation.11 | async-start | bytes 3932160 | tf_op jit(solution)/shard_map/all_gather | solution.py:42
  245.3 140.1 %reduce-scatter.11.cloned.1.call-start = ((), (), s32[]{:S(2)}) async-start(), calls=%async_computation.12 | async-start | bytes 3932160 | tf_op jit(solution)/shard_map/reduce_scatter | solution.py:49
  326.3 125.5 %all-gather.17.cloned.1.call-start = ((), (), s32[]{:S(2)}) async-start(), calls=%async_computation.13 | async-start | bytes 3932160 | tf_op jit(solution)/shard_map/all_gather | solution.py:42
  388.1 200.2 %reduce-scatter.13.cloned.1.call-start = ((), (), s32[]{:S(2)}) async-start(), calls=%async_computation.14 | async-start | bytes 3932160 | tf_op jit(solution)/shard_map/reduce_scatter | solution.py:49
  459.0 14.8 %collective-permute-start.7 = (bf16[1,1024,256]{2,1,0:T(8,128)(2,1)}, bf16[1,1024,256]{2,1,0:T(8,128)(2,1)}, u32[]{:S(2)}, u32[]{:S(2)}) collective-permute-start(bf16[1,1024,256]{2,1,0:T(8,128)(2,1)} %slice.458), channel_id=1, source_target_pairs={{0,8},{4,12},{1,9},{5,13},{2,10},{6,14},{3,11},{7,15},{16,24},{20,... | collective-permute-start | bytes 1572872 | tf_op jit(solution)/shard_map/ppermute | solution.py:38
  475.3 16.8 %collective-permute-start.3 = (bf16[1,1024,256]{2,1,0:T(8,128)(2,1)S(1)}, bf16[1,1024,256]{2,1,0:T(8,128)(2,1)S(1)}, u32[]{:S(2)}, u32[]{:S(2)}) collective-permute-start(bf16[1,1024,256]{2,1,0:T(8,128)(2,1)S(1)} %get-tuple-element.215), channel_id=1, source_target_pairs={{0,8},{4,12},{1,9},{5,13},{2,10},{6,14},{3,11},{7,15},{16,24},{20,... | collective-permute-start | bytes 1572872 | tf_op jit(solution)/shard_map/ppermute | solution.py:38
  479.8 21.6 %collective-permute-start.5 = (bf16[1,1024,256]{2,1,0:T(8,128)(2,1)S(1)}, bf16[1,1024,256]{2,1,0:T(8,128)(2,1)S(1)}, u32[]{:S(2)}, u32[]{:S(2)}) collective-permute-start(bf16[1,1024,256]{2,1,0:T(8,128)(2,1)S(1)} %get-tuple-element.214), channel_id=1, source_target_pairs={{0,8},{4,12},{1,9},{5,13},{2,10},{6,14},{3,11},{7,15},{16,24},{20,... | collective-permute-start | bytes 1572872 | tf_op jit(solution)/shard_map/ppermute | solution.py:38
  481.4 20.7 %collective-permute-start.8 = (bf16[1,1024,256]{2,1,0:T(8,128)(2,1)S(1)}, bf16[1,1024,256]{2,1,0:T(8,128)(2,1)S(1)}, u32[]{:S(2)}, u32[]{:S(2)}) collective-permute-start(bf16[1,1024,256]{2,1,0:T(8,128)(2,1)S(1)} %get-tuple-element.213), channel_id=1, source_target_pairs={{0,4},{4,0},{8,12},{12,8},{1,5},{5,1},{9,13},{13,9},{2,6},{6,2},{1... | collective-permute-start | bytes 1572872 | tf_op jit(solution)/shard_map/ppermute | solution.py:79
  501.5 8.0 collective-permute-start.4
  501.6 14.8 %collective-permute-start.6 = (bf16[1,1024,256]{2,1,0:T(8,128)(2,1)S(1)}, bf16[1,1024,256]{2,1,0:T(8,128)(2,1)S(1)}, u32[]{:S(2)}, u32[]{:S(2)}) collective-permute-start(bf16[1,1024,256]{2,1,0:T(8,128)(2,1)S(1)} %get-tuple-element.216), channel_id=1, source_target_pairs={{0,4},{4,0},{8,12},{12,8},{1,5},{5,1},{9,13},{13,9},{2,6},{6,2},{1... | collective-permute-start | bytes 1572872 | tf_op jit(solution)/shard_map/ppermute | solution.py:79
  527.8 127.0 %all-gather.19.cloned.1.call-start = ((), (), s32[]{:S(2)}) async-start(), calls=%async_computation.15 | async-start | bytes 3932160 | tf_op jit(solution)/shard_map/all_gather | solution.py:42
  591.0 146.5 %reduce-scatter.15.cloned.1.call-start = ((), (), s32[]{:S(2)}) async-start(), calls=%async_computation.16 | async-start | bytes 3932160 | tf_op jit(solution)/shard_map/reduce_scatter | solution.py:49
  678.5 130.3 %all-gather.21.cloned.1.call-start = ((), (), s32[]{:S(2)}) async-start(), calls=%async_computation.17 | async-start | bytes 3932160 | tf_op jit(solution)/shard_map/all_gather | solution.py:42
  701.8 39.7 %collective-permute-start.9 = (bf16[2,2,1,192,2,1024]{5,3,4,2,1,0:T(8,128)(2,1)}, bf16[2,2,1,192,2,1024]{5,3,4,2,1,0:T(8,128)(2,1)}, u32[]{:S(2)}, u32[]{:S(2)}) collective-permute-start(bf16[2,2,1,192,2,1024]{5,3,4,2,1,0:T(8,128)(2,1)} %dynamic-slice_convert_fusion.3), channel_id=1, source_target_pairs={{0,4},{4,0},{8,12},{12,8},{1,5},{5,1},{9,13},{13,9},{2,6},{6,2},{1... | collective-permute-start | bytes 9437192 | tf_op jit(solution)/shard_map/ppermute | solution.py:79
  741.1 220.4 %reduce-scatter.17.cloned.1.call-start = ((), (), s32[]{:S(2)}) async-start(), calls=%async_computation.18 | async-start | bytes 3932160 | tf_op jit(solution)/shard_map/reduce_scatter | solution.py:49
  741.4 7.4 collective-permute-start.11
  747.3 56.5 %collective-permute-start.10 = (bf16[1,2,1,192,2,1024]{5,3,4,2,1,0:T(8,128)(2,1)}, bf16[1,2,1,192,2,1024]{5,3,4,2,1,0:T(8,128)(2,1)}, u32[]{:S(2)}, u32[]{:S(2)}) collective-permute-start(bf16[1,2,1,192,2,1024]{5,3,4,2,1,0:T(8,128)(2,1)} %constant_dynamic-slice_fusion.10), channel_id=1, source_target_pairs={{0,16},{16,0},{1,17},{17,1},{2,18},{18,2},{3,19},{19,3},{4,20},{20... | collective-permute-start | bytes 4718600 | tf_op jit(solution)/shard_map/ppermute | solution.py:79
  753.0 48.2 %collective-permute-start.12 = (bf16[1,2,1,192,1024]{4,3,2,1,0:T(8,128)(2,1)}, bf16[1,2,1,192,1024]{4,3,2,1,0:T(8,128)(2,1)}, u32[]{:S(2)}, u32[]{:S(2)}) collective-permute-start(bf16[1,2,1,192,1024]{4,3,2,1,0:T(8,128)(2,1)} %constant_dynamic-slice_fusion.9), channel_id=1, source_target_pairs={{0,16},{16,0},{1,17},{17,1},{2,18},{18,2},{3,19},{19,3},{4,20},{20... | collective-permute-start | bytes 2359304 | tf_op jit(solution)/shard_map/ppermute | solution.py:79
  826.1 13.2 collective-permute-start.13
  838.8 16.3 %collective-permute-start.15 = (bf16[1,1024,256]{2,1,0:T(8,128)(2,1)S(1)}, bf16[1,1024,256]{2,1,0:T(8,128)(2,1)S(1)}, u32[]{:S(2)}, u32[]{:S(2)}) collective-permute-start(bf16[1,1024,256]{2,1,0:T(8,128)(2,1)S(1)} %get-tuple-element.78), channel_id=1, source_target_pairs={{0,4},{4,0},{8,12},{12,8},{1,5},{5,1},{9,13},{13,9},{2,6},{6,2},{1... | collective-permute-start | bytes 1572872 | tf_op jit(solution)/shard_map/ppermute | solution.py:79
  853.5 3.2 collective-permute-start.17
  853.6 16.8 %collective-permute-start.14 = (bf16[1,1024,256]{2,1,0:T(8,128)(2,1)S(1)}, bf16[1,1024,256]{2,1,0:T(8,128)(2,1)S(1)}, u32[]{:S(2)}, u32[]{:S(2)}) collective-permute-start(bf16[1,1024,256]{2,1,0:T(8,128)(2,1)S(1)} %fusion.192), channel_id=1, source_target_pairs={{8,0},{12,4},{9,1},{13,5},{10,2},{14,6},{11,3},{15,7},{24,16},{28,... | collective-permute-start | bytes 1572872 | tf_op jit(solution)/shard_map/ppermute | solution.py:38
  855.2 26.4 %collective-permute-start.16 = (bf16[1,1024,256]{2,1,0:T(8,128)(2,1)S(1)}, bf16[1,1024,256]{2,1,0:T(8,128)(2,1)S(1)}, u32[]{:S(2)}, u32[]{:S(2)}) collective-permute-start(bf16[1,1024,256]{2,1,0:T(8,128)(2,1)S(1)} %fusion.200), channel_id=1, source_target_pairs={{8,0},{12,4},{9,1},{13,5},{10,2},{14,6},{11,3},{15,7},{24,16},{28,... | collective-permute-start | bytes 1572872 | tf_op jit(solution)/shard_map/ppermute | solution.py:38
  856.9 35.4 %collective-permute-start.18 = (bf16[1,1024,256]{2,1,0:T(8,128)(2,1)S(1)}, bf16[1,1024,256]{2,1,0:T(8,128)(2,1)S(1)}, u32[]{:S(2)}, u32[]{:S(2)}) collective-permute-start(bf16[1,1024,256]{2,1,0:T(8,128)(2,1)S(1)} %fusion.205), channel_id=1, source_target_pairs={{8,0},{12,4},{9,1},{13,5},{10,2},{14,6},{11,3},{15,7},{24,16},{28,... | collective-permute-start | bytes 1572872 | tf_op jit(solution)/shard_map/ppermute | solution.py:38
  902.0 126.8 %all-gather.23.cloned.1.call-start = ((), (), s32[]{:S(2)}) async-start(), calls=%async_computation.19 | async-start | bytes 3932160 | tf_op jit(solution)/shard_map/all_gather | solution.py:42
  925.8 28.9 %collective-permute-start.19 = (bf16[1,1,1,192,2,1024]{5,3,4,2,1,0:T(8,128)(2,1)S(1)}, bf16[1,1,1,192,2,1024]{5,3,4,2,1,0:T(8,128)(2,1)S(1)}, u32[]{:S(2)}, u32[]{:S(2)}) collective-permute-start(bf16[1,1,1,192,2,1024]{5,3,4,2,1,0:T(8,128)(2,1)S(1)} %dynamic-slice_add_fusion.1), channel_id=1, source_target_pairs={{0,8},{4,12},{8,0},{12,4},{1,9},{5,13},{9,1},{13,5},{2,10},{6,14},... | collective-permute-start | bytes 2359304 | tf_op jit(solution)/shard_map/ppermute | solution.py:79
  926.0 27.2 %collective-permute-start.20 = (bf16[1,1,1,192,1024]{4,3,2,1,0:T(8,128)(2,1)S(1)}, bf16[1,1,1,192,1024]{4,3,2,1,0:T(8,128)(2,1)S(1)}, u32[]{:S(2)}, u32[]{:S(2)}) collective-permute-start(bf16[1,1,1,192,1024]{4,3,2,1,0:T(8,128)(2,1)S(1)} %dynamic-slice_add_fusion.3), channel_id=1, source_target_pairs={{0,8},{4,12},{8,0},{12,4},{1,9},{5,13},{9,1},{13,5},{2,10},{6,14},... | collective-permute-start | bytes 1179656 | tf_op jit(solution)/shard_map/ppermute | solution.py:79
  965.1 143.6 %reduce-scatter.19.cloned.1.call-start = ((), (), s32[]{:S(2)}) async-start(), calls=%async_computation.20 | async-start | bytes 3932160 | tf_op jit(solution)/shard_map/reduce_scatter | solution.py:49
  965.3 4.8 collective-permute-start.21
  965.4 8.3 collective-permute-start.23
  972.2 28.7 %collective-permute-start.22 = (bf16[1,2,1,192,1152]{4,3,2,1,0:T(8,128)(2,1)S(1)}, bf16[1,2,1,192,1152]{4,3,2,1,0:T(8,128)(2,1)S(1)}, u32[]{:S(2)}, u32[]{:S(2)}) collective-permute-start(bf16[1,2,1,192,1152]{4,3,2,1,0:T(8,128)(2,1)S(1)} %constant_dynamic-slice_fusion.8), channel_id=1, source_target_pairs={{0,16},{16,0},{1,17},{17,1},{2,18},{18,2},{3,19},{19,3},{4,20},{20... | collective-permute-start | bytes 2654216 | tf_op jit(solution)/shard_map/ppermute | solution.py:79
  973.9 26.3 %collective-permute-start.24 = (bf16[1,2,1,192,384]{4,3,2,1,0:T(8,128)(2,1)S(1)}, bf16[1,2,1,192,384]{4,3,2,1,0:T(8,128)(2,1)S(1)}, u32[]{:S(2)}, u32[]{:S(2)}) collective-permute-start(bf16[1,2,1,192,384]{4,3,2,1,0:T(8,128)(2,1)S(1)} %constant_dynamic-slice_fusion.7), channel_id=1, source_target_pairs={{0,16},{16,0},{1,17},{17,1},{2,18},{18,2},{3,19},{19,3},{4,20},{20... | collective-permute-start | bytes 884744 | tf_op jit(solution)/shard_map/ppermute | solution.py:79
  1049.6 132.9 %all-gather.25.cloned.1.call-start = ((), (), s32[]{:S(2)}) async-start(), calls=%async_computation.21 | async-start | bytes 3932160 | tf_op jit(solution)/shard_map/all_gather | solution.py:42
  1049.7 16.4 %collective-permute-start.25 = (bf16[1,1,1,192,1152]{4,3,2,1,0:T(8,128)(2,1)S(1)}, bf16[1,1,1,192,1152]{4,3,2,1,0:T(8,128)(2,1)S(1)}, u32[]{:S(2)}, u32[]{:S(2)}) collective-permute-start(bf16[1,1,1,192,1152]{4,3,2,1,0:T(8,128)(2,1)S(1)} %constant_dynamic-slice_fusion.6), channel_id=1, source_target_pairs={{0,8},{4,12},{8,0},{12,4},{1,9},{5,13},{9,1},{13,5},{2,10},{6,14},... | collective-permute-start | bytes 1327112 | tf_op jit(solution)/shard_map/ppermute | solution.py:79
  1051.3 13.5 collective-permute-start.26
  1084.9 30.1 %collective-permute-start.27 = (bf16[2,2,1,192,2,1024]{5,3,4,2,1,0:T(8,128)(2,1)}, bf16[2,2,1,192,2,1024]{5,3,4,2,1,0:T(8,128)(2,1)}, u32[]{:S(2)}, u32[]{:S(2)}) collective-permute-start(bf16[2,2,1,192,2,1024]{5,3,4,2,1,0:T(8,128)(2,1)} %dynamic-slice_convert_fusion.1), channel_id=1, source_target_pairs={{0,4},{4,0},{8,12},{12,8},{1,5},{5,1},{9,13},{13,9},{2,6},{6,2},{1... | collective-permute-start | bytes 9437192 | tf_op jit(solution)/shard_map/ppermute | solution.py:79
  1114.5 169.5 %reduce-scatter.21.cloned.1.call-start = ((), (), s32[]{:S(2)}) async-start(), calls=%async_computation.22 | async-start | bytes 3932160 | tf_op jit(solution)/shard_map/reduce_scatter | solution.py:49
  1114.9 7.4 collective-permute-start.29
  1120.8 56.6 %collective-permute-start.28 = (bf16[1,2,1,192,2,1024]{5,3,4,2,1,0:T(8,128)(2,1)}, bf16[1,2,1,192,2,1024]{5,3,4,2,1,0:T(8,128)(2,1)}, u32[]{:S(2)}, u32[]{:S(2)}) collective-permute-start(bf16[1,2,1,192,2,1024]{5,3,4,2,1,0:T(8,128)(2,1)} %constant_dynamic-slice_fusion.4), channel_id=1, source_target_pairs={{0,16},{16,0},{1,17},{17,1},{2,18},{18,2},{3,19},{19,3},{4,20},{20... | collective-permute-start | bytes 4718600 | tf_op jit(solution)/shard_map/ppermute | solution.py:79
  1125.1 49.7 %collective-permute-start.30 = (bf16[1,2,1,192,1024]{4,3,2,1,0:T(8,128)(2,1)}, bf16[1,2,1,192,1024]{4,3,2,1,0:T(8,128)(2,1)}, u32[]{:S(2)}, u32[]{:S(2)}) collective-permute-start(bf16[1,2,1,192,1024]{4,3,2,1,0:T(8,128)(2,1)} %constant_dynamic-slice_fusion.3), channel_id=1, source_target_pairs={{0,16},{16,0},{1,17},{17,1},{2,18},{18,2},{3,19},{19,3},{4,20},{20... | collective-permute-start | bytes 2359304 | tf_op jit(solution)/shard_map/ppermute | solution.py:79
  1211.1 218.9 %reduce-scatter.23.cloned.1.call-start = ((), (), s32[]{:S(2)}) async-start(), calls=%async_computation.23 | async-start | bytes 3932160 | tf_op jit(solution)/shard_map/reduce_scatter | solution.py:49
  1223.4 53.8 %collective-permute-start.31 = (bf16[1,1,1,192,2,1024]{5,3,4,2,1,0:T(8,128)(2,1)}, bf16[1,1,1,192,2,1024]{5,3,4,2,1,0:T(8,128)(2,1)}, u32[]{:S(2)}, u32[]{:S(2)}) collective-permute-start(bf16[1,1,1,192,2,1024]{5,3,4,2,1,0:T(8,128)(2,1)} %dynamic-slice_add_fusion), channel_id=1, source_target_pairs={{0,8},{4,12},{8,0},{12,4},{1,9},{5,13},{9,1},{13,5},{2,10},{6,14},... | collective-permute-start | bytes 2359304 | tf_op jit(solution)/shard_map/ppermute | solution.py:79
  1224.9 51.1 %collective-permute-start.32 = (bf16[1,1,1,192,1024]{4,3,2,1,0:T(8,128)(2,1)}, bf16[1,1,1,192,1024]{4,3,2,1,0:T(8,128)(2,1)}, u32[]{:S(2)}, u32[]{:S(2)}) collective-permute-start(bf16[1,1,1,192,1024]{4,3,2,1,0:T(8,128)(2,1)} %dynamic-slice_add_fusion.2), channel_id=1, source_target_pairs={{0,8},{4,12},{8,0},{12,4},{1,9},{5,13},{9,1},{13,5},{2,10},{6,14},... | collective-permute-start | bytes 1179656 | tf_op jit(solution)/shard_map/ppermute | solution.py:79
  1225.4 54.2 %collective-permute-start.36 = (bf16[2,2,1,192,768]{4,3,2,1,0:T(8,128)(2,1)}, bf16[2,2,1,192,768]{4,3,2,1,0:T(8,128)(2,1)}, u32[]{:S(2)}, u32[]{:S(2)}) collective-permute-start(bf16[2,2,1,192,768]{4,3,2,1,0:T(8,128)(2,1)} %dynamic-slice_convert_fusion.13), channel_id=1, source_target_pairs={{0,4},{4,0},{8,12},{12,8},{1,5},{5,1},{9,13},{13,9},{2,6},{6,2},{1... | collective-permute-start | bytes 3538952 | tf_op jit(solution)/shard_map/ppermute | solution.py:79
  1282.5 17.0 %collective-permute-start.37 = (bf16[1,2,1,192,768]{4,3,2,1,0:T(8,128)(2,1)}, bf16[1,2,1,192,768]{4,3,2,1,0:T(8,128)(2,1)}, u32[]{:S(2)}, u32[]{:S(2)}) collective-permute-start(bf16[1,2,1,192,768]{4,3,2,1,0:T(8,128)(2,1)} %constant_dynamic-slice_fusion.2), channel_id=1, source_target_pairs={{0,16},{16,0},{1,17},{17,1},{2,18},{18,2},{3,19},{19,3},{4,20},{20... | collective-permute-start | bytes 1769480 | tf_op jit(solution)/shard_map/ppermute | solution.py:79
  1286.5 8.5 collective-permute-start.33
  1295.1 14.3 collective-permute-start.34
  1320.8 7.2 collective-permute-start.35
  1340.7 2.5 collective-permute-start.38
  1344.0 11.6 collective-permute-start.39
  1355.7 10.6 collective-permute-start.40
  1369.5 7.1 collective-permute-start.43
  1379.8 28.4 %collective-permute-start.44 = (bf16[1,2,1,192,2,768]{5,3,4,2,1,0:T(8,128)(2,1)S(1)}, bf16[1,2,1,192,2,768]{5,3,4,2,1,0:T(8,128)(2,1)S(1)}, u32[]{:S(2)}, u32[]{:S(2)}) collective-permute-start(bf16[1,2,1,192,2,768]{5,3,4,2,1,0:T(8,128)(2,1)S(1)} %constant_dynamic-slice_fusion.1), channel_id=1, source_target_pairs={{0,16},{16,0},{1,17},{17,1},{2,18},{18,2},{3,19},{19,3},{4,20},{20... | collective-permute-start | bytes 3538952 | tf_op jit(solution)/shard_map/ppermute | solution.py:79
  1382.9 9.4 collective-permute-start.46
  1409.7 17.1 %collective-permute-start.45 = (bf16[1,1,1,192,2,768]{5,3,4,2,1,0:T(8,128)(2,1)}, bf16[1,1,1,192,2,768]{5,3,4,2,1,0:T(8,128)(2,1)}, u32[]{:S(2)}, u32[]{:S(2)}) collective-permute-start(bf16[1,1,1,192,2,768]{5,3,4,2,1,0:T(8,128)(2,1)} %constant_dynamic-slice_fusion), channel_id=1, source_target_pairs={{0,8},{4,12},{8,0},{12,4},{1,9},{5,13},{9,1},{13,5},{2,10},{6,14},... | collective-permute-start | bytes 1769480 | tf_op jit(solution)/shard_map/ppermute | solution.py:79
  1413.8 3.8 collective-permute-start.41
  1418.4 7.8 collective-permute-start.42
  (160 other events, 1946.0 us)
Sparse Core Ops, SparseCore 0:
  13.7 66.1 all-gather.10
  114.7 63.1 all-gather.12
  181.7 58.4 reduce-scatter.8
  245.4 63.5 all-gather.14
  326.4 58.8 reduce-scatter.10
  388.2 63.5 all-gather.16
  527.9 60.3 reduce-scatter.12
  591.2 63.5 all-gather.18
  678.6 58.8 reduce-scatter.14
  741.2 63.5 all-gather.20
  902.1 59.3 reduce-scatter.16
  965.2 63.5 all-gather.22
  1049.7 58.8 reduce-scatter.18
  1114.6 63.4 all-gather.24
  1211.2 60.2 reduce-scatter.20
  1350.2 58.3 reduce-scatter.22

commit v5 on v4

--- a/solution.py
+++ b/solution.py
@@ -19,16 +19,12 @@
 
 
 def carried_in(state, span, rate, axis, backward):
-    count, mine = (lax.axis_size(axis), lax.axis_index(axis))
     both = jnp.concatenate([state, span[:, None, :]], axis=1)
-    pieces = lax.all_gather(both, axis)
-    if backward:
-        mine = count - 1 - mine
+    sign = -1 if backward else 1
     total = jnp.zeros_like(state)
-    for position in range(count - 1):
-        piece = pieces[count - 1 - position if backward else position]
-        longer = jnp.exp(rate[None] * piece[:, -1:, :]) * total + piece[:, :-1]
-        total = jnp.where(position < mine, longer, total)
+    for by in range(lax.axis_size(axis) - 1, 0, -1):
+        piece = from_behind(both, axis, sign * by)
+        total = jnp.exp(rate[None] * piece[:, -1:, :]) * total + piece[:, :-1]
     return total
 
 
@@ -123,6 +119,23 @@
     other = partner(given, "seq", 2)
     total = kept.astype(jnp.float32) + other.astype(jnp.float32)
     return (total.reshape(total.shape[3:]), other)
+
+
+def plane_halves(given, kept=None):
+    if kept is None:
+        return plane_second(given).astype(jnp.float32)
+    row, half = (lax.axis_index("row"), lax.axis_index("seq") // 2)
+    held = joined(given, kept, "seq", 1).astype(jnp.bfloat16)
+    results = []
+    for index in range(2):
+        part = held[..., index, :]
+        hops = [(0, row, "row", 1), (1, half, "seq", 2)]
+        for axis, place, name, flip in hops if index == 0 else hops[::-1]:
+            given = lax.dynamic_slice_in_dim(part, 1 - place, 1, axis=axis)
+            part = lax.dynamic_slice_in_dim(part, place, 1, axis=axis)
+            part = joined(given.astype(jnp.bfloat16), part, name, flip)
+        results.append(part.reshape(part.shape[3:]))
+    return jnp.stack(results, axis=1)
 
 
 def doc_numbers(positions, starts):
@@ -840,13 +853,15 @@
         ).astype(jnp.bfloat16)
     )
     odd = lax.axis_index("seq") % 2 == 1
-    halos, results = ([], [])
+    halos, results, mark = ([], [], ())
     for head in range(heads):
         own = rowwise(pairs[:, :, 2 * head * HDIM : 2 * (head + 1) * HDIM])
         seconds = rowwise(from_behind(own, "seq", 2))
-        firsts = rowwise(partner(rowwise(jnp.where(odd, seconds, own)), "seq", 1))
+        handed = rowwise(jnp.where(odd, after(seconds, mark), own))
+        firsts = rowwise(partner(handed, "seq", 1))
         halos.append((seconds, firsts))
         results.append(attend(info, query, seconds, firsts, pairs, head))
+        mark = results[-1][0]
     attended = rowwise(jnp.concatenate([result[0] for result in results], axis=2))
     totals = [result[1] for result in results]
     partial_value = jnp.einsum(
@@ -1044,7 +1059,7 @@
     packed = after(jnp.concatenate(small), second_out)
     packed = spread_sum(packed, ("seq", "row"), jnp.bfloat16)
     parted = (after(parted[0], packed),) + parted[1:]
-    grad_mixer_in, _ = plane_third(plane_second(*parted))
+    grad_mixer_in = plane_halves(*parted)
     small, place = ([], 0)
     for count in counts:
         small.append(packed[place : place + count])

time: 1450 us -> 1450 us (level)
  waiting for transfers between devices: 742 us -> 721 us
  starting transfers between devices: 50.7 us -> 68.5 us
    ppermute x8 -> x14, waiting for transfers between devices: 60.5 us -> 46.9 us  [from_behind(): return lax.ppermute(x, axis, pairs)]
    ppermute x8 -> x14, starting transfers between devices: 18.3 us -> 30.9 us  [from_behind(): return lax.ppermute(x, axis, pairs)]
    ppermute x39 -> x41, starting transfers between devices: 29.9 us -> 35.4 us  [partner(): lax.ppermute(x, axis, [(i, i ^ flip) for i in range(lax.axis_size(axis))])]
    ppermute x39 -> x41, waiting for transfers between devices: 201 us -> 196 us  [partner(): lax.ppermute(x, axis, [(i, i ^ flip) for i in range(lax.axis_size(axis))])]
    unnamed x332 -> x340, local copies, waits for them, and re-layouts: 44.6 us -> 49.1 us
    slice x35 -> x37, local copies, waits for them, and re-layouts: 29 us -> 30.6 us  [after(): event[(0,) * event.ndim].astype(jnp.float32)]
  transfers between devices with their start and end apart: 63 -> 71, of which waited for: 35 -> 37; matrix products, arithmetic and copies ran while one was open for 18% -> 18% of each run, Pallas kernels for 8% -> 8%
where the time goes in v5:
time: 1450 us; the launch traced here: 1440 us
  waiting for transfers between devices  721 us (50%)
  matrix products  185 us (13%)
  local copies, waits for them, and re-layouts  167 us (12%)
  Pallas kernels  165 us (11%)
  other arithmetic  85 us (6%)
  starting transfers between devices  68.5 us (5%)
  between operations  46 us (3%)
    all_gather x8, waiting for transfers between devices, gather_rows(): return lax.all_gather(local, 'tp', axis=1, tiled=True)  268 us
    reduce_scatter x8, waiting for transfers between devices, reduce_rows(): return lax.psum_scatter(low, 'tp', scatter_dimension=1, tiled=True)  210 us
    ppermute x41, waiting for transfers between devices, partner(): lax.ppermute(x, axis, [(i, i ^ flip) for i in range(lax.axis_size(axis))])  196 us
    unnamed x340, local copies, waits for them, and re-layouts  49.1 us
    ppermute x14, waiting for transfers between devices, from_behind(): return lax.ppermute(x, axis, pairs)  46.9 us
    pallas_call x1, Pallas kernels, scan_back(): pl.pallas_call(back_kernel, grid=(n,), in_specs=[big, big, big, thin, thi...  42.7 us
    pallas_call x3, Pallas kernels, attend_back(): pl.pallas_call(body, grid=(rows, length // block), in_specs=[pl.BlockSpec...  38.8 us
    ppermute x41, starting transfers between devices, partner(): lax.ppermute(x, axis, [(i, i ^ flip) for i in range(lax.axis_size(axis))])  35.4 us
  transfers between devices with their start and end apart: 71, of which 37 were waited for; matrix products, arithmetic and copies ran while one was open for 18% of the time, Pallas kernels for 8%

profile of v5, /device:TPU:0, one launch (start us, length us, event | category | flops | bytes accessed | tf_op | source)
XLA Modules:
  0.0 1437.4 jit_solution(15742344405822929953)
XLA Ops:
  21.5 58.4 %all-gather.9.cloned.1.call-done = bf16[1,1024,1536]{2,1,0:T(8,128)(2,1)} async-done(((bf16[1,256,1536]{2,1,0:T(8,128)(2,1)}), bf16[1,1024,1536]{2,1,0:T(8,128)(2,1)}) %all-gather.9.cloned.1.call-update) | async-done | bytes 3145744 | tf_op jit(solution)/shard_map/all_gather | solution.py:38
  79.9 8.3 fusion.106
  98.0 8.3 collective-permute-done.1
  114.8 7.1 collective-permute-done.2
  123.0 5.4 convert_multiply_fusion.5
  130.5 10.2 shard_map.340
  146.8 19.1 %shard_map.341 = (f32[1,1024,768]{2,1,0:T(8,128)S(1)}, f32[1,8,16,768]{3,2,1,0:T(8,128)S(1)}) custom-call(f32[1,1024,768]{2,1,0:T(8,128)} %copy-done.6, f32[1,1024,768]{2,1,0:T(8,128)} %get-tuple-element.211.push_ref, f32[1,16,1024]{2,1,0:T(8,128)S(1)} %get-tuple-element.199.write_ref, f32[1,16,1024]{2,1,0:T(8,128)S(1)} %get-tuple-element.198.read_ref, ...), custom_call_target="tpu_custom_call" | custom-call | flops 20999999488 | bytes 63000000 | tf_op jit(solution)/shard_map/pallas_call | solution.py:308
  181.7 58.5 %reduce-scatter.9.cloned.1.call-done = bf16[1,256,1536]{1,2,0:T(8,128)(2,1)} async-done(((bf16[1,1024,1536]{1,2,0:T(8,128)(2,1)}), bf16[1,256,1536]{1,2,0:T(8,128)(2,1)}) %reduce-scatter.9.cloned.1.call-update) | async-done | bytes 786448 | tf_op jit(solution)/shard_map/reduce_scatter | solution.py:45
  245.5 63.4 %all-gather.13.cloned.1.call-done = bf16[1,1024,1536]{2,1,0:T(8,128)(2,1)} async-done(((bf16[1,256,1536]{2,1,0:T(8,128)(2,1)}), bf16[1,1024,1536]{2,1,0:T(8,128)(2,1)}) %all-gather.13.cloned.1.call-update) | async-done | bytes 3145744 | tf_op jit(solution)/shard_map/all_gather | solution.py:38
  309.0 10.2 convert_bitcast_fusion.5
  321.2 5.1 fusion.61
  326.3 59.0 %reduce-scatter.11.cloned.1.call-done.part_ref = bf16[1,256,1536]{2,1,0:T(8,128)(2,1)} async-done(((bf16[1,1024,1536]{2,1,0:T(8,128)(2,1)}), bf16[1,256,1536]{2,1,0:T(8,128)(2,1)}) %reduce-scatter.11.cloned.1.call-update) | async-done | bytes 786448 | tf_op jit(solution)/shard_map/reduce_scatter | solution.py:45
  388.2 6.1 copy.116
  397.8 54.0 %all-gather.15.cloned.1.call-done = bf16[1,1024,1536]{2,1,0:T(8,128)(2,1)} async-done(((bf16[1,256,1536]{2,1,0:T(8,128)(2,1)}), bf16[1,1024,1536]{2,1,0:T(8,128)(2,1)}) %all-gather.15.cloned.1.call-update) | async-done | bytes 3145744 | tf_op jit(solution)/shard_map/all_gather | solution.py:38
  451.8 5.2 fusion.158.refs_4_.refs_5_
  463.2 10.6 collective-permute-done.6.refs_2_.refs_3_
  479.6 5.2 collective-permute-start.8
  484.8 7.4 shard_map.344
  497.5 5.6 collective-permute-start.10
  505.6 7.4 shard_map.345
  523.2 7.5 shard_map.346
  535.3 58.3 %reduce-scatter.13.cloned.1.call-done.part_ref = bf16[1,256,1536]{2,1,0:T(8,128)(2,1)} async-done(((bf16[1,1024,1536]{2,1,0:T(8,128)(2,1)}), bf16[1,256,1536]{2,1,0:T(8,128)(2,1)}) %reduce-scatter.13.cloned.1.call-update) | async-done | bytes 786448 | tf_op jit(solution)/shard_map/reduce_scatter | solution.py:45
  596.4 63.6 %all-gather.17.cloned.1.call-done = bf16[1,1024,1536]{2,1,0:T(8,128)(2,1)} async-done(((bf16[1,256,1536]{2,1,0:T(8,128)(2,1)}), bf16[1,1024,1536]{2,1,0:T(8,128)(2,1)}) %all-gather.17.cloned.1.call-update) | async-done | bytes 3145744 | tf_op jit(solution)/shard_map/all_gather | solution.py:38
  660.0 10.2 convert_bitcast_fusion.4
  670.2 5.1 fusion.133
  675.4 8.3 multiply_reduce_fusion.3
  688.2 4.9 copy.124
  693.2 9.7 fusion.44
  724.1 18.7 %reduce-scatter.15.cloned.1.call-done.part_ref = bf16[1,256,1536]{2,1,0:T(8,128)(2,1)} async-done(((bf16[1,1024,1536]{2,1,0:T(8,128)(2,1)}), bf16[1,256,1536]{2,1,0:T(8,128)(2,1)}) %reduce-scatter.15.cloned.1.call-update) | async-done | bytes 786448 | tf_op jit(solution)/shard_map/reduce_scatter | solution.py:45
  746.7 4.5 add_convert_fusion.1
  762.0 44.5 %collective-permute-done.15 = bf16[1,2,1,192,1024]{4,3,2,1,0:T(8,128)(2,1)} collective-permute-done((bf16[1,2,1,192,1024]{4,3,2,1,0:T(8,128)(2,1)}, bf16[1,2,1,192,1024]{4,3,2,1,0:T(8,128)(2,1)}, u32[]{:S(2)}, u32[]{:S(2)}) %collective-permute-start.15) | collective-permute-done | bytes 786464 | tf_op jit(solution)/shard_map/ppermute | solution.py:75
  818.4 13.1 shard_map.349
  831.6 12.8 shard_map.350
  846.3 12.8 shard_map.351
  864.5 11.6 collective-permute-done.17
  876.3 11.0 collective-permute-done.19
  887.5 10.4 collective-permute-done.21
  910.2 4.9 copy.127
  921.2 6.8 copy.128
  932.1 6.9 fusion.120
  943.4 13.8 collective-permute-done.23
  978.6 25.7 %collective-permute-done.27 = bf16[1,2,1,192,384]{4,3,2,1,0:T(8,128)(2,1)S(1)} collective-permute-done((bf16[1,2,1,192,384]{4,3,2,1,0:T(8,128)(2,1)S(1)}, bf16[1,2,1,192,384]{4,3,2,1,0:T(8,128)(2,1)S(1)}, u32[]{:S(2)}, u32[]{:S(2)}) %collective-permute-start.27) | collective-permute-done | bytes 294944 | tf_op jit(solution)/shard_map/ppermute | solution.py:75
  1007.0 25.9 %all-gather.21.cloned.1.call-done = bf16[1,1024,1536]{2,1,0:T(8,128)(2,1)} async-done(((bf16[1,256,1536]{2,1,0:T(8,128)(2,1)}), bf16[1,1024,1536]{2,1,0:T(8,128)(2,1)}) %all-gather.21.cloned.1.call-update) | async-done | bytes 3145744 | tf_op jit(solution)/shard_map/all_gather | solution.py:38
  1032.9 9.1 fusion.134
  1041.9 11.7 multiply_reduce_fusion.1
  1057.2 4.7 copy.130
  1061.9 7.0 collective-permute-done.29
  1070.8 4.8 copy.131
  1075.6 9.1 fusion.42
  1101.4 11.3 reduce-scatter.19.cloned.1.call-done.part_ref
  1119.1 4.5 add_convert_fusion
  1127.9 49.6 %collective-permute-done.33 = bf16[1,2,1,192,1024]{4,3,2,1,0:T(8,128)(2,1)S(1)} collective-permute-done((bf16[1,2,1,192,1024]{4,3,2,1,0:T(8,128)(2,1)S(1)}, bf16[1,2,1,192,1024]{4,3,2,1,0:T(8,128)(2,1)S(1)}, u32[]{:S(2)}, u32[]{:S(2)}) %collective-permute-start.33) | collective-permute-done | bytes 786464 | tf_op jit(solution)/shard_map/ppermute | solution.py:75
  1182.4 12.5 fusion.74
  1194.9 9.9 shard_map.354
  1226.1 42.7 %shard_map.355 = (f32[1,1024,768]{2,1,0:T(8,128)S(1)}, f32[1,1024,768]{2,1,0:T(8,128)}, f32[1,1,16384]{2,1,0:T(1,128)S(1)}, f32[1,1,16384]{2,1,0:T(1,128)S(1)}, f32[16,768]{1,0:T(8,128)S(1)}) custom-call(f32[1,1024,768]{2,1,0:T(8,128)} %copy-done.6, f32[1,1024,768]{2,1,0:T(8,128)} %get-tuple-element.211.push_ref, f32[1,1024,768]{2,1,0:T(8,128)} %bitcast.573, ...), custom_call_target="tpu_custom_call" | custom-call | flops 46000001024 | bytes 138000000 | tf_op jit(solution)/shard_map/pallas_call | solution.py:413
  1268.8 4.7 convert_reduce_fusion
  1290.3 5.5 collective-permute-done.39
  1301.5 7.8 collective-permute-done.40
  1310.1 9.6 multiply_reduce_fusion.4
  1331.7 6.6 multiply_reduce_fusion
  1344.7 4.6 copy.138
  1349.3 5.5 collective-permute-done.45
  1355.5 7.5 fusion.75
  1404.1 9.5 collective-permute-done.52
  (705 shorter events, 347.4 us)
Async XLA Ops:
  7.2 72.7 %all-gather.9.cloned.1.call-start = ((), (), s32[]{:S(2)}) async-start(), calls=%async_computation.8 | async-start | bytes 3932160 | tf_op jit(solution)/shard_map/all_gather | solution.py:38
  13.6 164.3 %all-gather.11.cloned.1.call-start = ((), (), s32[]{:S(2)}) async-start(), calls=%async_computation.9 | async-start | bytes 3932160 | tf_op jit(solution)/shard_map/all_gather | solution.py:38
  97.9 8.5 collective-permute-start.1
  107.1 14.8 %collective-permute-start.2 = (bf16[1,1024,128]{1,2,0:T(8,128)(2,1)S(1)}, bf16[1,1024,128]{1,2,0:T(8,128)(2,1)}, u32[]{:S(2)}, u32[]{:S(2)}) collective-permute-start(bf16[1,1024,128]{1,2,0:T(8,128)(2,1)S(1)} %add_convert_fusion.21), channel_id=1, source_target_pairs={{0,2},{1,3},{2,0},{3,1},{4,6},{5,7},{6,4},{7,5},{8,10},{9,11},{10,... | collective-permute-start | bytes 786440 | tf_op jit(solution)/shard_map/ppermute | solution.py:75
  114.6 125.7 %reduce-scatter.9.cloned.1.call-start = ((), (), s32[]{:S(2)}) async-start(), calls=%async_computation.10 | async-start | bytes 3932160 | tf_op jit(solution)/shard_map/reduce_scatter | solution.py:45
  181.6 127.3 %all-gather.13.cloned.1.call-start = ((), (), s32[]{:S(2)}) async-start(), calls=%async_computation.11 | async-start | bytes 3932160 | tf_op jit(solution)/shard_map/all_gather | solution.py:38
  245.3 140.1 %reduce-scatter.11.cloned.1.call-start = ((), (), s32[]{:S(2)}) async-start(), calls=%async_computation.12 | async-start | bytes 3932160 | tf_op jit(solution)/shard_map/reduce_scatter | solution.py:45
  326.3 125.5 %all-gather.15.cloned.1.call-start = ((), (), s32[]{:S(2)}) async-start(), calls=%async_computation.13 | async-start | bytes 3932160 | tf_op jit(solution)/shard_map/all_gather | solution.py:38
  388.1 205.4 %reduce-scatter.13.cloned.1.call-start = ((), (), s32[]{:S(2)}) async-start(), calls=%async_computation.14 | async-start | bytes 3932160 | tf_op jit(solution)/shard_map/reduce_scatter | solution.py:45
  459.0 14.8 %collective-permute-start.6 = (bf16[1,1024,256]{2,1,0:T(8,128)(2,1)}, bf16[1,1024,256]{2,1,0:T(8,128)(2,1)}, u32[]{:S(2)}, u32[]{:S(2)}) collective-permute-start(bf16[1,1024,256]{2,1,0:T(8,128)(2,1)} %slice.430), channel_id=1, source_target_pairs={{0,8},{4,12},{1,9},{5,13},{2,10},{6,14},{3,11},{7,15},{16,24},{20,... | collective-permute-start | bytes 1572872 | tf_op jit(solution)/shard_map/ppermute | solution.py:34
  476.3 8.5 collective-permute-start.7
  479.6 16.5 %collective-permute-start.8 = (bf16[1,1024,256]{2,1,0:T(8,128)(2,1)}, bf16[1,1024,256]{2,1,0:T(8,128)(2,1)}, u32[]{:S(2)}, u32[]{:S(2)}) collective-permute-start(bf16[1,1024,256]{2,1,0:T(8,128)(2,1)} %get-tuple-element.193), channel_id=1, source_target_pairs={{0,8},{4,12},{1,9},{5,13},{2,10},{6,14},{3,11},{7,15},{16,24},{20,... | collective-permute-start | bytes 1572872 | tf_op jit(solution)/shard_map/ppermute | solution.py:34
  497.4 5.7 collective-permute-start.9
  497.5 19.9 %collective-permute-start.10 = (bf16[1,1024,256]{2,1,0:T(8,128)(2,1)}, bf16[1,1024,256]{2,1,0:T(8,128)(2,1)}, u32[]{:S(2)}, u32[]{:S(2)}) collective-permute-start(bf16[1,1024,256]{2,1,0:T(8,128)(2,1)} %get-tuple-element.191), channel_id=1, source_target_pairs={{0,8},{4,12},{1,9},{5,13},{2,10},{6,14},{3,11},{7,15},{16,24},{20,... | collective-permute-start | bytes 1572872 | tf_op jit(solution)/shard_map/ppermute | solution.py:34
  535.2 124.8 %all-gather.17.cloned.1.call-start = ((), (), s32[]{:S(2)}) async-start(), calls=%async_computation.15 | async-start | bytes 3932160 | tf_op jit(solution)/shard_map/all_gather | solution.py:38
  596.3 146.5 %reduce-scatter.15.cloned.1.call-start = ((), (), s32[]{:S(2)}) async-start(), calls=%async_computation.16 | async-start | bytes 3932160 | tf_op jit(solution)/shard_map/reduce_scatter | solution.py:45
  683.8 130.3 %all-gather.19.cloned.1.call-start = ((), (), s32[]{:S(2)}) async-start(), calls=%async_computation.17 | async-start | bytes 3932160 | tf_op jit(solution)/shard_map/all_gather | solution.py:38
  707.1 39.6 %collective-permute-start.12 = (bf16[2,2,1,192,2,1024]{5,3,4,2,1,0:T(8,128)(2,1)}, bf16[2,2,1,192,2,1024]{5,3,4,2,1,0:T(8,128)(2,1)}, u32[]{:S(2)}, u32[]{:S(2)}) collective-permute-start(bf16[2,2,1,192,2,1024]{5,3,4,2,1,0:T(8,128)(2,1)} %dynamic-slice_convert_fusion.3), channel_id=1, source_target_pairs={{0,4},{4,0},{8,12},{12,8},{1,5},{5,1},{9,13},{13,9},{2,6},{6,2},{1... | collective-permute-start | bytes 9437192 | tf_op jit(solution)/shard_map/ppermute | solution.py:75
  746.4 219.2 %reduce-scatter.17.cloned.1.call-start = ((), (), s32[]{:S(2)}) async-start(), calls=%async_computation.18 | async-start | bytes 3932160 | tf_op jit(solution)/shard_map/reduce_scatter | solution.py:45
  746.6 7.4 collective-permute-start.14
  752.5 56.5 %collective-permute-start.13 = (bf16[1,2,1,192,2,1024]{5,3,4,2,1,0:T(8,128)(2,1)}, bf16[1,2,1,192,2,1024]{5,3,4,2,1,0:T(8,128)(2,1)}, u32[]{:S(2)}, u32[]{:S(2)}) collective-permute-start(bf16[1,2,1,192,2,1024]{5,3,4,2,1,0:T(8,128)(2,1)} %constant_dynamic-slice_fusion.8), channel_id=1, source_target_pairs={{0,16},{16,0},{1,17},{17,1},{2,18},{18,2},{3,19},{19,3},{4,20},{20... | collective-permute-start | bytes 4718600 | tf_op jit(solution)/shard_map/ppermute | solution.py:75
  758.3 48.2 %collective-permute-start.15 = (bf16[1,2,1,192,1024]{4,3,2,1,0:T(8,128)(2,1)}, bf16[1,2,1,192,1024]{4,3,2,1,0:T(8,128)(2,1)}, u32[]{:S(2)}, u32[]{:S(2)}) collective-permute-start(bf16[1,2,1,192,1024]{4,3,2,1,0:T(8,128)(2,1)} %constant_dynamic-slice_fusion.7), channel_id=1, source_target_pairs={{0,16},{16,0},{1,17},{17,1},{2,18},{18,2},{3,19},{19,3},{4,20},{20... | collective-permute-start | bytes 2359304 | tf_op jit(solution)/shard_map/ppermute | solution.py:75
  831.5 13.4 collective-permute-start.16
  844.4 16.3 %collective-permute-start.18 = (bf16[1,1024,256]{2,1,0:T(8,128)(2,1)S(1)}, bf16[1,1024,256]{2,1,0:T(8,128)(2,1)S(1)}, u32[]{:S(2)}, u32[]{:S(2)}) collective-permute-start(bf16[1,1024,256]{2,1,0:T(8,128)(2,1)S(1)} %get-tuple-element.78), channel_id=1, source_target_pairs={{0,4},{4,0},{8,12},{12,8},{1,5},{5,1},{9,13},{13,9},{2,6},{6,2},{1... | collective-permute-start | bytes 1572872 | tf_op jit(solution)/shard_map/ppermute | solution.py:75
  859.2 16.8 %collective-permute-start.17 = (bf16[1,1024,256]{2,1,0:T(8,128)(2,1)S(1)}, bf16[1,1024,256]{2,1,0:T(8,128)(2,1)S(1)}, u32[]{:S(2)}, u32[]{:S(2)}) collective-permute-start(bf16[1,1024,256]{2,1,0:T(8,128)(2,1)S(1)} %fusion.192), channel_id=1, source_target_pairs={{8,0},{12,4},{9,1},{13,5},{10,2},{14,6},{11,3},{15,7},{24,16},{28,... | collective-permute-start | bytes 1572872 | tf_op jit(solution)/shard_map/ppermute | solution.py:34
  860.9 26.4 %collective-permute-start.19 = (bf16[1,1024,256]{2,1,0:T(8,128)(2,1)S(1)}, bf16[1,1024,256]{2,1,0:T(8,128)(2,1)S(1)}, u32[]{:S(2)}, u32[]{:S(2)}) collective-permute-start(bf16[1,1024,256]{2,1,0:T(8,128)(2,1)S(1)} %fusion.200), channel_id=1, source_target_pairs={{8,0},{12,4},{9,1},{13,5},{10,2},{14,6},{11,3},{15,7},{24,16},{28,... | collective-permute-start | bytes 1572872 | tf_op jit(solution)/shard_map/ppermute | solution.py:34
  862.5 35.4 %collective-permute-start.21 = (bf16[1,1024,256]{2,1,0:T(8,128)(2,1)S(1)}, bf16[1,1024,256]{2,1,0:T(8,128)(2,1)S(1)}, u32[]{:S(2)}, u32[]{:S(2)}) collective-permute-start(bf16[1,1024,256]{2,1,0:T(8,128)(2,1)S(1)} %fusion.205), channel_id=1, source_target_pairs={{8,0},{12,4},{9,1},{13,5},{10,2},{14,6},{11,3},{15,7},{24,16},{28,... | collective-permute-start | bytes 1572872 | tf_op jit(solution)/shard_map/ppermute | solution.py:34
  906.0 126.8 %all-gather.21.cloned.1.call-start = ((), (), s32[]{:S(2)}) async-start(), calls=%async_computation.19 | async-start | bytes 3932160 | tf_op jit(solution)/shard_map/all_gather | solution.py:38
  929.9 28.9 %collective-permute-start.22 = (bf16[1,1,1,192,2,1024]{5,3,4,2,1,0:T(8,128)(2,1)S(1)}, bf16[1,1,1,192,2,1024]{5,3,4,2,1,0:T(8,128)(2,1)S(1)}, u32[]{:S(2)}, u32[]{:S(2)}) collective-permute-start(bf16[1,1,1,192,2,1024]{5,3,4,2,1,0:T(8,128)(2,1)S(1)} %dynamic-slice_add_fusion.1), channel_id=1, source_target_pairs={{0,8},{4,12},{8,0},{12,4},{1,9},{5,13},{9,1},{13,5},{2,10},{6,14},... | collective-permute-start | bytes 2359304 | tf_op jit(solution)/shard_map/ppermute | solution.py:75
  930.0 27.2 %collective-permute-start.23 = (bf16[1,1,1,192,1024]{4,3,2,1,0:T(8,128)(2,1)S(1)}, bf16[1,1,1,192,1024]{4,3,2,1,0:T(8,128)(2,1)S(1)}, u32[]{:S(2)}, u32[]{:S(2)}) collective-permute-start(bf16[1,1,1,192,1024]{4,3,2,1,0:T(8,128)(2,1)S(1)} %dynamic-slice_add_fusion.3), channel_id=1, source_target_pairs={{0,8},{4,12},{8,0},{12,4},{1,9},{5,13},{9,1},{13,5},{2,10},{6,14},... | collective-permute-start | bytes 1179656 | tf_op jit(solution)/shard_map/ppermute | solution.py:75
  969.2 143.6 %reduce-scatter.19.cloned.1.call-start = ((), (), s32[]{:S(2)}) async-start(), calls=%async_computation.20 | async-start | bytes 3932160 | tf_op jit(solution)/shard_map/reduce_scatter | solution.py:45
  969.4 4.8 collective-permute-start.24
  969.5 8.3 collective-permute-start.26
  976.2 28.7 %collective-permute-start.25 = (bf16[1,2,1,192,1152]{4,3,2,1,0:T(8,128)(2,1)S(1)}, bf16[1,2,1,192,1152]{4,3,2,1,0:T(8,128)(2,1)S(1)}, u32[]{:S(2)}, u32[]{:S(2)}) collective-permute-start(bf16[1,2,1,192,1152]{4,3,2,1,0:T(8,128)(2,1)S(1)} %constant_dynamic-slice_fusion.6), channel_id=1, source_target_pairs={{0,16},{16,0},{1,17},{17,1},{2,18},{18,2},{3,19},{19,3},{4,20},{20... | collective-permute-start | bytes 2654216 | tf_op jit(solution)/shard_map/ppermute | solution.py:75
  978.0 26.3 %collective-permute-start.27 = (bf16[1,2,1,192,384]{4,3,2,1,0:T(8,128)(2,1)S(1)}, bf16[1,2,1,192,384]{4,3,2,1,0:T(8,128)(2,1)S(1)}, u32[]{:S(2)}, u32[]{:S(2)}) collective-permute-start(bf16[1,2,1,192,384]{4,3,2,1,0:T(8,128)(2,1)S(1)} %constant_dynamic-slice_fusion.5), channel_id=1, source_target_pairs={{0,16},{16,0},{1,17},{17,1},{2,18},{18,2},{3,19},{19,3},{4,20},{20... | collective-permute-start | bytes 884744 | tf_op jit(solution)/shard_map/ppermute | solution.py:75
  1053.7 128.7 %all-gather.23.cloned.1.call-start = ((), (), s32[]{:S(2)}) async-start(), calls=%async_computation.21 | async-start | bytes 3932160 | tf_op jit(solution)/shard_map/all_gather | solution.py:38
  1053.8 16.3 %collective-permute-start.28 = (bf16[1,1,1,192,1152]{4,3,2,1,0:T(8,128)(2,1)S(1)}, bf16[1,1,1,192,1152]{4,3,2,1,0:T(8,128)(2,1)S(1)}, u32[]{:S(2)}, u32[]{:S(2)}) collective-permute-start(bf16[1,1,1,192,1152]{4,3,2,1,0:T(8,128)(2,1)S(1)} %constant_dynamic-slice_fusion.4), channel_id=1, source_target_pairs={{0,8},{4,12},{8,0},{12,4},{1,9},{5,13},{9,1},{13,5},{2,10},{6,14},... | collective-permute-start | bytes 1327112 | tf_op jit(solution)/shard_map/ppermute | solution.py:75
  1055.3 13.5 collective-permute-start.29
  1088.9 30.1 %collective-permute-start.30 = (bf16[2,2,1,192,2,1024]{5,3,4,2,1,0:T(8,128)(2,1)}, bf16[2,2,1,192,2,1024]{5,3,4,2,1,0:T(8,128)(2,1)}, u32[]{:S(2)}, u32[]{:S(2)}) collective-permute-start(bf16[2,2,1,192,2,1024]{5,3,4,2,1,0:T(8,128)(2,1)} %dynamic-slice_convert_fusion.1), channel_id=1, source_target_pairs={{0,4},{4,0},{8,12},{12,8},{1,5},{5,1},{9,13},{13,9},{2,6},{6,2},{1... | collective-permute-start | bytes 9437192 | tf_op jit(solution)/shard_map/ppermute | solution.py:75
  1118.5 166.0 %reduce-scatter.21.cloned.1.call-start = ((), (), s32[]{:S(2)}) async-start(), calls=%async_computation.22 | async-start | bytes 3932160 | tf_op jit(solution)/shard_map/reduce_scatter | solution.py:45
  1119.0 6.3 collective-permute-start.32
  1123.8 54.9 %collective-permute-start.31 = (bf16[1,2,1,192,2,1024]{5,3,4,2,1,0:T(8,128)(2,1)S(1)}, bf16[1,2,1,192,2,1024]{5,3,4,2,1,0:T(8,128)(2,1)S(1)}, u32[]{:S(2)}, u32[]{:S(2)}) collective-permute-start(bf16[1,2,1,192,2,1024]{5,3,4,2,1,0:T(8,128)(2,1)S(1)} %constant_dynamic-slice_fusion.2), channel_id=1, source_target_pairs={{0,16},{16,0},{1,17},{17,1},{2,18},{18,2},{3,19},{19,3},{4,20},{20... | collective-permute-start | bytes 4718600 | tf_op jit(solution)/shard_map/ppermute | solution.py:75
  1126.4 51.0 %collective-permute-start.33 = (bf16[1,2,1,192,1024]{4,3,2,1,0:T(8,128)(2,1)S(1)}, bf16[1,2,1,192,1024]{4,3,2,1,0:T(8,128)(2,1)S(1)}, u32[]{:S(2)}, u32[]{:S(2)}) collective-permute-start(bf16[1,2,1,192,1024]{4,3,2,1,0:T(8,128)(2,1)S(1)} %constant_dynamic-slice_fusion.1), channel_id=1, source_target_pairs={{0,16},{16,0},{1,17},{17,1},{2,18},{18,2},{3,19},{19,3},{4,20},{20... | collective-permute-start | bytes 2359304 | tf_op jit(solution)/shard_map/ppermute | solution.py:75
  1204.9 20.1 %collective-permute-start.34 = (f32[1,17,768]{2,1,0:T(8,128)S(1)}, f32[1,17,768]{2,1,0:T(8,128)S(1)}, u32[]{:S(2)}, u32[]{:S(2)}) collective-permute-start(f32[1,17,768]{2,1,0:T(8,128)S(1)} %pad_maximum_fusion.12), channel_id=1, source_target_pairs={{4,0},{8,4},{12,8},{5,1},{9,5},{13,9},{6,2},{10,6},{14,10},{7,3},{... | collective-permute-start | bytes 156680 | tf_op jit(solution)/shard_map/ppermute | solution.py:34
  1206.2 18.8 %collective-permute-start.35 = (f32[1,17,768]{2,1,0:T(8,128)S(1)}, f32[1,17,768]{2,1,0:T(8,128)S(1)}, u32[]{:S(2)}, u32[]{:S(2)}) collective-permute-start(f32[1,17,768]{2,1,0:T(8,128)S(1)} %pad_maximum_fusion.12), channel_id=1, source_target_pairs={{8,0},{12,4},{9,1},{13,5},{10,2},{14,6},{11,3},{15,7},{24,16},{28,... | collective-permute-start | bytes 156680 | tf_op jit(solution)/shard_map/ppermute | solution.py:34
  1207.5 17.4 %collective-permute-start.36 = (f32[1,17,768]{2,1,0:T(8,128)S(1)}, f32[1,17,768]{2,1,0:T(8,128)S(1)}, u32[]{:S(2)}, u32[]{:S(2)}) collective-permute-start(f32[1,17,768]{2,1,0:T(8,128)S(1)} %pad_maximum_fusion.12), channel_id=1, source_target_pairs={{12,0},{13,1},{14,2},{15,3},{28,16},{29,17},{30,18},{31,19}} | collective-permute-start | bytes 156680 | tf_op jit(solution)/shard_map/ppermute | solution.py:34
  1216.9 63.3 %collective-permute-start.42 = (bf16[2,2,1,192,768]{4,3,2,1,0:T(8,128)(2,1)}, bf16[2,2,1,192,768]{4,3,2,1,0:T(8,128)(2,1)}, u32[]{:S(2)}, u32[]{:S(2)}) collective-permute-start(bf16[2,2,1,192,768]{4,3,2,1,0:T(8,128)(2,1)} %dynamic-slice_convert_fusion.13), channel_id=1, source_target_pairs={{0,4},{4,0},{8,12},{12,8},{1,5},{5,1},{9,13},{13,9},{2,6},{6,2},{1... | collective-permute-start | bytes 3538952 | tf_op jit(solution)/shard_map/ppermute | solution.py:75
  1220.4 206.5 %reduce-scatter.23.cloned.1.call-start = ((), (), s32[]{:S(2)}) async-start(), calls=%async_computation.23 | async-start | bytes 3932160 | tf_op jit(solution)/shard_map/reduce_scatter | solution.py:45
  1221.3 56.4 %collective-permute-start.37 = (bf16[1,1,1,192,2,1024]{5,3,4,2,1,0:T(8,128)(2,1)}, bf16[1,1,1,192,2,1024]{5,3,4,2,1,0:T(8,128)(2,1)}, u32[]{:S(2)}, u32[]{:S(2)}) collective-permute-start(bf16[1,1,1,192,2,1024]{5,3,4,2,1,0:T(8,128)(2,1)} %dynamic-slice_add_fusion), channel_id=1, source_target_pairs={{0,8},{4,12},{8,0},{12,4},{1,9},{5,13},{9,1},{13,5},{2,10},{6,14},... | collective-permute-start | bytes 2359304 | tf_op jit(solution)/shard_map/ppermute | solution.py:75
  1224.9 51.6 %collective-permute-start.38 = (bf16[1,1,1,192,1024]{4,3,2,1,0:T(8,128)(2,1)}, bf16[1,1,1,192,1024]{4,3,2,1,0:T(8,128)(2,1)}, u32[]{:S(2)}, u32[]{:S(2)}) collective-permute-start(bf16[1,1,1,192,1024]{4,3,2,1,0:T(8,128)(2,1)} %dynamic-slice_add_fusion.2), channel_id=1, source_target_pairs={{0,8},{4,12},{8,0},{12,4},{1,9},{5,13},{9,1},{13,5},{2,10},{6,14},... | collective-permute-start | bytes 1179656 | tf_op jit(solution)/shard_map/ppermute | solution.py:75
  1283.0 16.0 %collective-permute-start.43 = (bf16[1,2,1,192,768]{4,3,2,1,0:T(8,128)(2,1)}, bf16[1,2,1,192,768]{4,3,2,1,0:T(8,128)(2,1)}, u32[]{:S(2)}, u32[]{:S(2)}) collective-permute-start(bf16[1,2,1,192,768]{4,3,2,1,0:T(8,128)(2,1)} %constant_dynamic-slice_fusion), channel_id=1, source_target_pairs={{0,16},{16,0},{1,17},{17,1},{2,18},{18,2},{3,19},{19,3},{4,20},{20... | collective-permute-start | bytes 1769480 | tf_op jit(solution)/shard_map/ppermute | solution.py:75
  1288.1 7.7 collective-permute-start.39
  1295.9 13.4 collective-permute-start.40
  1319.8 6.9 collective-permute-start.41
  1343.2 11.6 collective-permute-start.45
  1354.9 10.6 collective-permute-start.46
  1368.6 26.7 %collective-permute-start.49 = (bf16[2,2,1,192,2,768]{5,3,4,2,1,0:T(8,128)(2,1)}, bf16[2,2,1,192,2,768]{5,3,4,2,1,0:T(8,128)(2,1)}, u32[]{:S(2)}, u32[]{:S(2)}) collective-permute-start(bf16[2,2,1,192,2,768]{5,3,4,2,1,0:T(8,128)(2,1)} %fusion.119), channel_id=1, source_target_pairs={{0,4},{4,0},{8,12},{12,8},{1,5},{5,1},{9,13},{13,9},{2,6},{6,2},{1... | collective-permute-start | bytes 7077896 | tf_op jit(solution)/shard_map/ppermute | solution.py:75
  1382.2 9.5 collective-permute-start.54
  1395.3 5.5 collective-permute-start.47
  1398.5 15.2 %collective-permute-start.52 = (bf16[2,1,1,192,768]{4,3,0,2,1:T(8,128)(2,1)S(1)}, bf16[2,1,1,192,768]{4,3,0,2,1:T(8,128)(2,1)S(1)}, u32[]{:S(2)}, u32[]{:S(2)}) collective-permute-start(bf16[2,1,1,192,768]{4,3,0,2,1:T(8,128)(2,1)S(1)} %dynamic-slice_bitcast_fusion), channel_id=1, source_target_pairs={{0,8},{4,12},{8,0},{12,4},{1,9},{5,13},{9,1},{13,5},{2,10},{6,14},... | collective-permute-start | bytes 1769480 | tf_op jit(solution)/shard_map/ppermute | solution.py:75
  1400.1 15.0 %collective-permute-start.50 = (bf16[1,2,1,192,768]{4,3,2,1,0:T(8,128)(2,1)S(1)}, bf16[1,2,1,192,768]{4,3,2,1,0:T(8,128)(2,1)S(1)}, u32[]{:S(2)}, u32[]{:S(2)}) collective-permute-start(bf16[1,2,1,192,768]{4,3,2,1,0:T(8,128)(2,1)S(1)} %dynamic-slice_bitcast_fusion.1), channel_id=1, source_target_pairs={{0,16},{16,0},{1,17},{17,1},{2,18},{18,2},{3,19},{19,3},{4,20},{20... | collective-permute-start | bytes 1769480 | tf_op jit(solution)/shard_map/ppermute | solution.py:75
  1401.3 19.6 %collective-permute-start.48 = (f32[8,768]{1,0:T(8,128)}, f32[8,768]{1,0:T(8,128)}, u32[]{:S(2)}, u32[]{:S(2)}) collective-permute-start(f32[8,768]{1,0:T(8,128)} %slice_add_fusion.6), channel_id=1, source_target_pairs={{0,2},{1,3},{2,0},{3,1},{4,6},{5,7},{6,4},{7,5},{8,10},{9,11},{10,... | collective-permute-start | bytes 73736 | tf_op jit(solution)/shard_map/ppermute | solution.py:75
  1414.5 8.2 collective-permute-start.53
  1416.0 7.9 collective-permute-start.51
  (171 other events, 2536.7 us)
Sparse Core Ops, SparseCore 0:
  13.7 66.1 all-gather.8
  114.7 63.1 all-gather.10
  181.7 58.4 reduce-scatter.8
  245.4 63.5 all-gather.12
  326.4 58.8 reduce-scatter.10
  388.2 63.5 all-gather.14
  535.3 58.1 reduce-scatter.12
  596.4 63.5 all-gather.16
  683.9 58.8 reduce-scatter.14
  746.5 63.5 all-gather.18
  906.2 59.3 reduce-scatter.16
  969.3 63.5 all-gather.20
  1053.8 58.8 reduce-scatter.18
  1118.7 63.4 all-gather.22
  1220.5 61.8 reduce-scatter.20
  1349.4 59.1 reduce-scatter.22
